TPU v7x, 256 devices: a whole 4x4x8 slice. The times are simulated.
256 devices in a mesh: neg: 32 (over x_hi, z, core), dp: 8 (over y, x_lo).
Axes of the slice: x: 4 (x_hi: 2, x_lo: 2; x = x_hi * 2 + x_lo), y: 4, z: 8, core: 2. Of those that a mesh axis runs over, the one named last changes fastest.
Arguments:
- observations: bfloat16 [8, 10240, 256], P('dp', 'neg'), may hold values from -6 to 6
- actions: bfloat16 [8, 10240, 16], P('dp', 'neg'), may hold values from -12 to 12
- replay_index: int32 [8, 8192], P('dp', 'neg'), may hold values from 0 to 255
- future_offset: int32 [8, 8192], P('dp', 'neg'), may hold values from 1 to 64
- sa_obs: bfloat16 [256, 1024], replicated, may hold values from -0.375 to 0.375
- sa_act: bfloat16 [16, 1024], replicated, may hold values from -1.5 to 1.5
- sa_mid: bfloat16 [1024, 1024], replicated, may hold values from -0.1875 to 0.1875
- sa_out: bfloat16 [1024, 256], replicated, may hold values from -0.1875 to 0.1875
- goal_obs: bfloat16 [256, 1024], replicated, may hold values from -0.375 to 0.375
- goal_mid: bfloat16 [1024, 1024], replicated, may hold values from -0.1875 to 0.1875
- goal_out: bfloat16 [1024, 256], replicated, may hold values from -0.1875 to 0.1875
Outputs:
- row_loss: float32 [8, 8192], P('dp', 'neg')
- sa_obs_grad: float32 [256, 1024], P(None, ('neg', 'dp'))
- sa_act_grad: float32 [16, 1024], P(None, ('neg', 'dp'))
- sa_mid_grad: float32 [1024, 1024], P(('neg', 'dp'))
- sa_out_grad: float32 [1024, 256], P(('neg', 'dp'))
- goal_obs_grad: float32 [256, 1024], P(None, ('neg', 'dp'))
- goal_mid_grad: float32 [1024, 1024], P(('neg', 'dp'))
- goal_out_grad: float32 [1024, 256], P(('neg', 'dp'))
Inputs may be any that keep to these rules, and one draw needn't show every extreme that they name: `replay_index`: a row of the device's own slab, so that the future row stays inside it.
All inputs are finite; a program needn't handle non-finite values.
Results may differ from a plain program's by a relative error of at most 0.012.
Values may be sent and summed in bfloat16 or wider, within the bound.
No kernel may reach another device: no remote copies, remote signals or barrier semaphores. Data moves between devices by JAX's collectives and lax.ppermute only.
A program may use at most 128 MiB of HBM per device.

v0:
```python
import math

import jax
import jax.numpy as jnp
from jax import lax
from jax.sharding import PartitionSpec as P

NORM_EPS = 1e-05
UNIT_EPS = 1e-06


def swish_grad(normed):
    sigma = jax.nn.sigmoid(normed)
    return sigma * (1.0 + normed * (1.0 - sigma))


def normalize(values):
    center = values - jnp.mean(values, axis=-1, keepdims=True)
    factor = lax.rsqrt(jnp.mean(center * center, axis=-1, keepdims=True) + NORM_EPS)
    return (center * factor, factor)


def norm_back(grad, normed, factor):
    return factor * (
        grad
        - jnp.mean(grad, axis=-1, keepdims=True)
        - normed * jnp.mean(grad * normed, axis=-1, keepdims=True)
    )


def encode(inputs, extra, w_first, w_extra, w_mid, w_last):
    first = jnp.dot(inputs, w_first, preferred_element_type=jnp.float32)
    if extra is not None:
        first = first + jnp.dot(extra, w_extra, preferred_element_type=jnp.float32)
    normed_one, factor_one = normalize(first)
    hidden_one = jax.nn.silu(normed_one).astype(jnp.bfloat16)
    second = jnp.dot(hidden_one, w_mid, preferred_element_type=jnp.float32)
    normed_two, factor_two = normalize(second)
    hidden_two = jax.nn.silu(normed_two).astype(jnp.bfloat16)
    embed = jnp.dot(hidden_two, w_last, preferred_element_type=jnp.float32)
    width = embed.shape[-1]
    inverse = lax.rsqrt(jnp.mean(embed * embed, axis=-1, keepdims=True) + UNIT_EPS)
    unit = embed * inverse * width ** (-0.5)
    saved = (normed_one, factor_one, hidden_one, normed_two, factor_two, hidden_two, embed, inverse)
    return (unit, saved)


def backward(grad_unit, inputs, extra, saved, w_mid, w_last):
    normed_one, factor_one, hidden_one, normed_two, factor_two, hidden_two, embed, inverse = saved
    width = embed.shape[-1]
    along = jnp.mean(grad_unit * embed, axis=-1, keepdims=True)
    grad_embed = (
        width ** (-0.5) * inverse * (grad_unit - embed * inverse * inverse * along)
    ).astype(jnp.bfloat16)
    grad_last = jnp.dot(hidden_two.T, grad_embed, preferred_element_type=jnp.float32)
    back_two = jnp.dot(grad_embed, w_last.T, preferred_element_type=jnp.float32) * swish_grad(
        normed_two
    )
    pre_two = norm_back(back_two, normed_two, factor_two).astype(jnp.bfloat16)
    grad_mid = jnp.dot(hidden_one.T, pre_two, preferred_element_type=jnp.float32)
    back_one = jnp.dot(pre_two, w_mid.T, preferred_element_type=jnp.float32) * swish_grad(
        normed_one
    )
    pre_one = norm_back(back_one, normed_one, factor_one).astype(jnp.bfloat16)
    grad_first = jnp.dot(inputs.T, pre_one, preferred_element_type=jnp.float32)
    if extra is None:
        return (grad_first, grad_mid, grad_last)
    grad_extra = jnp.dot(extra.T, pre_one, preferred_element_type=jnp.float32)
    return (grad_first, grad_extra, grad_mid, grad_last)


def body(
    observations,
    actions,
    replay_index,
    future_offset,
    sa_obs,
    sa_act,
    sa_mid,
    sa_out,
    goal_obs,
    goal_mid,
    goal_out,
):
    replay = replay_index[0]
    future = replay + future_offset[0]
    state_rows = jnp.take(observations[0], replay, axis=0)
    action_rows = jnp.take(actions[0], replay, axis=0)
    goal_rows = jnp.take(observations[0], future, axis=0)
    unit_q, saved_q = encode(state_rows, action_rows, sa_obs, sa_act, sa_mid, sa_out)
    unit_t, saved_t = encode(goal_rows, None, goal_obs, None, goal_mid, goal_out)
    queries = unit_q.astype(jnp.bfloat16)
    targets = unit_t.astype(jnp.bfloat16)
    embed_width = queries.shape[1]
    logit_scale = 3.0 * math.sqrt(embed_width)
    grad_coef = logit_scale / (2.0 * lax.axis_size("dp"))
    positive = logit_scale * jnp.sum(
        queries.astype(jnp.float32) * targets.astype(jnp.float32), axis=-1
    )
    block = jnp.exp(
        logit_scale
        * jnp.einsum(
            "re,ce->rc",
            queries,
            lax.all_gather(targets, "neg", axis=0, tiled=True),
            preferred_element_type=jnp.float32,
        )
    )
    rowsum = jnp.sum(block, axis=1)
    block = jnp.exp(
        logit_scale
        * jnp.einsum(
            "ce,re->cr",
            lax.all_gather(queries, "neg", axis=0, tiled=True),
            targets,
            preferred_element_type=jnp.float32,
        )
    )
    colsum = jnp.sum(block, axis=0)
    every_colsum = lax.all_gather(colsum, "neg", axis=0, tiled=True)
    row_loss = 0.5 * (jnp.log(rowsum) - positive + jnp.log(colsum) - positive)
    every_rowsum = lax.all_gather(rowsum, "neg", axis=0, tiled=True)
    piece = lax.all_gather(targets, "neg", axis=0, tiled=True)
    block = jnp.exp(
        logit_scale * jnp.einsum("re,ce->rc", queries, piece, preferred_element_type=jnp.float32)
    )
    weights = (block / rowsum[:, None] + block / every_colsum[None, :]).astype(jnp.bfloat16)
    query_sum = jnp.dot(weights, piece, preferred_element_type=jnp.float32)
    piece = lax.all_gather(queries, "neg", axis=0, tiled=True)
    block = jnp.exp(
        logit_scale * jnp.einsum("ce,re->cr", piece, targets, preferred_element_type=jnp.float32)
    )
    weights = (block / every_rowsum[:, None] + block / colsum[None, :]).astype(jnp.bfloat16)
    target_sum = jnp.einsum("cr,ce->re", weights, piece, preferred_element_type=jnp.float32)
    query_grad = grad_coef * (query_sum - 2.0 * targets.astype(jnp.float32))
    target_grad = grad_coef * (target_sum - 2.0 * queries.astype(jnp.float32))
    terms = backward(query_grad, state_rows, action_rows, saved_q, sa_mid, sa_out) + backward(
        target_grad, goal_rows, None, saved_t, goal_mid, goal_out
    )
    summed = (
        lax.psum_scatter(terms[0], ("neg", "dp"), scatter_dimension=1, tiled=True),
        lax.psum_scatter(terms[1], ("neg", "dp"), scatter_dimension=1, tiled=True),
        lax.psum_scatter(terms[2], ("neg", "dp"), scatter_dimension=0, tiled=True),
        lax.psum_scatter(terms[3], ("neg", "dp"), scatter_dimension=0, tiled=True),
        lax.psum_scatter(terms[4], ("neg", "dp"), scatter_dimension=1, tiled=True),
        lax.psum_scatter(terms[5], ("neg", "dp"), scatter_dimension=0, tiled=True),
        lax.psum_scatter(terms[6], ("neg", "dp"), scatter_dimension=0, tiled=True),
    )
    return (
        row_loss[None, :],
        summed[0],
        summed[1],
        summed[2],
        summed[3],
        summed[4],
        summed[5],
        summed[6],
    )


def solution(mesh):
    return jax.shard_map(
        body,
        mesh=mesh,
        in_specs=(
            P("dp", "neg", None),
            P("dp", "neg", None),
            P("dp", "neg"),
            P("dp", "neg"),
            P(),
            P(),
            P(),
            P(),
            P(),
            P(),
            P(),
        ),
        out_specs=(
            P("dp", "neg"),
            P(None, ("neg", "dp")),
            P(None, ("neg", "dp")),
            P(("neg", "dp"), None),
            P(("neg", "dp"), None),
            P(None, ("neg", "dp")),
            P(("neg", "dp"), None),
            P(("neg", "dp"), None),
        ),
        check_vma=False,
    )
```

profile of v0, /device:TPU:1, one launch (start us, length us, event | category | flops | bytes accessed | tf_op | source)
XLA Modules:
  0.0 575.1 jit_solution(13697444257526935283)
XLA Ops:
  10.3 1.9 gather_fusion.1
  13.1 1.4 fusion.15
  14.5 1.2 fusion.32
  17.9 1.2 multiply_convert_fusion.6
  20.3 1.5 fusion.34
  22.2 2.6 fusion.35
  27.5 1.4 fusion.13
  29.7 90.5 %all-gather.7.cloned.1.call-done = bf16[8192,256]{0,1:T(8,128)(2,1)} async-done(((bf16[256,256]{0,1:T(8,128)(2,1)}), bf16[8192,256]{0,1:T(8,128)(2,1)}) %all-gather.7.cloned.1.call-update) | async-done | bytes 4194320 | tf_op jit(solution)/shard_map/all_gather | solution.py:114
  120.2 7.3 %fusion.36 = (f32[256]{0:T(256)S(1)}, f32[8192,256]{1,0:T(8,128)}) fusion(bf16[8192,256]{0,1:T(8,128)(2,1)} %all-gather.7.cloned.1.call-done, bf16[256,256]{0,1:T(8,128)(2,1)} %get-tuple-element.26), kind=kOutput, calls=%fused_computation.125 | convolution fusion | flops 1077935872 | bytes 12715008 | tf_op jit(solution)/shard_map/ce,re->cr/dot_general | solution.py:112
  128.1 42.1 %all-gather = f32[32,1,256]{2,1,0:T(1,128)} all-gather(f32[1,1,256]{2,1,0:T(1,128)S(1)} %bitcast.49), channel_id=1, replica_groups=mesh['neg'=32,'dp'=8] {'neg'}, dimensions={0}, use_global_device_ids=true | all-gather | bytes 33792 | tf_op jit(solution)/shard_map/all_gather | solution.py:120
  170.2 36.5 %all-gather.5.cloned.1.call-done = bf16[8192,256]{0,1:T(8,128)(2,1)} async-done(((bf16[256,256]{0,1:T(8,128)(2,1)}), bf16[8192,256]{0,1:T(8,128)(2,1)}) %all-gather.5.cloned.1.call-update) | async-done | bytes 4194320 | tf_op jit(solution)/shard_map/all_gather | solution.py:105
  206.7 3.9 fusion.37
  210.8 1.5 multiply_reduce_fusion.9
  213.4 1.3 fusion.30
  215.1 1.4 fusion.14
  216.5 1.2 fusion.17
  217.7 3.1 fusion.24
  220.8 1.3 fusion.38
  222.2 39.5 %all-gather.1 = f32[32,1,256]{2,1,0:T(1,128)S(1)} all-gather(f32[1,1,256]{2,1,0:T(1,128)S(1)} %bitcast.46), channel_id=1, replica_groups=mesh['neg'=32,'dp'=8] {'neg'}, dimensions={0}, use_global_device_ids=true | all-gather | bytes 33792 | tf_op jit(solution)/shard_map/all_gather | solution.py:122
  261.8 1.6 multiply_reduce_fusion.8
  265.3 1.4 fusion.28
  266.7 3.1 fusion.26
  269.9 1.3 fusion.39
  271.2 1.6 fusion.8
  274.3 285.2 %all-reduce.10.cloned.1.call-done = (f32[256,1024]{0,1:T(8,128)}, f32[16,1024]{0,1:T(8,128)}, f32[1024,1024]{1,0:T(8,128)}, f32[1024,256]{1,0:T(8,128)}, f32[256...) async-done(((f32[256,1024]{0,1:T(8,128)}, f32[16,1024]{0,1:T(8,128)}, f32[1024,1024]{1,0:T(8,128)}, f32[1024,256]{1,0:T(8,128)}, f32[256,1024]{0,1:T(8,128)}, ...) | async-done | bytes 12648464
  559.5 1.3 constant_dynamic-slice_fusion.6
  560.7 1.3 constant_dynamic-slice_fusion.5
  562.0 1.4 constant_dynamic-slice_fusion.4
  563.4 1.3 constant_dynamic-slice_fusion.3
  564.7 1.3 constant_dynamic-slice_fusion.2
  566.0 1.4 constant_dynamic-slice_fusion.1
  567.3 1.3 constant_dynamic-slice_fusion
  (164 shorter events, 16.1 us)
Async XLA Ops:
  7.2 8.8 %copy-start = (bf16[1024,1024]{1,0:T(8,128)(2,1)S(1)}, bf16[1024,1024]{1,0:T(8,128)(2,1)}, u32[]{:S(2)}) copy-start(bf16[1024,1024]{1,0:T(8,128)(2,1)} %param.19) | copy-start | bytes 6291460
  7.2 113.0 %all-gather.7.cloned.1.call-start = ((), (), s32[]{:S(2)}) async-start(), calls=%async_computation.1 | async-start | bytes 4325376 | tf_op jit(solution)/shard_map/all_gather | solution.py:114
  9.4 10.9 %copy-start.37 = (pred[256]{0:T(512)(128)(4,1)}, pred[256]{0:T(512)(128)(4,1)S(1)}, u32[]{:S(2)}) copy-start(pred[256]{0:T(512)(128)(4,1)S(1)} %get-tuple-element.27) | copy-start | bytes 772
  13.1 2.9 copy-start.21
  16.0 3.2 copy-start.2
  16.9 2.2 copy-start.35
  17.9 6.9 %copy-start.46 = (f32[256]{0:T(256)}, f32[256]{0:T(256)S(1)}, u32[]{:S(2)}) copy-start(f32[256]{0:T(256)S(1)} %add_rsqrt_fusion.4) | copy-start | bytes 3076
  20.3 4.5 copy-start.19
  21.8 3.0 copy-start.3
  21.8 2.9 copy-start.31
  22.1 3.0 copy-start.42
  22.1 3.6 copy-start.7
  22.1 3.6 copy-start.23
  22.1 4.4 copy-start.25
  25.1 3.8 copy-start.44
  28.8 177.9 %all-gather.5.cloned.1.call-start = ((), (), s32[]{:S(2)}) async-start(), calls=%async_computation | async-start | bytes 4325376 | tf_op jit(solution)/shard_map/all_gather | solution.py:105
  29.6 177.1 %copy-start.16 = (bf16[256,256]{0,1:T(8,128)(2,1)S(1)}, bf16[256,256]{0,1:T(8,128)(2,1)}, u32[]{:S(2)}) copy-start(bf16[256,256]{0,1:T(8,128)(2,1)} %get-tuple-element.25) | copy-start | bytes 393220
  29.6 529.8 %all-reduce.10.cloned.1.call-start = ((), (), s32[]{:S(2)}) async-start(), calls=%async_computation.2 | async-start | bytes 26214400
  206.7 4.0 copy-start.9
  206.7 4.0 copy-start.15
  206.7 4.0 copy-start.27
  206.7 4.0 copy-start.28
  210.7 11.5 %copy-start.29 = (f32[256]{0:T(256)}, f32[256]{0:T(256)S(1)}, u32[]{:S(2)}) copy-start(f32[256]{0:T(256)S(1)} %get-tuple-element.48) | copy-start | bytes 3076
  213.3 48.4 %slice-start = ((s8[8388608]{0:T(1024)(128)(4,1)}), s8[4194304]{0:T(1024)(128)(4,1)S(1)}, s32[]{:S(2)}) async-start(s8[8388608]{0:T(1024)(128)(4,1)} %bitcast.55), calls=%async_computation.3 | async-start | bytes 8388608
  214.7 47.0 %slice-start.1 = ((s8[8388608]{0:T(1024)(128)(4,1)}), s8[4194304]{0:T(1024)(128)(4,1)S(1)}, s32[]{:S(2)}) async-start(s8[8388608]{0:T(1024)(128)(4,1)} %bitcast.55), calls=%async_computation.4 | async-start | bytes 8388608
  217.7 3.1 copy-start.8
  217.7 44.0 %copy-start.51 = (f32[256]{0:T(256)S(1)}, f32[256]{0:T(256)}, u32[]{:S(2)}) copy-start(f32[256]{0:T(256)} %copy-done.50) | copy-start | bytes 3076
  217.7 44.0 %copy-start.52 = (bf16[8192,256]{0,1:T(8,128)(2,1)S(1)}, bf16[8192,256]{0,1:T(8,128)(2,1)}, u32[]{:S(2)}) copy-start(bf16[8192,256]{0,1:T(8,128)(2,1)} %all-gather.7.cloned.1.call-done) | copy-start | bytes 12582916
  266.7 3.2 copy-start.6
  266.7 4.5 copy-start.20
  266.7 4.5 copy-start.38
  272.9 295.8 %copy-start.1 = (bf16[1024,1024]{1,0:T(8,128)(2,1)S(1)}, bf16[1024,1024]{1,0:T(8,128)(2,1)}, u32[]{:S(2)}) copy-start(bf16[1024,1024]{1,0:T(8,128)(2,1)} %param.19) | copy-start | bytes 6291460
  (27 other events, 37.1 us)
Sparse Core Ops, SparseCore 0:
  29.0 91.1 all-gather.6
  122.7 83.9 all-gather.4
  273.0 286.3 all-reduce.9
where the time goes:
time: 577 us; the launch traced here: 575 us
  waiting for transfers between devices  413 us (72%)
  blocking collectives  81.7 us (14%)
  matrix products  40.4 us (7%)
  local copies, waits for them, and re-layouts  17.7 us (3%)
  between operations  14.5 us (3%)
  other arithmetic  7.89 us (1%)
    unnamed x4, waiting for transfers between devices  286 us
    all_gather x1, waiting for transfers between devices, body(): lax.all_gather(queries, 'neg', axis=0, tiled=True)  90.5 us
    all_gather x1, blocking collectives, body(): every_colsum = lax.all_gather(colsum, 'neg', axis=0, tiled=True)  42.1 us
    all_gather x1, blocking collectives, body(): every_rowsum = lax.all_gather(rowsum, 'neg', axis=0, tiled=True)  39.5 us
    all_gather x1, waiting for transfers between devices, body(): lax.all_gather(targets, 'neg', axis=0, tiled=True)  36.5 us
    unnamed x120, local copies, waits for them, and re-layouts  13.8 us
  transfers between devices with their start and end apart: 3, of which 3 were waited for; matrix products, arithmetic and copies ran while one was open for 1% of the time, Pallas kernels for 0%

commit v1 on v0

v1 whole, which is shorter than its diff:
```python
import functools
import math

import jax
import jax.numpy as jnp
import numpy as np
from jax import lax
from jax.experimental import pallas as pl
from jax.experimental.pallas import tpu as pltpu
from jax.sharding import Mesh
from jax.sharding import PartitionSpec as P

NORM_EPS = 1e-05
UNIT_EPS = 1e-06
ROWS = 256
CHIP = 512
HID = 1024
EMB = 256
WIDE = 384
COLS = HID + EMB + WIDE
LANES = 128
BF = jnp.bfloat16
F32 = jnp.float32
VMEM = pl.BlockSpec(memory_space=pltpu.VMEM)
SMEM = pl.BlockSpec(memory_space=pltpu.SMEM)
ANY = pl.BlockSpec(memory_space=pl.ANY)
PARAMS = pltpu.CompilerParams(vmem_limit_bytes=50 * 1024 * 1024)


def shape(dims, dtype):
    return jax.ShapeDtypeStruct(dims, dtype)


def dot_nn(a, b):
    return lax.dot_general(a, b, (((1,), (0,)), ((), ())), preferred_element_type=F32)


def dot_nt(a, b):
    return lax.dot_general(a, b, (((1,), (1,)), ((), ())), preferred_element_type=F32)


def dot_tn(a, b):
    return lax.dot_general(a, b, (((0,), (0,)), ((), ())), preferred_element_type=F32)


def sigmoid(v):
    return 0.5 + 0.5 * jnp.tanh(0.5 * v)


def call(kernel, outs, in_specs, scratch=(), cost=None):
    specs = [VMEM] * len(outs)
    return pl.pallas_call(
        kernel,
        out_shape=outs,
        in_specs=in_specs,
        out_specs=specs,
        scratch_shapes=list(scratch),
        compiler_params=PARAMS,
        cost_estimate=cost,
    )


def pick_kernel(place, replay, offset, obs, act, keep, send):
    role = place[2]
    index = replay[...]
    ahead = index + offset[...]
    count = obs.shape[0]
    spot = lax.broadcasted_iota(jnp.int32, (count, ROWS), 0)
    for out, rows in (
        (keep, jnp.where(role == 0, index, ahead)),
        (send, jnp.where(role == 0, ahead, index)),
    ):
        hot = jnp.where(spot == rows, 1.0, 0.0).astype(BF)
        out[:, :EMB] = dot_tn(hot, obs[...]).astype(BF)
        extra = dot_tn(hot, act[...])
        pad = jnp.zeros((ROWS, LANES - extra.shape[1]), F32)
        out[:, EMB:] = jnp.concatenate([extra, pad], axis=1).astype(BF)


def by_role(role, pairs, sems):
    for k in range(2):

        @pl.when(role == k)
        def _():
            for n, (sources, target) in enumerate(pairs):
                if sources[k] is not None:
                    pltpu.make_async_copy(sources[k], target, sems.at[n]).start()


def wait_role(role, pairs, sems):
    for k in range(2):

        @pl.when(role == k)
        def _():
            for n, (sources, target) in enumerate(pairs):
                if sources[k] is not None:
                    pltpu.make_async_copy(sources[k], target, sems.at[n]).wait()


def forward_kernel(
    place, keep, recv, sa_obs, sa_act, sa_mid, sa_out, goal_obs, goal_mid, goal_out,
    x, n1, f1, n2, f2, embed, inv, unit,
    w_first, w_mid, w_out, sems,
):
    role = place[2]
    acts = sa_act.shape[0]
    w_first[EMB:, :] = jnp.zeros((WIDE - EMB, HID), BF)
    pairs = [
        ((sa_obs, goal_obs), w_first.at[pl.ds(0, EMB)]),
        ((sa_act, None), w_first.at[pl.ds(EMB, acts)]),
        ((sa_mid, goal_mid), w_mid),
        ((sa_out, goal_out), w_out),
    ]
    by_role(role, pairs, sems)
    own = pl.multiple_of(role * ROWS, ROWS)
    other = pl.multiple_of((1 - role) * ROWS, ROWS)
    x[pl.ds(own, ROWS), :] = keep[...]
    x[pl.ds(other, ROWS), :] = recv[...]
    wait_role(role, pairs, sems)
    for start in range(0, CHIP, LANES):
        rows = pl.ds(start, LANES)

        def norm(values, normed, factor):
            center = values - jnp.mean(values, axis=-1, keepdims=True)
            scale = lax.rsqrt(jnp.mean(center * center, axis=-1, keepdims=True) + NORM_EPS)
            v = center * scale
            normed[rows, :] = v
            factor[rows, :] = scale
            return (v * sigmoid(v)).astype(BF)

        h1 = norm(dot_nn(x[rows, :], w_first[...]), n1, f1)
        h2 = norm(dot_nn(h1, w_mid[...]), n2, f2)
        e = dot_nn(h2, w_out[...])
        scale = lax.rsqrt(jnp.mean(e * e, axis=-1, keepdims=True) + UNIT_EPS)
        embed[rows, :] = e
        inv[rows, :] = scale
        unit[rows, :] = (e * scale * EMB ** (-0.5)).astype(BF)


def to_lanes(values):
    return jnp.sum(values.T, axis=0, keepdims=True)


def score_kernel(n_blocks, first, last, factor, *refs):
    refs = list(refs)
    ours, theirs = refs[:2]
    blocks = refs[2 : 2 + n_blocks]
    refs = refs[2 + n_blocks :]
    if not first:
        old_sum, old_total = refs[:2]
        refs = refs[2:]
    expo, part, total = refs[:3]
    for start in range(0, 2 * CHIP, ROWS):
        source = ours if start < CHIP else theirs
        q = source[pl.ds(start % CHIP, ROWS), :]
        rows = pl.ds(start, ROWS)
        acc = None if first else old_total[rows, :]
        sums = None if first else old_sum[rows, :]
        at = 0
        for block in blocks:
            t = block[...]
            width = t.shape[0]
            e = jnp.exp2(dot_nt(q, t) * factor)
            for lane in range(0, width, LANES):
                piece = e[:, lane : lane + LANES]
                sums = piece if sums is None else sums + piece
            e16 = e.astype(BF)
            expo[rows, at : at + width] = e16
            add = dot_nn(e16, t)
            acc = add if acc is None else acc + add
            at += width
        total[rows, :] = acc
        if last:
            for k in range(ROWS // LANES):
                line = start // LANES + k
                part[line : line + 1, :] = to_lanes(sums[k * LANES : (k + 1) * LANES, :])
        else:
            part[rows, :] = sums


def scores(ours, theirs, blocks, prev, last, factor):
    width = sum(b.shape[0] for b in blocks)
    outs = [
        shape((2 * CHIP, width), BF),
        shape((8, LANES) if last else (2 * CHIP, LANES), F32),
        shape((2 * CHIP, EMB), F32),
    ]
    args = [ours, theirs, *blocks] + list(prev or ())
    kernel = functools.partial(score_kernel, len(blocks), prev is None, last, factor)
    cost = pl.CostEstimate(
        flops=4 * 2 * CHIP * width * EMB,
        bytes_accessed=2 * 2 * CHIP * width + 4 * 2 * CHIP * EMB,
        transcendentals=2 * CHIP * width,
    )
    return call(kernel, outs, [VMEM] * len(args), cost=cost)(*args)


def mix_kernel(n_z, logit, place, sums, total, ours, *refs):
    n_exp = n_z // 2 + 1
    expos = refs[:n_exp]
    blocks = refs[n_exp : n_exp + n_z + 1]
    own, send, loss = refs[n_exp + n_z + 1 : n_exp + n_z + 4]
    lines, scaled = refs[n_exp + n_z + 4 :]
    xh, z, role = place[0], place[1], place[2]

    def full(x_at, z_at, side):
        mine = sums[(x_at * n_z + z_at) * 2 + side]
        partner = sums[((1 - x_at) * n_z + z_at) * 2 + side]
        return mine[:4] + partner[4:]

    order = [0]
    for k in range(1, n_z // 2):
        order += [n_z - k, k]
    order.append(n_z // 2)
    lines[...] = jnp.ones((LANES, LANES), F32)
    for k, shift in enumerate(order):
        lines[4 * k : 4 * k + 4, :] = 1.0 / full(xh, lax.rem(z + shift, n_z), 1 - role)
    mine = full(xh, z, role)
    lines[4 * n_z : 4 * n_z + 4, :] = 1.0 / mine
    lines[4 * n_z + 4 : 4 * n_z + 8, :] = 1.0 / full(1 - xh, z, role)
    columns = lines[...].T

    logs = jnp.log(mine) + jnp.log(full(xh, z, 1 - role))
    logs = jnp.where(role == 0, logs[:2], logs[2:])
    at = pl.multiple_of(role * ROWS, ROWS)
    both = ours[pl.ds(at, ROWS), :].astype(F32) * blocks[0][pl.ds(at, ROWS), :].astype(F32)
    both = both[:, :LANES] + both[:, LANES:]
    for k in range(2):
        positive = logit * to_lanes(both[k * LANES : (k + 1) * LANES, :])
        loss[:, k * LANES : (k + 1) * LANES] = 0.5 * logs[k : k + 1, :] - positive

    at = 0
    for block in blocks:
        for start in range(0, block.shape[0], LANES):
            line = at // LANES
            t = block[pl.ds(start, LANES), :].astype(F32)
            scaled[pl.ds(at, LANES), :] = (t * columns[:, line : line + 1]).astype(BF)
            at += LANES
    for start in range(0, 2 * CHIP, ROWS):
        rows = pl.ds(start, ROWS)
        acc = None
        at = 0
        for expo in expos:
            width = expo.shape[1]
            add = dot_nn(expo[rows, :], scaled[pl.ds(at, width), :])
            acc = add if acc is None else acc + add
            at += width
        for k in range(ROWS // LANES):
            line = 4 * n_z + start // LANES + k
            half = pl.ds(start + k * LANES, LANES)
            value = total[half, :] * columns[:, line : line + 1]
            value = value + acc[k * LANES : (k + 1) * LANES, :]
            if start < CHIP:
                own[half, :] = value
            else:
                send[pl.ds(start - CHIP + k * LANES, LANES), :] = value.astype(BF)


def backward_kernel(
    coef, n_y, place, own, recv, other, embed, inv, n1, f1, n2, f2, x,
    sa_mid, sa_out, goal_mid, goal_out,
    grads,
    w_mid, w_out, ge_s, h1_s, h2_s, p1_s, p2_s, sems,
):
    role = place[2]
    pairs = [((sa_out, goal_out), w_out), ((sa_mid, goal_mid), w_mid)]
    by_role(role, pairs, sems)
    wait_role(role, pairs, sems)
    for start in range(0, CHIP, LANES):
        rows = pl.ds(start, LANES)
        grad = coef * (
            own[rows, :] + recv[rows, :].astype(F32) - 2.0 * other[rows, :].astype(F32)
        )
        e = embed[rows, :]
        scale = inv[rows, :]
        along = jnp.mean(grad * e, axis=-1, keepdims=True)
        ge = (EMB ** (-0.5) * scale * (grad - e * (scale * scale * along))).astype(BF)
        ge_s[rows, :] = ge

        def step(back, normed, factor, hidden, out):
            v = normed[rows, :]
            gate = sigmoid(v)
            h = v * gate
            hidden[rows, :] = h.astype(BF)
            back = back * (gate * (1.0 + v - h))
            mean = jnp.mean(back, axis=-1, keepdims=True)
            tilt = jnp.mean(back * v, axis=-1, keepdims=True)
            pre = (factor[rows, :] * (back - mean - v * tilt)).astype(BF)
            out[rows, :] = pre
            return pre

        p2 = step(dot_nt(ge, w_out[...]), n2, f2, h2_s, p2_s)
        step(dot_nt(p2, w_mid[...]), n1, f1, h1_s, p1_s)
    tall = 256
    for start in range(0, HID, tall):
        span = slice(start, start + tall)
        for left, right, at in ((h1_s, p2_s, 0), (h2_s, ge_s, HID), (p1_s, x, HID + EMB)):
            width = right.shape[1]
            value = dot_tn(left[:, span], right[...])
            value = value.reshape(tall // (8 * n_y), n_y, 8, width)
            for y in range(n_y):
                piece = value[:, y].reshape(tall // n_y, width).astype(BF)
                first = start // n_y
                grads[y, first : first + tall // n_y, at : at + width] = piece


def sum_kernel(parts, order, out):
    value = parts[0].astype(F32)
    for k in range(1, parts.shape[0]):
        value = value + parts[k].astype(F32)
    out[...] = dot_nn(order[...], value.astype(BF)).astype(BF)


def add_kernel(parts, out):
    value = parts[0].astype(F32)
    for k in range(1, parts.shape[0]):
        value = value + parts[k].astype(F32)
    out[...] = value.astype(BF)


def shifted(value, axis, shift):
    count = lax.axis_size(axis)
    return lax.ppermute(value, axis, [(k, (k + shift) % count) for k in range(count)])


def body(
    observations,
    actions,
    replay_index,
    future_offset,
    sa_obs,
    sa_act,
    sa_mid,
    sa_out,
    goal_obs,
    goal_mid,
    goal_out,
):
    n_z, n_y, n_xl = lax.axis_size("z"), lax.axis_size("y"), lax.axis_size("xl")
    logit = 3.0 * math.sqrt(EMB)
    coef = logit / (2.0 * n_y * n_xl)
    role = lax.axis_index("c")
    place = jnp.stack([lax.axis_index("xh"), lax.axis_index("z"), role]).astype(jnp.int32)

    keep, send = call(
        pick_kernel, [shape((ROWS, WIDE), BF)] * 2, [SMEM] + [VMEM] * 4
    )(place, replay_index, future_offset, observations[0], actions[0])
    recv = shifted(send, "c", 1)
    x, n1, f1, n2, f2, embed, inv, unit = call(
        forward_kernel,
        [
            shape((CHIP, WIDE), BF),
            shape((CHIP, HID), F32),
            shape((CHIP, 1), F32),
            shape((CHIP, HID), F32),
            shape((CHIP, 1), F32),
            shape((CHIP, EMB), F32),
            shape((CHIP, 1), F32),
            shape((CHIP, EMB), BF),
        ],
        [SMEM, VMEM, VMEM] + [ANY] * 7,
        scratch=[
            pltpu.VMEM((WIDE, HID), BF),
            pltpu.VMEM((HID, HID), BF),
            pltpu.VMEM((HID, EMB), BF),
            pltpu.SemaphoreType.DMA((4,)),
        ],
    )(place, keep, recv, sa_obs, sa_act, sa_mid, sa_out, goal_obs, goal_mid, goal_out)

    other = shifted(unit, "c", 1)
    ahead = back = other
    theirs = shifted(unit, "xh", 1)
    blocks = [other]
    steps = [[other]]
    for k in range(1, n_z // 2):
        ahead, back = shifted(ahead, "z", 1), shifted(back, "z", -1)
        steps.append([ahead, back])
        blocks += [ahead, back]
    last = [shifted(ahead[:ROWS], "z", 1), shifted(back[ROWS:], "z", -1)]
    steps.append(last)
    blocks += last
    factor = logit * math.log2(math.e)
    expos = []
    prev = None
    for k, step in enumerate(steps):
        expo, part, total = scores(unit, theirs, step, prev, k == len(steps) - 1, factor)
        expos.append(expo)
        prev = (part, total)
    everyone = jnp.broadcast_to(part[None], (4 * n_z, 8, LANES))
    sums = lax.all_to_all(everyone, ("xh", "z", "c"), 0, 0)
    own, partial, loss = call(
        functools.partial(mix_kernel, n_z, logit),
        [shape((CHIP, EMB), F32), shape((CHIP, EMB), BF), shape((1, ROWS), F32)],
        [SMEM] + [VMEM] * (3 + len(expos) + len(blocks)),
        scratch=[pltpu.VMEM((LANES, LANES), F32), pltpu.VMEM((n_z * CHIP, EMB), BF)],
    )(place, sums, total, unit, *expos, *blocks)
    added = shifted(partial, "xh", 1)
    grads = call(
        functools.partial(backward_kernel, coef, n_y),
        [shape((n_y, HID // n_y, COLS), BF)],
        [SMEM] + [VMEM] * 10 + [ANY] * 4,
        scratch=[
            pltpu.VMEM((HID, HID), BF),
            pltpu.VMEM((HID, EMB), BF),
            pltpu.VMEM((CHIP, EMB), BF),
            pltpu.VMEM((CHIP, HID), BF),
            pltpu.VMEM((CHIP, HID), BF),
            pltpu.VMEM((CHIP, HID), BF),
            pltpu.VMEM((CHIP, HID), BF),
            pltpu.SemaphoreType.DMA((2,)),
        ],
    )(place, own, added, other, embed, inv, n1, f1, n2, f2, x, sa_mid, sa_out, goal_mid, goal_out)[0]

    tall = HID // n_y
    r = 8 // n_xl
    source = np.arange(tall).reshape(2, 2 * n_z, n_xl, r).transpose(0, 2, 1, 3).reshape(-1)
    order = jnp.asarray(np.eye(tall, dtype=np.float32)[source], BF)
    grads = lax.all_to_all(grads, "y", 0, 0)
    grads = call(sum_kernel, [shape((tall, COLS), BF)], [VMEM] * 2)(grads, order)[0]
    tall = tall // (2 * n_xl)
    grads = lax.all_to_all(grads.reshape(2 * n_xl, tall, COLS), ("xh", "xl"), 0, 0)
    grads = call(add_kernel, [shape((tall, COLS), BF)], [VMEM])(grads)[0]
    grads = lax.all_to_all(grads.reshape(n_z, 2 * r, COLS), "z", 0, 0)
    grads = jnp.sum(grads.astype(F32), axis=0)
    low, high = grads[:r], grads[r:]
    keep = jnp.where(role == 0, low, high)
    swap = shifted(jnp.where(role == 0, high, low), "c", 1)
    sa = jnp.where(role == 0, keep, swap)
    goal = jnp.where(role == 0, swap, keep)
    acts = sa_act.shape[0]
    low = HID + EMB
    return (
        loss,
        sa[:, low : low + EMB].T,
        sa[:, low + EMB : low + EMB + acts].T,
        sa[:, :HID],
        sa[:, HID:low],
        goal[:, low : low + EMB].T,
        goal[:, :HID],
        goal[:, HID:low],
    )


def solution(mesh):
    fine = Mesh(mesh.devices.reshape(2, -1, 2, mesh.shape["dp"] // 2, 2), ("xh", "z", "c", "y", "xl"))
    neg = ("xh", "z", "c")
    dp = ("y", "xl")
    return jax.shard_map(
        body,
        mesh=fine,
        in_specs=(
            P(dp, neg, None),
            P(dp, neg, None),
            P(dp, neg),
            P(dp, neg),
            P(),
            P(),
            P(),
            P(),
            P(),
            P(),
            P(),
        ),
        out_specs=(
            P(dp, neg),
            P(None, neg + dp),
            P(None, neg + dp),
            P(neg + dp, None),
            P(neg + dp, None),
            P(None, neg + dp),
            P(neg + dp, None),
            P(neg + dp, None),
        ),
        check_vma=False,
    )
```

time: 577 us -> 200 us (0.35)
  waiting for transfers between devices: 413 us -> 26.7 us
  Pallas kernels: 0 us -> 47 us
  matrix products: 40.4 us -> 0 us
  starting transfers between devices: 0.12 us -> 31.8 us
  between operations: 14.5 us -> 0.77 us
  other arithmetic: 7.89 us -> 0.13 us
  blocking collectives: 81.7 us -> 75.8 us
    unnamed x4 -> x0, waiting for transfers between devices: 286 us -> none
    all_gather x2 -> x0, waiting for transfers between devices: 127 us -> none  [the longest x1 90.5 us: body(): lax.all_gather(queries, 'neg', axis=0, tiled=True)]
    all_gather x2 -> x0, blocking collectives: 81.7 us -> none  [the longest x1 42.1 us: body(): every_colsum = lax.all_gather(colsum, 'neg', axis=0, tiled=True)]
    all_to_all x0 -> x3, blocking collectives: none -> 75.8 us  [the longest x1 43.5 us: body(): grads = lax.all_to_all(grads, 'y', 0, 0)]
    pallas_call x0 -> x11, Pallas kernels: none -> 47 us  [the longest x5 14.7 us: scores(): return call(kernel, outs, [VMEM] * len(args), cost=cost)(*args)]
    dot_general x22 -> x0, matrix products: 40.4 us -> none  [the longest x1 7.32 us: body(): jnp.einsum('ce,re->cr', lax.all_gather(queries, 'neg', axis=0, tiled=True...]
    ppermute x0 -> x13, starting transfers between devices: none -> 24.5 us  [shifted(): lax.ppermute(value, axis, [(k, (k + shift) % count) for k in range(count)])]
    ppermute x0 -> x13, waiting for transfers between devices: none -> 17.7 us  [shifted(): lax.ppermute(value, axis, [(k, (k + shift) % count) for k in range(count)])]
  transfers between devices with their start and end apart: 3 -> 14, of which waited for: 3 -> 7; matrix products, arithmetic and copies ran while one was open for 1% -> 0% of each run, Pallas kernels for 0% -> 6%
where the time goes in v1:
time: 200 us; the launch traced here: 199 us
  blocking collectives  75.8 us (38%)
  Pallas kernels  47 us (24%)
  starting transfers between devices  31.8 us (16%)
  waiting for transfers between devices  26.7 us (13%)
  local copies, waits for them, and re-layouts  16.5 us (8%)
    all_to_all x1, blocking collectives, body(): grads = lax.all_to_all(grads, 'y', 0, 0)  43.5 us
    ppermute x13, starting transfers between devices, shifted(): lax.ppermute(value, axis, [(k, (k + shift) % count) for k in range(count)])  24.5 us
    all_to_all x1, blocking collectives, body(): sums = lax.all_to_all(everyone, ('xh', 'z', 'c'), 0, 0)  20.4 us
    ppermute x13, waiting for transfers between devices, shifted(): lax.ppermute(value, axis, [(k, (k + shift) % count) for k in range(count)])  17.7 us
    pallas_call x5, Pallas kernels, scores(): return call(kernel, outs, [VMEM] * len(args), cost=cost)(*args)  14.7 us
    unnamed x35, local copies, waits for them, and re-layouts  14.1 us
    pallas_call x1, Pallas kernels, body(): call(functools.partial(backward_kernel, coef, n_y), [shape((n_y, HID // n...  12.5 us
    all_to_all x1, blocking collectives, body(): lax.all_to_all(grads.reshape(2 * n_xl, tall, COLS), ('xh', 'xl'), 0, 0)  11.9 us
  transfers between devices with their start and end apart: 14, of which 7 were waited for; matrix products, arithmetic and copies ran while one was open for 0% of the time, Pallas kernels for 6%

profile of v1, /device:TPU:1, one launch (start us, length us, event | category | flops | bytes accessed | tf_op | source)
XLA Modules:
  0.0 198.7 jit_solution(8458193431821261445)
XLA Ops:
  4.8 3.3 %collective-permute-start = (bf16[256,384]{1,0:T(8,128)(2,1)S(1)}, bf16[256,384]{1,0:T(8,128)(2,1)S(1)}, u32[]{:S(2)}, u32[]{:S(2)}) collective-permute-start(bf16[256,384]{1,0:T(8,128)(2,1)S(1)} %get-tuple-element.37), channel_id=1, source_target_pairs={{0,8},{8,0},{1,9},{9,1},{2,10},{10,2},{3,11},{11,3},{4,12},{12,4},... | collective-permute-start | bytes 589832 | tf_op jit(solution)/shard_map/ppermute | solution.py:323
  8.1 1.1 collective-permute-done.recv
  9.2 1.0 copy-done
  10.3 1.0 copy-done.7
  11.3 1.0 copy-done.8
  13.1 8.7 %shard_map.180 = (bf16[512,384]{1,0:T(8,128)(2,1)S(1)}, f32[512,1024]{1,0:T(8,128)}, f32[512,1]{1,0:T(8,128)S(1)}, f32[512,1024]{1,0:T(8,128)}, f32[512,1]{1,0:T...) custom-call(s32[3]{0:T(128)S(1)} %pad_add_fusion.place, ...), custom_call_target="tpu_custom_call" | custom-call | tf_op jit(solution)/shard_map/pallas_call | solution.py:349
  22.2 1.2 collective-permute-done.2.refs_2_.refs_5_.other
  23.4 3.8 %collective-permute-start.7 = (bf16[512,256]{1,0:T(8,128)(2,1)S(1)}, bf16[512,256]{1,0:T(8,128)(2,1)S(1)}, u32[]{:S(2)}, u32[]{:S(2)}) collective-permute-start(bf16[512,256]{1,0:T(8,128)(2,1)S(1)} %collective-permute-done.2.refs_2_.refs_5_.other), channel_id=1, source_target_pairs={{0,112},{16,0},{32,16},{48,32},{64,48},{80,64},{96,80},{112,96},{1... | collective-permute-start | bytes 786440 | tf_op jit(solution)/shard_map/ppermute | solution.py:323
  27.3 5.4 %collective-permute-done.7.refs_3_.refs_7_ = bf16[512,256]{1,0:T(8,128)(2,1)S(1)} collective-permute-done((bf16[512,256]{1,0:T(8,128)(2,1)S(1)}, bf16[512,256]{1,0:T(8,128)(2,1)S(1)}, u32[]{:S(2)}, u32[]{:S(2)}) %collective-permute-start.7) | collective-permute-done | bytes 262176 | tf_op jit(solution)/shard_map/ppermute | solution.py:323
  32.6 3.4 %collective-permute-start.8 = (bf16[512,256]{1,0:T(8,128)(2,1)S(1)}, bf16[512,256]{1,0:T(8,128)(2,1)S(1)}, u32[]{:S(2)}, u32[]{:S(2)}) collective-permute-start(bf16[512,256]{1,0:T(8,128)(2,1)S(1)} %collective-permute-done.7.refs_3_.refs_7_), channel_id=1, source_target_pairs={{0,112},{16,0},{32,16},{48,32},{64,48},{80,64},{96,80},{112,96},{1... | collective-permute-start | bytes 786440 | tf_op jit(solution)/shard_map/ppermute | solution.py:323
  36.1 2.7 %collective-permute-start.1 = (bf16[512,256]{1,0:T(8,128)(2,1)S(1)}, bf16[512,256]{1,0:T(8,128)(2,1)S(1)}, u32[]{:S(2)}, u32[]{:S(2)}) collective-permute-start(bf16[512,256]{1,0:T(8,128)(2,1)S(1)} %get-tuple-element.38.refs_0_.ours), channel_id=1, source_target_pairs={{0,128},{128,0},{1,129},{129,1},{2,130},{130,2},{3,131},{131,3},{4... | collective-permute-start | bytes 786440 | tf_op jit(solution)/shard_map/ppermute | solution.py:323
  38.8 1.7 collective-permute-done.8.refs_3_.refs_9_
  40.5 3.4 %collective-permute-start.9 = (bf16[512,256]{1,0:T(8,128)(2,1)S(1)}, bf16[512,256]{1,0:T(8,128)(2,1)S(1)}, u32[]{:S(2)}, u32[]{:S(2)}) collective-permute-start(bf16[512,256]{1,0:T(8,128)(2,1)S(1)} %collective-permute-done.8.refs_3_.refs_9_), channel_id=1, source_target_pairs={{0,112},{16,0},{32,16},{48,32},{64,48},{80,64},{96,80},{112,96},{1... | collective-permute-start | bytes 786440 | tf_op jit(solution)/shard_map/ppermute | solution.py:323
  45.8 1.1 copy-done.14
  46.9 3.8 %shard_map.182 = (bf16[1024,1024]{1,0:T(8,128)(2,1)}, f32[1024,128]{1,0:T(8,128)S(1)}, f32[1024,256]{1,0:T(8,128)S(1)}) custom-call(bf16[512,256]{1,0:T(8,128)(2,1)S(1)} %get-tuple-element.38.refs_0_.ours, bf16[512,256]{1,0:T(8,128)(2,1)S(1)} %collective-permute-done.1.refs_1_, bf16[512,256]{1,0:T(8,128)(2,1)S(1)} %collective-permute-done.3.refs_2_.refs_6_, ...), custom_call_target="tpu_custom_call" | custom-call | flops 1073741824 | bytes 3145728 | tf_op jit(solution)/shard_map/pallas_call | solution.py:195
  51.7 2.7 %collective-permute-start.10 = (bf16[256,256]{1,0:T(8,128)(2,1)S(1)}, bf16[256,256]{1,0:T(8,128)(2,1)S(1)}, u32[]{:S(2)}, u32[]{:S(2)}) collective-permute-start(bf16[256,256]{1,0:T(8,128)(2,1)S(1)} %slice.45), channel_id=1, source_target_pairs={{0,112},{16,0},{32,16},{48,32},{64,48},{80,64},{96,80},{112,96},{1... | collective-permute-start | bytes 393224 | tf_op jit(solution)/shard_map/ppermute | solution.py:323
  54.6 3.9 %shard_map.183 = (bf16[1024,1024]{1,0:T(8,128)(2,1)}, f32[1024,128]{1,0:T(8,128)S(1)}, f32[1024,256]{1,0:T(8,128)S(1)}) custom-call(bf16[512,256]{1,0:T(8,128)(2,1)S(1)} %get-tuple-element.38.refs_0_.ours, bf16[512,256]{1,0:T(8,128)(2,1)S(1)} %collective-permute-done.1.refs_1_, bf16[512,256]{1,0:T(8,128)(2,1)S(1)} %collective-permute-done.4.refs_2_.refs_8_, ...), custom_call_target="tpu_custom_call" | custom-call | flops 1073741824 | bytes 3145728 | tf_op jit(solution)/shard_map/pallas_call | solution.py:195
  58.5 1.0 copy-done.16
  59.5 3.8 %shard_map.184 = (bf16[1024,1024]{1,0:T(8,128)(2,1)}, f32[1024,128]{1,0:T(8,128)S(1)}, f32[1024,256]{1,0:T(8,128)S(1)}) custom-call(bf16[512,256]{1,0:T(8,128)(2,1)S(1)} %get-tuple-element.38.refs_0_.ours, bf16[512,256]{1,0:T(8,128)(2,1)S(1)} %collective-permute-done.1.refs_1_, bf16[512,256]{1,0:T(8,128)(2,1)S(1)} %collective-permute-done.5.refs_2_.refs_10_, ...), custom_call_target="tpu_custom_call" | custom-call | flops 1073741824 | bytes 3145728 | tf_op jit(solution)/shard_map/pallas_call | solution.py:195
  63.3 1.0 copy-done.6
  64.4 2.3 %shard_map.185 = (bf16[1024,512]{1,0:T(8,128)(2,1)S(1)}, f32[8,128]{1,0:T(8,128)S(1)}, f32[1024,256]{1,0:T(8,128)S(1)}) custom-call(bf16[512,256]{1,0:T(8,128)(2,1)S(1)} %get-tuple-element.38.refs_0_.ours, bf16[512,256]{1,0:T(8,128)(2,1)S(1)} %collective-permute-done.1.refs_1_, bf16[256,256]{1,0:T(8,128)(2,1)S(1)} %collective-permute-done.6.refs_2_.refs_12_, ...), custom_call_target="tpu_custom_call" | custom-call | flops 536870912 | bytes 2097152 | tf_op jit(solution)/shard_map/pallas_call | solution.py:195
  67.6 1.0 copy-done.5
  68.6 20.4 %all_to_all.20.sums = f32[32,8,128]{2,1,0:T(8,128)S(1)} all-to-all(f32[32,8,128]{2,1,0:T(8,128)S(1)} %broadcast_in_dim.2), channel_id=1, replica_groups=mesh['xh'=2,'z'=8,'c'=2,'y'=4,'xl'=2] {'xh','z','c'}, dimensions={0} | all-to-all | bytes 262144 | tf_op jit(solution)/shard_map/all_to_all | solution.py:390
  89.0 6.8 %shard_map.186 = (f32[512,256]{1,0:T(8,128)S(1)}, bf16[512,256]{1,0:T(8,128)(2,1)S(1)}, f32[1,256]{1,0:T(1,128)}) custom-call(s32[3]{0:T(128)S(1)} %pad_add_fusion.place, f32[32,8,128]{2,1,0:T(8,128)S(1)} %all_to_all.20.sums, f32[1024,256]{1,0:T(8,128)} %copy-done.5, bf16[512,256]{1,0:T(8,128)(2,1)S(1)} %get-tuple-element.38.refs_0_.ours, ...), custom_call_target="tpu_custom_call" | custom-call | tf_op jit(solution)/shard_map/pallas_call | solution.py:391
  96.0 7.5 %collective-permute-done.11.recv = bf16[512,256]{1,0:T(8,128)(2,1)S(1)} collective-permute-done((bf16[512,256]{1,0:T(8,128)(2,1)S(1)}, bf16[512,256]{1,0:T(8,128)(2,1)S(1)}, u32[]{:S(2)}, u32[]{:S(2)}) %collective-permute-start.11) | collective-permute-done | bytes 262176 | tf_op jit(solution)/shard_map/ppermute | solution.py:323
  103.5 12.5 %shard_map.187 = bf16[4,256,1664]{2,1,0:T(8,128)(2,1)} custom-call(s32[3]{0:T(128)S(1)} %pad_add_fusion.place, f32[512,256]{1,0:T(8,128)S(1)} %get-tuple-element.55.own, bf16[512,256]{1,0:T(8,128)(2,1)S(1)} %collective-permute-done.11.recv, bf16[512,256]{1,0:T(8,128)(2,1)S(1)} %collective-permute-done.2.refs_2_.refs_5_.other, ...), custom_call_target="tpu_custom_call" | custom-call | tf_op jit(solution)/shard_map/pallas_call | solution.py:398
  116.0 43.5 %all_to_all.21.parts = bf16[4,256,1664]{2,1,0:T(8,128)(2,1)} all-to-all(bf16[4,256,1664]{2,1,0:T(8,128)(2,1)} %shard_map.187), channel_id=1, replica_groups=mesh['xh'=2,'z'=8,'c'=2,'y'=4,'xl'=2] {'y'}, dimensions={0} | all-to-all | bytes 6815744 | tf_op jit(solution)/shard_map/all_to_all | solution.py:418
  159.4 2.7 %shard_map.188 = bf16[256,1664]{1,0:T(8,128)(2,1)S(1)} custom-call(bf16[4,256,1664]{2,1,0:T(8,128)(2,1)} %all_to_all.21.parts, bf16[256,256]{1,0:T(8,128)(2,1)S(1)} %copy-done.10), custom_call_target="tpu_custom_call" | custom-call | tf_op jit(solution)/shard_map/pallas_call | solution.py:419
  162.1 11.9 %all_to_all.22.parts = bf16[4,64,1664]{2,1,0:T(8,128)(2,1)S(1)} all-to-all(bf16[4,64,1664]{2,1,0:T(8,128)(2,1)S(1)} %bitcast.13), channel_id=1, replica_groups=mesh['xh'=2,'z'=8,'c'=2,'y'=4,'xl'=2] {'xh','xl'}, dimensions={0} | all-to-all | bytes 1703936 | tf_op jit(solution)/shard_map/all_to_all | solution.py:421
  174.8 7.3 %all-to-all-start.3 = ((bf16[8,8,1664]{2,1,0:T(8,128)(2,1)}), bf16[8,8,1664]{2,1,0:T(8,128)(2,1)S(1)}, u32[]{:S(2)}, u32[]{:S(2)}) async-start(bf16[8,8,1664]{2,1,0:T(8,128)(2,1)} %bitcast.6), calls=%async_computation.3 | async-start | bytes 425984 | tf_op jit(solution)/shard_map/all_to_all | solution.py:423
  182.1 8.9 %all-to-all-done.3 = bf16[8,8,1664]{2,1,0:T(8,128)(2,1)S(1)} async-done(((bf16[8,8,1664]{2,1,0:T(8,128)(2,1)}), bf16[8,8,1664]{2,1,0:T(8,128)(2,1)S(1)}, u32[]{:S(2)}, u32[]{:S(2)}) %all-to-all-start.3) | async-done | bytes 213024 | tf_op jit(solution)/shard_map/all_to_all | solution.py:423
  191.1 4.4 %collective-permute-start.12 = (f32[4,1664]{1,0:T(4,128)S(1)}, f32[4,1664]{1,0:T(4,128)S(1)}, u32[]{:S(2)}, u32[]{:S(2)}) collective-permute-start(f32[4,1664]{1,0:T(4,128)S(1)} %slice_select_fusion), channel_id=1, source_target_pairs={{0,8},{8,0},{1,9},{9,1},{2,10},{10,2},{3,11},{11,3},{4,12},{12,4},... | collective-permute-start | bytes 79880 | tf_op jit(solution)/shard_map/ppermute | solution.py:323
  (56 shorter events, 13.6 us)
Async XLA Ops:
  1.5 0.9 copy-start.9
  2.5 0.7 copy-start.12
  3.1 0.7 copy-start.13
  4.8 4.4 %collective-permute-start = (bf16[256,384]{1,0:T(8,128)(2,1)S(1)}, bf16[256,384]{1,0:T(8,128)(2,1)S(1)}, u32[]{:S(2)}, u32[]{:S(2)}) collective-permute-start(bf16[256,384]{1,0:T(8,128)(2,1)S(1)} %get-tuple-element.37), channel_id=1, source_target_pairs={{0,8},{8,0},{1,9},{9,1},{2,10},{10,2},{3,11},{11,3},{4,12},{12,4},... | collective-permute-start | bytes 589832 | tf_op jit(solution)/shard_map/ppermute | solution.py:323
  9.2 1.0 copy-start
  10.3 1.0 copy-start.7
  11.3 1.0 copy-start.8
  12.3 0.8 copy-start.11
  21.8 1.6 collective-permute-start.2
  23.4 9.2 %collective-permute-start.7 = (bf16[512,256]{1,0:T(8,128)(2,1)S(1)}, bf16[512,256]{1,0:T(8,128)(2,1)S(1)}, u32[]{:S(2)}, u32[]{:S(2)}) collective-permute-start(bf16[512,256]{1,0:T(8,128)(2,1)S(1)} %collective-permute-done.2.refs_2_.refs_5_.other), channel_id=1, source_target_pairs={{0,112},{16,0},{32,16},{48,32},{64,48},{80,64},{96,80},{112,96},{1... | collective-permute-start | bytes 786440 | tf_op jit(solution)/shard_map/ppermute | solution.py:323
  27.3 8.8 %collective-permute-start.3 = (bf16[512,256]{1,0:T(8,128)(2,1)S(1)}, bf16[512,256]{1,0:T(8,128)(2,1)S(1)}, u32[]{:S(2)}, u32[]{:S(2)}) collective-permute-start(bf16[512,256]{1,0:T(8,128)(2,1)S(1)} %collective-permute-done.2.refs_2_.refs_5_.other), channel_id=1, source_target_pairs={{0,16},{16,32},{32,48},{48,64},{64,80},{80,96},{96,112},{112,0},{1... | collective-permute-start | bytes 786440 | tf_op jit(solution)/shard_map/ppermute | solution.py:323
  32.6 7.9 %collective-permute-start.8 = (bf16[512,256]{1,0:T(8,128)(2,1)S(1)}, bf16[512,256]{1,0:T(8,128)(2,1)S(1)}, u32[]{:S(2)}, u32[]{:S(2)}) collective-permute-start(bf16[512,256]{1,0:T(8,128)(2,1)S(1)} %collective-permute-done.7.refs_3_.refs_7_), channel_id=1, source_target_pairs={{0,112},{16,0},{32,16},{48,32},{64,48},{80,64},{96,80},{112,96},{1... | collective-permute-start | bytes 786440 | tf_op jit(solution)/shard_map/ppermute | solution.py:323
  36.1 7.9 %collective-permute-start.4 = (bf16[512,256]{1,0:T(8,128)(2,1)S(1)}, bf16[512,256]{1,0:T(8,128)(2,1)S(1)}, u32[]{:S(2)}, u32[]{:S(2)}) collective-permute-start(bf16[512,256]{1,0:T(8,128)(2,1)S(1)} %collective-permute-done.3.refs_2_.refs_6_), channel_id=1, source_target_pairs={{0,16},{16,32},{32,48},{48,64},{64,80},{80,96},{96,112},{112,0},{1... | collective-permute-start | bytes 786440 | tf_op jit(solution)/shard_map/ppermute | solution.py:323
  36.1 7.9 %collective-permute-start.1 = (bf16[512,256]{1,0:T(8,128)(2,1)S(1)}, bf16[512,256]{1,0:T(8,128)(2,1)S(1)}, u32[]{:S(2)}, u32[]{:S(2)}) collective-permute-start(bf16[512,256]{1,0:T(8,128)(2,1)S(1)} %get-tuple-element.38.refs_0_.ours), channel_id=1, source_target_pairs={{0,128},{128,0},{1,129},{129,1},{2,130},{130,2},{3,131},{131,3},{4... | collective-permute-start | bytes 786440 | tf_op jit(solution)/shard_map/ppermute | solution.py:323
  40.5 11.2 %collective-permute-start.9 = (bf16[512,256]{1,0:T(8,128)(2,1)S(1)}, bf16[512,256]{1,0:T(8,128)(2,1)S(1)}, u32[]{:S(2)}, u32[]{:S(2)}) collective-permute-start(bf16[512,256]{1,0:T(8,128)(2,1)S(1)} %collective-permute-done.8.refs_3_.refs_9_), channel_id=1, source_target_pairs={{0,112},{16,0},{32,16},{48,32},{64,48},{80,64},{96,80},{112,96},{1... | collective-permute-start | bytes 786440 | tf_op jit(solution)/shard_map/ppermute | solution.py:323
  43.9 10.6 %collective-permute-start.5 = (bf16[512,256]{1,0:T(8,128)(2,1)S(1)}, bf16[512,256]{1,0:T(8,128)(2,1)S(1)}, u32[]{:S(2)}, u32[]{:S(2)}) collective-permute-start(bf16[512,256]{1,0:T(8,128)(2,1)S(1)} %collective-permute-done.4.refs_2_.refs_8_), channel_id=1, source_target_pairs={{0,16},{16,32},{32,48},{48,64},{64,80},{80,96},{96,112},{112,0},{1... | collective-permute-start | bytes 786440 | tf_op jit(solution)/shard_map/ppermute | solution.py:323
  44.8 1.0 copy-start.3
  45.8 1.1 copy-start.14
  50.7 1.0 copy-start.15
  51.7 12.6 %collective-permute-start.10 = (bf16[256,256]{1,0:T(8,128)(2,1)S(1)}, bf16[256,256]{1,0:T(8,128)(2,1)S(1)}, u32[]{:S(2)}, u32[]{:S(2)}) collective-permute-start(bf16[256,256]{1,0:T(8,128)(2,1)S(1)} %slice.45), channel_id=1, source_target_pairs={{0,112},{16,0},{32,16},{48,32},{64,48},{80,64},{96,80},{112,96},{1... | collective-permute-start | bytes 393224 | tf_op jit(solution)/shard_map/ppermute | solution.py:323
  54.5 9.9 %collective-permute-start.6 = (bf16[256,256]{1,0:T(8,128)(2,1)S(1)}, bf16[256,256]{1,0:T(8,128)(2,1)S(1)}, u32[]{:S(2)}, u32[]{:S(2)}) collective-permute-start(bf16[256,256]{1,0:T(8,128)(2,1)S(1)} %slice.44), channel_id=1, source_target_pairs={{0,16},{16,32},{32,48},{48,64},{64,80},{80,96},{96,112},{112,0},{1... | collective-permute-start | bytes 393224 | tf_op jit(solution)/shard_map/ppermute | solution.py:323
  58.5 1.0 copy-start.16
  63.3 1.0 copy-start.6
  66.6 1.0 copy-start.4
  67.6 1.0 copy-start.5
  89.0 14.5 %copy-start.1 = (bf16[1024,256]{1,0:T(8,128)(2,1)S(1)}, bf16[1024,256]{1,0:T(8,128)(2,1)}, u32[]{:S(2)}) copy-start(bf16[1024,256]{1,0:T(8,128)(2,1)} %sa_out.3) | copy-start | bytes 1572868
  89.0 14.5 %copy-start.2 = (bf16[1024,256]{1,0:T(8,128)(2,1)S(1)}, bf16[1024,256]{1,0:T(8,128)(2,1)}, u32[]{:S(2)}) copy-start(bf16[1024,256]{1,0:T(8,128)(2,1)} %goal_out.3) | copy-start | bytes 1572868
  95.8 7.7 %collective-permute-start.11 = (bf16[512,256]{1,0:T(8,128)(2,1)S(1)}, bf16[512,256]{1,0:T(8,128)(2,1)S(1)}, u32[]{:S(2)}, u32[]{:S(2)}) collective-permute-start(bf16[512,256]{1,0:T(8,128)(2,1)S(1)} %get-tuple-element.56), channel_id=1, source_target_pairs={{0,128},{128,0},{1,129},{129,1},{2,130},{130,2},{3,131},{131,3},{4... | collective-permute-start | bytes 786440 | tf_op jit(solution)/shard_map/ppermute | solution.py:323
  115.9 43.5 %copy-start.10 = (bf16[256,256]{1,0:T(8,128)(2,1)S(1)}, bf16[256,256]{1,0:T(8,128)(2,1)}, u32[]{:S(2)}) copy-start(bf16[256,256]{1,0:T(8,128)(2,1)} %constant.20.clone.order) | copy-start | bytes 393220
  174.8 16.2 %all-to-all-start.3 = ((bf16[8,8,1664]{2,1,0:T(8,128)(2,1)}), bf16[8,8,1664]{2,1,0:T(8,128)(2,1)S(1)}, u32[]{:S(2)}, u32[]{:S(2)}) async-start(bf16[8,8,1664]{2,1,0:T(8,128)(2,1)} %bitcast.6), calls=%async_computation.3 | async-start | bytes 425984 | tf_op jit(solution)/shard_map/all_to_all | solution.py:423
  191.1 5.2 %collective-permute-start.12 = (f32[4,1664]{1,0:T(4,128)S(1)}, f32[4,1664]{1,0:T(4,128)S(1)}, u32[]{:S(2)}, u32[]{:S(2)}) collective-permute-start(f32[4,1664]{1,0:T(4,128)S(1)} %slice_select_fusion), channel_id=1, source_target_pairs={{0,8},{8,0},{1,9},{9,1},{2,10},{10,2},{3,11},{11,3},{4,12},{12,4},... | collective-permute-start | bytes 79880 | tf_op jit(solution)/shard_map/ppermute | solution.py:323

commit v2 on v1

--- a/solution.py
+++ b/solution.py
@@ -3,7 +3,6 @@
 
 import jax
 import jax.numpy as jnp
-import numpy as np
 from jax import lax
 from jax.experimental import pallas as pl
 from jax.experimental.pallas import tpu as pltpu
@@ -17,14 +16,14 @@
 HID = 1024
 EMB = 256
 WIDE = 384
-COLS = HID + EMB + WIDE
+TILES = (HID + 2 * EMB) // 128
 LANES = 128
 BF = jnp.bfloat16
 F32 = jnp.float32
 VMEM = pl.BlockSpec(memory_space=pltpu.VMEM)
 SMEM = pl.BlockSpec(memory_space=pltpu.SMEM)
-ANY = pl.BlockSpec(memory_space=pl.ANY)
-PARAMS = pltpu.CompilerParams(vmem_limit_bytes=50 * 1024 * 1024)
+HBM = pl.BlockSpec(memory_space=pltpu.HBM)
+PARAMS = pltpu.CompilerParams(vmem_limit_bytes=20 * 1024 * 1024)
 
 
 def shape(dims, dtype):
@@ -60,21 +59,30 @@
     )
 
 
-def pick_kernel(place, replay, offset, obs, act, keep, send):
+def pick_kernel(place, replay, offset, obs, act, keep, send, replay_s, offset_s, obs_s, act_s, sems):
+    copies = [
+        pltpu.make_async_copy(source, target, sems.at[n])
+        for n, (source, target) in enumerate(
+            ((replay, replay_s), (offset, offset_s), (obs, obs_s), (act, act_s))
+        )
+    ]
+    for copy in copies:
+        copy.start()
+    for copy in copies:
+        copy.wait()
     role = place[2]
-    index = replay[...]
-    ahead = index + offset[...]
-    count = obs.shape[0]
-    spot = lax.broadcasted_iota(jnp.int32, (count, ROWS), 0)
+    index = replay_s[...]
+    ahead = index + offset_s[...]
+    spot = lax.broadcasted_iota(jnp.int32, (obs_s.shape[0], ROWS), 0)
     for out, rows in (
         (keep, jnp.where(role == 0, index, ahead)),
         (send, jnp.where(role == 0, ahead, index)),
     ):
         hot = jnp.where(spot == rows, 1.0, 0.0).astype(BF)
-        out[:, :EMB] = dot_tn(hot, obs[...]).astype(BF)
-        extra = dot_tn(hot, act[...])
-        pad = jnp.zeros((ROWS, LANES - extra.shape[1]), F32)
-        out[:, EMB:] = jnp.concatenate([extra, pad], axis=1).astype(BF)
+        out[:, :EMB] = dot_tn(hot, obs_s[...]).astype(BF)
+        extra = dot_nn(act_s[...], hot)
+        copies = LANES // extra.shape[0]
+        out[:, EMB:] = jnp.concatenate([extra] * copies, axis=0).T.astype(BF)
 
 
 def by_role(role, pairs, sems):
@@ -87,14 +95,14 @@
                     pltpu.make_async_copy(sources[k], target, sems.at[n]).start()
 
 
-def wait_role(role, pairs, sems):
+def wait_role(role, pairs, sems, first):
     for k in range(2):
 
         @pl.when(role == k)
         def _():
             for n, (sources, target) in enumerate(pairs):
                 if sources[k] is not None:
-                    pltpu.make_async_copy(sources[k], target, sems.at[n]).wait()
+                    pltpu.make_async_copy(sources[k], target, sems.at[first + n]).wait()
 
 
 def forward_kernel(
@@ -116,7 +124,6 @@
     other = pl.multiple_of((1 - role) * ROWS, ROWS)
     x[pl.ds(own, ROWS), :] = keep[...]
     x[pl.ds(other, ROWS), :] = recv[...]
-    wait_role(role, pairs, sems)
     for start in range(0, CHIP, LANES):
         rows = pl.ds(start, LANES)
 
@@ -128,7 +135,11 @@
             factor[rows, :] = scale
             return (v * sigmoid(v)).astype(BF)
 
+        if start == 0:
+            wait_role(role, pairs[:2], sems, 0)
         h1 = norm(dot_nn(x[rows, :], w_first[...]), n1, f1)
+        if start == 0:
+            wait_role(role, pairs[2:], sems, 2)
         h2 = norm(dot_nn(h1, w_mid[...]), n2, f2)
         e = dot_nn(h2, w_out[...])
         scale = lax.rsqrt(jnp.mean(e * e, axis=-1, keepdims=True) + UNIT_EPS)
@@ -195,12 +206,26 @@
     return call(kernel, outs, [VMEM] * len(args), cost=cost)(*args)
 
 
-def mix_kernel(n_z, logit, place, sums, total, ours, *refs):
+def mix_rows(expos, scaled, total, columns, line, start, write):
+    acc = None
+    at = 0
+    for expo in expos:
+        width = expo.shape[1]
+        add = dot_nn(expo[pl.ds(start, ROWS), :], scaled[pl.ds(at, width), :])
+        acc = add if acc is None else acc + add
+        at += width
+    for k in range(ROWS // LANES):
+        here = line + start // LANES + k
+        value = total[pl.ds(start + k * LANES, LANES), :] * columns[:, here : here + 1]
+        write(start + k * LANES, value + acc[k * LANES : (k + 1) * LANES, :])
+
+
+def send_kernel(n_z, logit, place, sums, total, ours, *refs):
     n_exp = n_z // 2 + 1
     expos = refs[:n_exp]
     blocks = refs[n_exp : n_exp + n_z + 1]
-    own, send, loss = refs[n_exp + n_z + 1 : n_exp + n_z + 4]
-    lines, scaled = refs[n_exp + n_z + 4 :]
+    send, scaled, across, loss = refs[n_exp + n_z + 1 : n_exp + n_z + 5]
+    lines = refs[n_exp + n_z + 5]
     xh, z, role = place[0], place[1], place[2]
 
     def full(x_at, z_at, side):
@@ -219,6 +244,21 @@
     lines[4 * n_z : 4 * n_z + 4, :] = 1.0 / mine
     lines[4 * n_z + 4 : 4 * n_z + 8, :] = 1.0 / full(1 - xh, z, role)
     columns = lines[...].T
+    across[...] = columns
+
+    at = 0
+    for block in blocks:
+        for start in range(0, block.shape[0], LANES):
+            line = at // LANES
+            t = block[pl.ds(start, LANES), :].astype(F32)
+            scaled[pl.ds(at, LANES), :] = (t * columns[:, line : line + 1]).astype(BF)
+            at += LANES
+
+    def write(start, value):
+        send[pl.ds(start - CHIP, LANES), :] = value.astype(BF)
+
+    for start in range(CHIP, 2 * CHIP, ROWS):
+        mix_rows(expos, scaled, total, columns, 4 * n_z, start, write)
 
     logs = jnp.log(mine) + jnp.log(full(xh, z, 1 - role))
     logs = jnp.where(role == 0, logs[:2], logs[2:])
@@ -229,35 +269,20 @@
         positive = logit * to_lanes(both[k * LANES : (k + 1) * LANES, :])
         loss[:, k * LANES : (k + 1) * LANES] = 0.5 * logs[k : k + 1, :] - positive
 
-    at = 0
-    for block in blocks:
-        for start in range(0, block.shape[0], LANES):
-            line = at // LANES
-            t = block[pl.ds(start, LANES), :].astype(F32)
-            scaled[pl.ds(at, LANES), :] = (t * columns[:, line : line + 1]).astype(BF)
-            at += LANES
-    for start in range(0, 2 * CHIP, ROWS):
-        rows = pl.ds(start, ROWS)
-        acc = None
-        at = 0
-        for expo in expos:
-            width = expo.shape[1]
-            add = dot_nn(expo[rows, :], scaled[pl.ds(at, width), :])
-            acc = add if acc is None else acc + add
-            at += width
-        for k in range(ROWS // LANES):
-            line = 4 * n_z + start // LANES + k
-            half = pl.ds(start + k * LANES, LANES)
-            value = total[half, :] * columns[:, line : line + 1]
-            value = value + acc[k * LANES : (k + 1) * LANES, :]
-            if start < CHIP:
-                own[half, :] = value
-            else:
-                send[pl.ds(start - CHIP + k * LANES, LANES), :] = value.astype(BF)
+
+def own_kernel(n_z, total, scaled, across, *refs):
+    expos, own = refs[:-1], refs[-1]
+    columns = across[...]
+
+    def write(start, value):
+        own[pl.ds(start, LANES), :] = value
+
+    for start in range(0, CHIP, ROWS):
+        mix_rows(expos, scaled, total, columns, 4 * n_z, start, write)
 
 
 def backward_kernel(
-    coef, n_y, place, own, recv, other, embed, inv, n1, f1, n2, f2, x,
+    coef, place, own, recv, other, embed, inv, n1, f1, n2, f2, x,
     sa_mid, sa_out, goal_mid, goal_out,
     grads,
     w_mid, w_out, ge_s, h1_s, h2_s, p1_s, p2_s, sems,
@@ -265,7 +290,6 @@
     role = place[2]
     pairs = [((sa_out, goal_out), w_out), ((sa_mid, goal_mid), w_mid)]
     by_role(role, pairs, sems)
-    wait_role(role, pairs, sems)
     for start in range(0, CHIP, LANES):
         rows = pl.ds(start, LANES)
         grad = coef * (
@@ -289,33 +313,85 @@
             out[rows, :] = pre
             return pre
 
+        if start == 0:
+            wait_role(role, pairs[:1], sems, 0)
         p2 = step(dot_nt(ge, w_out[...]), n2, f2, h2_s, p2_s)
+        if start == 0:
+            wait_role(role, pairs[1:], sems, 1)
         step(dot_nt(p2, w_mid[...]), n1, f1, h1_s, p1_s)
     tall = 256
+    unit = lax.broadcasted_iota(jnp.int32, (tall, tall), 1)
+    origin = (unit // 4 % 8) * 32 + unit // 64 * 8 + (unit // 32 % 2) * 4 + unit % 4
+    order = jnp.where(lax.broadcasted_iota(jnp.int32, (tall, tall), 0) == origin, 1.0, 0.0).astype(BF)
+    line = lax.broadcasted_iota(jnp.int32, (tall, LANES), 0)
+    lane = lax.broadcasted_iota(jnp.int32, (tall, LANES), 1)
+    wanted = lane // 16 == (line // 32 % 2) * 4 + line % 4
+    pack_row = lax.broadcasted_iota(jnp.int32, (32, tall), 0)
+    pack_col = lax.broadcasted_iota(jnp.int32, (32, tall), 1)
+    pack = (pack_col // 64 == pack_row // 8) & (pack_col // 4 % 8 == pack_row % 8)
+    pack = jnp.where(pack, 1.0, 0.0).astype(BF)
+    packed = []
     for start in range(0, HID, tall):
         span = slice(start, start + tall)
-        for left, right, at in ((h1_s, p2_s, 0), (h2_s, ge_s, HID), (p1_s, x, HID + EMB)):
-            width = right.shape[1]
-            value = dot_tn(left[:, span], right[...])
-            value = value.reshape(tall // (8 * n_y), n_y, 8, width)
-            for y in range(n_y):
-                piece = value[:, y].reshape(tall // n_y, width).astype(BF)
-                first = start // n_y
-                grads[y, first : first + tall // n_y, at : at + width] = piece
-
-
-def sum_kernel(parts, order, out):
-    value = parts[0].astype(F32)
+        xh, half = start // tall // 2, start // tall % 2
+        for left, right, tile in ((h1_s, p2_s, 0), (h2_s, ge_s, 8), (p1_s, x, 10)):
+            units = dot_nn(left[:, span], order).astype(BF)
+            value = dot_tn(units, right[:, : right.shape[1] // EMB * EMB])
+            for k in range(value.shape[1] // LANES):
+                for part in range(8):
+                    piece = value[part * 32 : part * 32 + 32, k * LANES : (k + 1) * LANES]
+                    at = (tile + k) * 64 + half * 32
+                    dest = part // 2 * 4 + xh * 2 + part % 2
+                    grads[dest, at : at + 32, :] = piece.astype(BF)
+            if tile == 10:
+                value = jnp.where(wanted, dot_tn(units, x[:, EMB:]), 0.0).astype(BF)
+                packed.append(dot_nn(pack, value))
+    for dest in range(16):
+        y, xh = dest // 4, dest // 2 % 2
+        two = [packed[2 * xh + half][y * 8 : y * 8 + 8] for half in range(2)]
+        grads[dest, TILES * 64 : TILES * 64 + 16, :] = jnp.concatenate(two, axis=0).astype(BF)
+
+
+def plus(parts, rows):
+    value = parts[0, rows, :].astype(F32)
     for k in range(1, parts.shape[0]):
-        value = value + parts[k].astype(F32)
-    out[...] = dot_nn(order[...], value.astype(BF)).astype(BF)
-
-
-def add_kernel(parts, out):
-    value = parts[0].astype(F32)
-    for k in range(1, parts.shape[0]):
-        value = value + parts[k].astype(F32)
-    out[...] = value.astype(BF)
+        value = value + parts[k, rows, :].astype(F32)
+    return value
+
+
+def sum_kernel(parts, out):
+    tiles = [plus(parts, pl.ds(k * 64, 64)) for k in range(TILES)]
+    extra = plus(parts, pl.ds(TILES * 64, 16))
+    for z in range(out.shape[0]):
+        rows = [tile[z * 8 : z * 8 + 8] for tile in tiles] + [extra]
+        out[z] = jnp.concatenate(rows, axis=0).astype(BF)
+
+
+def split_kernel(place, parts, keep, send, extra):
+    role = place[2]
+    value = plus(parts, slice(None))
+    extra[...] = value[TILES * 8 :]
+    for k in range(TILES):
+        low, high = value[k * 8 : k * 8 + 4], value[k * 8 + 4 : k * 8 + 8]
+        keep[k * 4 : k * 4 + 4, :] = jnp.where(role == 0, low, high)
+        send[k * 4 : k * 4 + 4, :] = jnp.where(role == 0, high, low)
+    blank = jnp.zeros((8, LANES), F32)
+    for out, side in ((keep, role), (send, 1 - role)):
+        out[TILES * 4 :, :] = blank + extra[pl.ds(place[1] * 2 + side, 1), :]
+
+
+def last_kernel(place, keep, recv, obs_a, act_a, mid_a, out_a, obs_b, mid_b, out_b):
+    role, xl = place[2], place[3]
+    sa = jnp.where(role == 0, keep[...], recv[...])
+    goal = jnp.where(role == 0, recv[...], keep[...])
+    for value, mid, out, obs in ((sa, mid_a, out_a, obs_a), (goal, mid_b, out_b, obs_b)):
+        for k in range(TILES):
+            target, at = (mid, k) if k < 8 else (out, k - 8) if k < 10 else (obs, k - 10)
+            target[:, at * LANES : (at + 1) * LANES] = value[k * 4 : k * 4 + 4]
+    line = sa[TILES * 4 : TILES * 4 + 1]
+    line = jnp.where(xl == 0, line[:, :64], line[:, 64:])
+    for r in range(4):
+        act_a[r : r + 1, :] = line[:, r * 16 : r * 16 + 16]
 
 
 def shifted(value, axis, shift):
@@ -336,15 +412,31 @@
     goal_mid,
     goal_out,
 ):
-    n_z, n_y, n_xl = lax.axis_size("z"), lax.axis_size("y"), lax.axis_size("xl")
+    n_z = lax.axis_size("z")
+    weights = (sa_obs, sa_act, sa_mid, sa_out, goal_obs, goal_mid, goal_out)
+    sa_obs, sa_act, sa_mid, sa_out, goal_obs, goal_mid, goal_out = (
+        pltpu.with_memory_space_constraint(weight, pltpu.HBM) for weight in weights
+    )
+    slabs = (replay_index, future_offset, observations[0], actions[0].T)
+    slabs = [pltpu.with_memory_space_constraint(slab, pltpu.HBM) for slab in slabs]
     logit = 3.0 * math.sqrt(EMB)
-    coef = logit / (2.0 * n_y * n_xl)
-    role = lax.axis_index("c")
-    place = jnp.stack([lax.axis_index("xh"), lax.axis_index("z"), role]).astype(jnp.int32)
-
+    coef = logit / (2.0 * lax.axis_size("y") * lax.axis_size("xl"))
+    place = jnp.stack([lax.axis_index(axis) for axis in ("xh", "z", "c", "xl")]).astype(jnp.int32)
+
+    acts = actions.shape[2]
+    tall = observations.shape[1]
     keep, send = call(
-        pick_kernel, [shape((ROWS, WIDE), BF)] * 2, [SMEM] + [VMEM] * 4
-    )(place, replay_index, future_offset, observations[0], actions[0])
+        pick_kernel,
+        [shape((ROWS, WIDE), BF)] * 2,
+        [SMEM] + [HBM] * 4,
+        scratch=[
+            pltpu.VMEM((1, ROWS), jnp.int32),
+            pltpu.VMEM((1, ROWS), jnp.int32),
+            pltpu.VMEM((tall, EMB), BF),
+            pltpu.VMEM((acts, tall), BF),
+            pltpu.SemaphoreType.DMA((4,)),
+        ],
+    )(place, *slabs)
     recv = shifted(send, "c", 1)
     x, n1, f1, n2, f2, embed, inv, unit = call(
         forward_kernel,
@@ -358,7 +450,7 @@
             shape((CHIP, 1), F32),
             shape((CHIP, EMB), BF),
         ],
-        [SMEM, VMEM, VMEM] + [ANY] * 7,
+        [SMEM, VMEM, VMEM] + [HBM] * 7,
         scratch=[
             pltpu.VMEM((WIDE, HID), BF),
             pltpu.VMEM((HID, HID), BF),
@@ -370,35 +462,52 @@
     other = shifted(unit, "c", 1)
     ahead = back = other
     theirs = shifted(unit, "xh", 1)
-    blocks = [other]
     steps = [[other]]
-    for k in range(1, n_z // 2):
-        ahead, back = shifted(ahead, "z", 1), shifted(back, "z", -1)
-        steps.append([ahead, back])
-        blocks += [ahead, back]
-    last = [shifted(ahead[:ROWS], "z", 1), shifted(back[ROWS:], "z", -1)]
-    steps.append(last)
-    blocks += last
     factor = logit * math.log2(math.e)
     expos = []
     prev = None
-    for k, step in enumerate(steps):
-        expo, part, total = scores(unit, theirs, step, prev, k == len(steps) - 1, factor)
+    for k in range(n_z // 2 + 1):
+        if k < n_z // 2 - 1:
+            ahead, back = shifted(ahead, "z", 1), shifted(back, "z", -1)
+            steps.append([ahead, back])
+        elif k == n_z // 2 - 1:
+            steps.append([shifted(ahead[:ROWS], "z", 1), shifted(back[ROWS:], "z", -1)])
+        expo, part, total = scores(unit, theirs, steps[k], prev, k == n_z // 2, factor)
         expos.append(expo)
         prev = (part, total)
+        if k < n_z // 2 - 1:
+            ahead, back, part, total = lax.optimization_barrier((ahead, back, part, total))
+            steps[-1] = [ahead, back]
+            prev = (part, total)
+    blocks = [block for step in steps for block in step]
     everyone = jnp.broadcast_to(part[None], (4 * n_z, 8, LANES))
     sums = lax.all_to_all(everyone, ("xh", "z", "c"), 0, 0)
-    own, partial, loss = call(
-        functools.partial(mix_kernel, n_z, logit),
-        [shape((CHIP, EMB), F32), shape((CHIP, EMB), BF), shape((1, ROWS), F32)],
+    partial, scaled, across, loss = call(
+        functools.partial(send_kernel, n_z, logit),
+        [
+            shape((CHIP, EMB), BF),
+            shape((n_z * CHIP, EMB), BF),
+            shape((LANES, LANES), F32),
+            shape((1, ROWS), F32),
+        ],
         [SMEM] + [VMEM] * (3 + len(expos) + len(blocks)),
-        scratch=[pltpu.VMEM((LANES, LANES), F32), pltpu.VMEM((n_z * CHIP, EMB), BF)],
+        scratch=[pltpu.VMEM((LANES, LANES), F32)],
     )(place, sums, total, unit, *expos, *blocks)
     added = shifted(partial, "xh", 1)
+    own = call(
+        functools.partial(own_kernel, n_z),
+        [shape((CHIP, EMB), F32)],
+        [VMEM] * (3 + len(expos)),
+        cost=pl.CostEstimate(
+            flops=2 * CHIP * n_z * CHIP * EMB,
+            bytes_accessed=2 * n_z * CHIP * (CHIP + EMB),
+            transcendentals=0,
+        ),
+    )(total, scaled, across, *expos)[0]
     grads = call(
-        functools.partial(backward_kernel, coef, n_y),
-        [shape((n_y, HID // n_y, COLS), BF)],
-        [SMEM] + [VMEM] * 10 + [ANY] * 4,
+        functools.partial(backward_kernel, coef),
+        [shape((16, TILES * 64 + 16, LANES), BF)],
+        [SMEM] + [VMEM] * 10 + [HBM] * 4,
         scratch=[
             pltpu.VMEM((HID, HID), BF),
             pltpu.VMEM((HID, EMB), BF),
@@ -411,34 +520,30 @@
         ],
     )(place, own, added, other, embed, inv, n1, f1, n2, f2, x, sa_mid, sa_out, goal_mid, goal_out)[0]
 
-    tall = HID // n_y
-    r = 8 // n_xl
-    source = np.arange(tall).reshape(2, 2 * n_z, n_xl, r).transpose(0, 2, 1, 3).reshape(-1)
-    order = jnp.asarray(np.eye(tall, dtype=np.float32)[source], BF)
-    grads = lax.all_to_all(grads, "y", 0, 0)
-    grads = call(sum_kernel, [shape((tall, COLS), BF)], [VMEM] * 2)(grads, order)[0]
-    tall = tall // (2 * n_xl)
-    grads = lax.all_to_all(grads.reshape(2 * n_xl, tall, COLS), ("xh", "xl"), 0, 0)
-    grads = call(add_kernel, [shape((tall, COLS), BF)], [VMEM])(grads)[0]
-    grads = lax.all_to_all(grads.reshape(n_z, 2 * r, COLS), "z", 0, 0)
-    grads = jnp.sum(grads.astype(F32), axis=0)
-    low, high = grads[:r], grads[r:]
-    keep = jnp.where(role == 0, low, high)
-    swap = shifted(jnp.where(role == 0, high, low), "c", 1)
-    sa = jnp.where(role == 0, keep, swap)
-    goal = jnp.where(role == 0, swap, keep)
-    acts = sa_act.shape[0]
-    low = HID + EMB
-    return (
-        loss,
-        sa[:, low : low + EMB].T,
-        sa[:, low + EMB : low + EMB + acts].T,
-        sa[:, :HID],
-        sa[:, HID:low],
-        goal[:, low : low + EMB].T,
-        goal[:, :HID],
-        goal[:, HID:low],
-    )
+    grads = lax.all_to_all(grads, ("y", "xh", "xl"), 0, 0)
+    grads = call(sum_kernel, [shape((n_z, TILES * 8 + 16, LANES), BF)], [VMEM])(grads)[0]
+    grads = lax.all_to_all(grads, "z", 0, 0)
+    keep, send = call(
+        split_kernel,
+        [shape((TILES * 4 + 8, LANES), F32)] * 2,
+        [SMEM, VMEM],
+        scratch=[pltpu.VMEM((16, LANES), F32)],
+    )(place, grads)
+    recv = shifted(send, "c", 1)
+    obs_a, act_a, mid_a, out_a, obs_b, mid_b, out_b = call(
+        last_kernel,
+        [
+            shape((4, EMB), F32),
+            shape((4, acts), F32),
+            shape((4, HID), F32),
+            shape((4, EMB), F32),
+            shape((4, EMB), F32),
+            shape((4, HID), F32),
+            shape((4, EMB), F32),
+        ],
+        [SMEM] + [VMEM] * 2,
+    )(place, keep, recv)
+    return (loss, obs_a.T, act_a.T, mid_a, out_a, obs_b.T, mid_b, out_b)
 
 
 def solution(mesh):

time: 200 us -> 157 us (0.79)
  local copies, waits for them, and re-layouts: 16.5 us -> 0.03 us
  Pallas kernels: 47 us -> 31.8 us
  starting transfers between devices: 31.8 us -> 22 us
    unnamed x35 -> x0, local copies, waits for them, and re-layouts: 14.1 us -> none
    all_to_all x1 -> x0, waiting for transfers between devices: 8.91 us -> none  [body(): grads = lax.all_to_all(grads.reshape(n_z, 2 * r, COLS), 'z', 0, 0)]
    pallas_call x5, Pallas kernels: 14.7 us -> 6.11 us  [scores(): return call(kernel, outs, [VMEM] * len(args), cost=cost)(*args)]
    ppermute x13, waiting for transfers between devices: 17.7 us -> 25.1 us  [shifted(): lax.ppermute(value, axis, [(k, (k + shift) % count) for k in range(count)])]
    all_to_all x1 -> x0, starting transfers between devices: 7.31 us -> none  [body(): grads = lax.all_to_all(grads.reshape(n_z, 2 * r, COLS), 'z', 0, 0)]
    pallas_call x5 -> x7, Pallas kernels: 23.6 us -> 19 us  [the longest x1 11 us: body(): call(functools.partial(backward_kernel, coef), [shape((16, TILES * 64 + 1...]
    ppermute x13, starting transfers between devices: 24.5 us -> 22 us  [shifted(): lax.ppermute(value, axis, [(k, (k + shift) % count) for k in range(count)])]
  transfers between devices with their start and end apart: 14 -> 13, of which waited for: 7 -> 11; matrix products, arithmetic and copies ran while one was open for 0% -> 0% of each run, Pallas kernels for 6% -> 4%
where the time goes in v2:
time: 157 us
  blocking collectives  77.1 us (49%)
  Pallas kernels  31.8 us (20%)
  waiting for transfers between devices  25.1 us (16%)
  starting transfers between devices  22 us (14%)
    all_to_all x1, blocking collectives, body(): grads = lax.all_to_all(grads, ('y', 'xh', 'xl'), 0, 0)  42.3 us
    ppermute x13, waiting for transfers between devices, shifted(): lax.ppermute(value, axis, [(k, (k + shift) % count) for k in range(count)])  25.1 us
    ppermute x13, starting transfers between devices, shifted(): lax.ppermute(value, axis, [(k, (k + shift) % count) for k in range(count)])  22 us
    all_to_all x1, blocking collectives, body(): sums = lax.all_to_all(everyone, ('xh', 'z', 'c'), 0, 0)  20.6 us
    all_to_all x1, blocking collectives, body(): grads = lax.all_to_all(grads, 'z', 0, 0)  14.2 us
    pallas_call x1, Pallas kernels, body(): call(functools.partial(backward_kernel, coef), [shape((16, TILES * 64 + 1...  11 us
    pallas_call x1, Pallas kernels, body(): call(forward_kernel, [shape((CHIP, WIDE), BF), shape((CHIP, HID), F32), s...  6.7 us
    pallas_call x5, Pallas kernels, scores(): return call(kernel, outs, [VMEM] * len(args), cost=cost)(*args)  6.11 us
  transfers between devices with their start and end apart: 13, of which 11 were waited for; matrix products, arithmetic and copies ran while one was open for 0% of the time, Pallas kernels for 4%

profile of v2, /device:TPU:1, one launch (start us, length us, event | category | flops | bytes accessed | tf_op | source)
XLA Modules:
  0.0 156.8 jit_solution(10067859068019391632)
XLA Ops:
  0.7 2.0 %shard_map.170 = (bf16[256,384]{1,0:T(8,128)(2,1)S(1)}, bf16[256,384]{1,0:T(8,128)(2,1)S(1)}) custom-call(s32[4]{0:T(128)S(1)} %pad_add_fusion.place, s32[1,256]{1,0:T(1,128)} %replay.1, s32[1,256]{1,0:T(1,128)} %offset.1, bf16[320,256]{1,0:T(8,128)(2,1)} %bitcast.11, bf16[16,320]{1,0:T(8,128)(2,1)} %bitcast.12), custom_call_target="tpu_custom_call" | custom-call | tf_op jit(solution)/shard_map/pallas_call | solution.py:428
  2.7 3.3 %collective-permute-start = (bf16[256,384]{1,0:T(8,128)(2,1)S(1)}, bf16[256,384]{1,0:T(8,128)(2,1)S(1)}, u32[]{:S(2)}, u32[]{:S(2)}) collective-permute-start(bf16[256,384]{1,0:T(8,128)(2,1)S(1)} %get-tuple-element.59), channel_id=1, source_target_pairs={{0,8},{8,0},{1,9},{9,1},{2,10},{10,2},{3,11},{11,3},{4,12},{12,4},... | collective-permute-start | bytes 589832 | tf_op jit(solution)/shard_map/ppermute | solution.py:399
  6.0 1.1 collective-permute-done.recv
  7.1 6.7 %shard_map.171 = (bf16[512,384]{1,0:T(8,128)(2,1)S(1)}, f32[512,1024]{1,0:T(8,128)S(1)}, f32[512,1]{1,0:T(8,128)S(1)}, f32[512,1024]{1,0:T(8,128)S(1)}, f32[512,...) custom-call(s32[4]{0:T(128)S(1)} %pad_add_fusion.place, ...), custom_call_target="tpu_custom_call" | custom-call | tf_op jit(solution)/shard_map/pallas_call | solution.py:441
  14.3 1.0 collective-permute-start.1
  15.5 5.4 %collective-permute-start.4 = (bf16[512,256]{1,0:T(8,128)(2,1)S(1)}, bf16[512,256]{1,0:T(8,128)(2,1)S(1)}, u32[]{:S(2)}, u32[]{:S(2)}) collective-permute-start(bf16[512,256]{1,0:T(8,128)(2,1)S(1)} %collective-permute-done.2.refs_2_.refs_5_.other), channel_id=1, source_target_pairs={{0,112},{16,0},{32,16},{48,32},{64,48},{80,64},{96,80},{112,96},{1... | collective-permute-start | bytes 786440 | tf_op jit(solution)/shard_map/ppermute | solution.py:399
  20.9 2.7 %collective-permute-done.1.refs_1_ = bf16[512,256]{1,0:T(8,128)(2,1)S(1)} collective-permute-done((bf16[512,256]{1,0:T(8,128)(2,1)S(1)}, bf16[512,256]{1,0:T(8,128)(2,1)S(1)}, u32[]{:S(2)}, u32[]{:S(2)}) %collective-permute-start.1) | collective-permute-done | bytes 262176 | tf_op jit(solution)/shard_map/ppermute | solution.py:399
  23.6 0.9 shard_map.172
  24.4 1.7 %collective-permute-done.4.refs_3_.refs_7_ = bf16[512,256]{1,0:T(8,128)(2,1)S(1)} collective-permute-done((bf16[512,256]{1,0:T(8,128)(2,1)S(1)}, bf16[512,256]{1,0:T(8,128)(2,1)S(1)}, u32[]{:S(2)}, u32[]{:S(2)}) %collective-permute-start.4) | collective-permute-done | bytes 262176 | tf_op jit(solution)/shard_map/ppermute | solution.py:399
  26.1 3.1 %collective-permute-done.3.refs_2_.refs_6_ = bf16[512,256]{1,0:T(8,128)(2,1)S(1)} collective-permute-done((bf16[512,256]{1,0:T(8,128)(2,1)S(1)}, bf16[512,256]{1,0:T(8,128)(2,1)S(1)}, u32[]{:S(2)}, u32[]{:S(2)}) %collective-permute-start.3) | collective-permute-done | bytes 262176 | tf_op jit(solution)/shard_map/ppermute | solution.py:399
  29.2 2.7 %collective-permute-start.6 = (bf16[512,256]{1,0:T(8,128)(2,1)S(1)}, bf16[512,256]{1,0:T(8,128)(2,1)S(1)}, u32[]{:S(2)}, u32[]{:S(2)}) collective-permute-start(bf16[512,256]{1,0:T(8,128)(2,1)S(1)} %collective-permute-done.4.refs_3_.refs_7_), channel_id=1, source_target_pairs={{0,112},{16,0},{32,16},{48,32},{64,48},{80,64},{96,80},{112,96},{1... | collective-permute-start | bytes 786440 | tf_op jit(solution)/shard_map/ppermute | solution.py:399
  31.9 1.4 shard_map.173
  33.3 3.3 %collective-permute-done.5.refs_2_.refs_8_ = bf16[512,256]{1,0:T(8,128)(2,1)S(1)} collective-permute-done((bf16[512,256]{1,0:T(8,128)(2,1)S(1)}, bf16[512,256]{1,0:T(8,128)(2,1)S(1)}, u32[]{:S(2)}, u32[]{:S(2)}) %collective-permute-start.5) | collective-permute-done | bytes 262176 | tf_op jit(solution)/shard_map/ppermute | solution.py:399
  36.7 2.7 %collective-permute-start.8 = (bf16[512,256]{1,0:T(8,128)(2,1)S(1)}, bf16[512,256]{1,0:T(8,128)(2,1)S(1)}, u32[]{:S(2)}, u32[]{:S(2)}) collective-permute-start(bf16[512,256]{1,0:T(8,128)(2,1)S(1)} %collective-permute-done.6.refs_3_.refs_9_), channel_id=1, source_target_pairs={{0,112},{16,0},{32,16},{48,32},{64,48},{80,64},{96,80},{112,96},{1... | collective-permute-start | bytes 786440 | tf_op jit(solution)/shard_map/ppermute | solution.py:399
  39.3 1.4 shard_map.174
  40.7 2.3 %collective-permute-done.7.refs_2_.refs_10_ = bf16[512,256]{1,0:T(8,128)(2,1)S(1)} collective-permute-done((bf16[512,256]{1,0:T(8,128)(2,1)S(1)}, bf16[512,256]{1,0:T(8,128)(2,1)S(1)}, u32[]{:S(2)}, u32[]{:S(2)}) %collective-permute-start.7) | collective-permute-done | bytes 262176 | tf_op jit(solution)/shard_map/ppermute | solution.py:399
  43.1 2.7 %collective-permute-start.10 = (bf16[256,256]{1,0:T(8,128)(2,1)S(1)}, bf16[256,256]{1,0:T(8,128)(2,1)S(1)}, u32[]{:S(2)}, u32[]{:S(2)}) collective-permute-start(bf16[256,256]{1,0:T(8,128)(2,1)S(1)} %slice.7), channel_id=1, source_target_pairs={{0,112},{16,0},{32,16},{48,32},{64,48},{80,64},{96,80},{112,96},{1... | collective-permute-start | bytes 393224 | tf_op jit(solution)/shard_map/ppermute | solution.py:399
  45.9 1.4 shard_map.175
  47.3 0.5 collective-permute-done.10.refs_3_.refs_13_
  47.8 3.1 %collective-permute-done.9.refs_2_.refs_12_ = bf16[256,256]{1,0:T(8,128)(2,1)S(1)} collective-permute-done((bf16[256,256]{1,0:T(8,128)(2,1)S(1)}, bf16[256,256]{1,0:T(8,128)(2,1)S(1)}, u32[]{:S(2)}, u32[]{:S(2)}) %collective-permute-start.9) | collective-permute-done | bytes 131104 | tf_op jit(solution)/shard_map/ppermute | solution.py:399
  50.9 1.0 shard_map.176
  52.0 20.6 %all_to_all.15.sums = f32[32,8,128]{2,1,0:T(8,128)S(1)} all-to-all(f32[32,8,128]{2,1,0:T(8,128)S(1)} %broadcast_in_dim.2), channel_id=1, replica_groups=mesh['xh'=2,'z'=8,'c'=2,'y'=4,'xl'=2] {'xh','z','c'}, dimensions={0} | all-to-all | bytes 262144 | tf_op jit(solution)/shard_map/all_to_all | solution.py:484
  72.6 2.4 %shard_map.177 = (bf16[512,256]{1,0:T(8,128)(2,1)S(1)}, bf16[4096,256]{1,0:T(8,128)(2,1)S(1)}, f32[128,128]{1,0:T(8,128)S(1)}, f32[1,256]{1,0:T(1,128)}) custom-call(s32[4]{0:T(128)S(1)} %pad_add_fusion.place, f32[32,8,128]{2,1,0:T(8,128)S(1)} %all_to_all.15.sums, f32[1024,256]{1,0:T(8,128)S(1)} %get-tuple-element.82.total, ...), custom_call_target="tpu_custom_call" | custom-call | tf_op jit(solution)/shard_map/pallas_call | solution.py:485
  75.2 1.2 shard_map.178.own
  76.4 6.3 %collective-permute-done.11.recv = bf16[512,256]{1,0:T(8,128)(2,1)S(1)} collective-permute-done((bf16[512,256]{1,0:T(8,128)(2,1)S(1)}, bf16[512,256]{1,0:T(8,128)(2,1)S(1)}, u32[]{:S(2)}, u32[]{:S(2)}) %collective-permute-start.11) | collective-permute-done | bytes 262176 | tf_op jit(solution)/shard_map/ppermute | solution.py:399
  82.7 11.0 %shard_map.179 = bf16[16,784,128]{2,1,0:T(8,128)(2,1)S(1)} custom-call(s32[4]{0:T(128)S(1)} %pad_add_fusion.place, f32[512,256]{1,0:T(8,128)S(1)} %shard_map.178.own, bf16[512,256]{1,0:T(8,128)(2,1)S(1)} %collective-permute-done.11.recv, bf16[512,256]{1,0:T(8,128)(2,1)S(1)} %collective-permute-done.2.refs_2_.refs_5_.other, ...), custom_call_target="tpu_custom_call" | custom-call | tf_op jit(solution)/shard_map/pallas_call | solution.py:507
  93.7 42.3 %all_to_all.16.parts = bf16[16,784,128]{2,1,0:T(8,128)(2,1)S(1)} all-to-all(bf16[16,784,128]{2,1,0:T(8,128)(2,1)S(1)} %shard_map.179), channel_id=1, replica_groups=mesh['xh'=2,'z'=8,'c'=2,'y'=4,'xl'=2] {'y','xh','xl'}, dimensions={0} | all-to-all | bytes 6422528 | tf_op jit(solution)/shard_map/all_to_all | solution.py:523
  136.4 14.2 %all_to_all.17.parts = bf16[8,112,128]{2,1,0:T(8,128)(2,1)S(1)} all-to-all(bf16[8,112,128]{2,1,0:T(8,128)(2,1)S(1)} %shard_map.180), channel_id=1, replica_groups=mesh['xh'=2,'z'=8,'c'=2,'y'=4,'xl'=2] {'z'}, dimensions={0} | all-to-all | bytes 458752 | tf_op jit(solution)/shard_map/all_to_all | solution.py:525
  150.6 0.6 shard_map.181
  151.2 3.5 %collective-permute-start.12 = (f32[56,128]{1,0:T(8,128)S(1)}, f32[56,128]{1,0:T(8,128)S(1)}, u32[]{:S(2)}, u32[]{:S(2)}) collective-permute-start(f32[56,128]{1,0:T(8,128)S(1)} %get-tuple-element.100), channel_id=1, source_target_pairs={{0,8},{8,0},{1,9},{9,1},{2,10},{10,2},{3,11},{11,3},{4,12},{12,4},... | collective-permute-start | bytes 86024 | tf_op jit(solution)/shard_map/ppermute | solution.py:399
  154.7 0.9 collective-permute-done.12.recv
  155.5 1.3 shard_map.182
  (14 shorter events, 1.3 us)
Async XLA Ops:
  2.7 4.4 %collective-permute-start = (bf16[256,384]{1,0:T(8,128)(2,1)S(1)}, bf16[256,384]{1,0:T(8,128)(2,1)S(1)}, u32[]{:S(2)}, u32[]{:S(2)}) collective-permute-start(bf16[256,384]{1,0:T(8,128)(2,1)S(1)} %get-tuple-element.59), channel_id=1, source_target_pairs={{0,8},{8,0},{1,9},{9,1},{2,10},{10,2},{3,11},{11,3},{4,12},{12,4},... | collective-permute-start | bytes 589832 | tf_op jit(solution)/shard_map/ppermute | solution.py:399
  13.8 1.6 %collective-permute-start.2 = (bf16[512,256]{1,0:T(8,128)(2,1)S(1)}, bf16[512,256]{1,0:T(8,128)(2,1)S(1)}, u32[]{:S(2)}, u32[]{:S(2)}) collective-permute-start(bf16[512,256]{1,0:T(8,128)(2,1)S(1)} %get-tuple-element.60.refs_0_.ours), channel_id=1, source_target_pairs={{0,8},{8,0},{1,9},{9,1},{2,10},{10,2},{3,11},{11,3},{4,12},{12,4},... | collective-permute-start | bytes 786440 | tf_op jit(solution)/shard_map/ppermute | solution.py:399
  14.3 9.3 %collective-permute-start.1 = (bf16[512,256]{1,0:T(8,128)(2,1)S(1)}, bf16[512,256]{1,0:T(8,128)(2,1)S(1)}, u32[]{:S(2)}, u32[]{:S(2)}) collective-permute-start(bf16[512,256]{1,0:T(8,128)(2,1)S(1)} %get-tuple-element.60.refs_0_.ours), channel_id=1, source_target_pairs={{0,128},{128,0},{1,129},{129,1},{2,130},{130,2},{3,131},{131,3},{4... | collective-permute-start | bytes 786440 | tf_op jit(solution)/shard_map/ppermute | solution.py:399
  15.5 10.7 %collective-permute-start.4 = (bf16[512,256]{1,0:T(8,128)(2,1)S(1)}, bf16[512,256]{1,0:T(8,128)(2,1)S(1)}, u32[]{:S(2)}, u32[]{:S(2)}) collective-permute-start(bf16[512,256]{1,0:T(8,128)(2,1)S(1)} %collective-permute-done.2.refs_2_.refs_5_.other), channel_id=1, source_target_pairs={{0,112},{16,0},{32,16},{48,32},{64,48},{80,64},{96,80},{112,96},{1... | collective-permute-start | bytes 786440 | tf_op jit(solution)/shard_map/ppermute | solution.py:399
  20.9 8.3 %collective-permute-start.3 = (bf16[512,256]{1,0:T(8,128)(2,1)S(1)}, bf16[512,256]{1,0:T(8,128)(2,1)S(1)}, u32[]{:S(2)}, u32[]{:S(2)}) collective-permute-start(bf16[512,256]{1,0:T(8,128)(2,1)S(1)} %collective-permute-done.2.refs_2_.refs_5_.other), channel_id=1, source_target_pairs={{0,16},{16,32},{32,48},{48,64},{64,80},{80,96},{96,112},{112,0},{1... | collective-permute-start | bytes 786440 | tf_op jit(solution)/shard_map/ppermute | solution.py:399
  29.2 7.4 %collective-permute-start.5 = (bf16[512,256]{1,0:T(8,128)(2,1)S(1)}, bf16[512,256]{1,0:T(8,128)(2,1)S(1)}, u32[]{:S(2)}, u32[]{:S(2)}) collective-permute-start(bf16[512,256]{1,0:T(8,128)(2,1)S(1)} %collective-permute-done.3.refs_2_.refs_6_), channel_id=1, source_target_pairs={{0,16},{16,32},{32,48},{48,64},{64,80},{80,96},{96,112},{112,0},{1... | collective-permute-start | bytes 786440 | tf_op jit(solution)/shard_map/ppermute | solution.py:399
  29.2 7.4 %collective-permute-start.6 = (bf16[512,256]{1,0:T(8,128)(2,1)S(1)}, bf16[512,256]{1,0:T(8,128)(2,1)S(1)}, u32[]{:S(2)}, u32[]{:S(2)}) collective-permute-start(bf16[512,256]{1,0:T(8,128)(2,1)S(1)} %collective-permute-done.4.refs_3_.refs_7_), channel_id=1, source_target_pairs={{0,112},{16,0},{32,16},{48,32},{64,48},{80,64},{96,80},{112,96},{1... | collective-permute-start | bytes 786440 | tf_op jit(solution)/shard_map/ppermute | solution.py:399
  36.7 6.4 %collective-permute-start.7 = (bf16[512,256]{1,0:T(8,128)(2,1)S(1)}, bf16[512,256]{1,0:T(8,128)(2,1)S(1)}, u32[]{:S(2)}, u32[]{:S(2)}) collective-permute-start(bf16[512,256]{1,0:T(8,128)(2,1)S(1)} %collective-permute-done.5.refs_2_.refs_8_), channel_id=1, source_target_pairs={{0,16},{16,32},{32,48},{48,64},{64,80},{80,96},{96,112},{112,0},{1... | collective-permute-start | bytes 786440 | tf_op jit(solution)/shard_map/ppermute | solution.py:399
  36.7 6.4 %collective-permute-start.8 = (bf16[512,256]{1,0:T(8,128)(2,1)S(1)}, bf16[512,256]{1,0:T(8,128)(2,1)S(1)}, u32[]{:S(2)}, u32[]{:S(2)}) collective-permute-start(bf16[512,256]{1,0:T(8,128)(2,1)S(1)} %collective-permute-done.6.refs_3_.refs_9_), channel_id=1, source_target_pairs={{0,112},{16,0},{32,16},{48,32},{64,48},{80,64},{96,80},{112,96},{1... | collective-permute-start | bytes 786440 | tf_op jit(solution)/shard_map/ppermute | solution.py:399
  43.1 4.7 %collective-permute-start.10 = (bf16[256,256]{1,0:T(8,128)(2,1)S(1)}, bf16[256,256]{1,0:T(8,128)(2,1)S(1)}, u32[]{:S(2)}, u32[]{:S(2)}) collective-permute-start(bf16[256,256]{1,0:T(8,128)(2,1)S(1)} %slice.7), channel_id=1, source_target_pairs={{0,112},{16,0},{32,16},{48,32},{64,48},{80,64},{96,80},{112,96},{1... | collective-permute-start | bytes 393224 | tf_op jit(solution)/shard_map/ppermute | solution.py:399
  45.9 5.0 %collective-permute-start.9 = (bf16[256,256]{1,0:T(8,128)(2,1)S(1)}, bf16[256,256]{1,0:T(8,128)(2,1)S(1)}, u32[]{:S(2)}, u32[]{:S(2)}) collective-permute-start(bf16[256,256]{1,0:T(8,128)(2,1)S(1)} %slice.6), channel_id=1, source_target_pairs={{0,16},{16,32},{32,48},{48,64},{64,80},{80,96},{96,112},{112,0},{1... | collective-permute-start | bytes 393224 | tf_op jit(solution)/shard_map/ppermute | solution.py:399
  75.0 7.7 %collective-permute-start.11 = (bf16[512,256]{1,0:T(8,128)(2,1)S(1)}, bf16[512,256]{1,0:T(8,128)(2,1)S(1)}, u32[]{:S(2)}, u32[]{:S(2)}) collective-permute-start(bf16[512,256]{1,0:T(8,128)(2,1)S(1)} %get-tuple-element.91), channel_id=1, source_target_pairs={{0,128},{128,0},{1,129},{129,1},{2,130},{130,2},{3,131},{131,3},{4... | collective-permute-start | bytes 786440 | tf_op jit(solution)/shard_map/ppermute | solution.py:399
  151.2 4.3 %collective-permute-start.12 = (f32[56,128]{1,0:T(8,128)S(1)}, f32[56,128]{1,0:T(8,128)S(1)}, u32[]{:S(2)}, u32[]{:S(2)}) collective-permute-start(f32[56,128]{1,0:T(8,128)S(1)} %get-tuple-element.100), channel_id=1, source_target_pairs={{0,8},{8,0},{1,9},{9,1},{2,10},{10,2},{3,11},{11,3},{4,12},{12,4},... | collective-permute-start | bytes 86024 | tf_op jit(solution)/shard_map/ppermute | solution.py:399

commit v3 on v2

--- a/solution.py
+++ b/solution.py
@@ -16,6 +16,7 @@
 HID = 1024
 EMB = 256
 WIDE = 384
+TALL = 256
 TILES = (HID + 2 * EMB) // 128
 LANES = 128
 BF = jnp.bfloat16
@@ -281,17 +282,50 @@
         mix_rows(expos, scaled, total, columns, 4 * n_z, start, write)
 
 
+def unit_order(tall):
+    unit = lax.broadcasted_iota(jnp.int32, (tall, tall), 1)
+    origin = (unit // 4 % 8) * 32 + unit // 64 * 8 + (unit // 32 % 2) * 4 + unit % 4
+    line = lax.broadcasted_iota(jnp.int32, (tall, tall), 0)
+    return jnp.where(line == origin, 1.0, 0.0).astype(BF)
+
+
+def turned(order, values):
+    return lax.dot_general(
+        order, values, (((0,), (1,)), ((), ())), preferred_element_type=F32
+    ).astype(BF)
+
+
+def slope_kernel(normed, slope, hidden):
+    order = unit_order(TALL)
+    for start in range(0, CHIP, ROWS):
+        rows = pl.ds(start, ROWS)
+        for at in range(0, HID, TALL):
+            v = normed[rows, at : at + TALL]
+            gate = sigmoid(v)
+            h = v * gate
+            slope[rows, at : at + TALL] = gate * (1.0 + v - h)
+            hidden[at : at + TALL, start : start + ROWS] = turned(order, h.astype(BF))
+
+
+def slopes(normed):
+    cost = pl.CostEstimate(
+        flops=2 * CHIP * HID * TALL, bytes_accessed=10 * CHIP * HID, transcendentals=CHIP * HID
+    )
+    outs = [shape((CHIP, HID), F32), shape((HID, CHIP), BF)]
+    return call(slope_kernel, outs, [VMEM], cost=cost)(normed)
+
+
 def backward_kernel(
-    coef, place, own, recv, other, embed, inv, n1, f1, n2, f2, x,
+    coef, place, own, recv, other, embed, inv, n1, f1, s1, h1, n2, f2, s2, h2, x,
     sa_mid, sa_out, goal_mid, goal_out,
     grads,
-    w_mid, w_out, ge_s, h1_s, h2_s, p1_s, p2_s, sems,
+    w_mid, w_out, ge_s, p1_s, p2_s, sems,
 ):
     role = place[2]
     pairs = [((sa_out, goal_out), w_out), ((sa_mid, goal_mid), w_mid)]
     by_role(role, pairs, sems)
-    for start in range(0, CHIP, LANES):
-        rows = pl.ds(start, LANES)
+    for start in range(0, CHIP, ROWS):
+        rows = pl.ds(start, ROWS)
         grad = coef * (
             own[rows, :] + recv[rows, :].astype(F32) - 2.0 * other[rows, :].astype(F32)
         )
@@ -301,12 +335,9 @@
         ge = (EMB ** (-0.5) * scale * (grad - e * (scale * scale * along))).astype(BF)
         ge_s[rows, :] = ge
 
-        def step(back, normed, factor, hidden, out):
+        def step(back, normed, factor, slope, out):
             v = normed[rows, :]
-            gate = sigmoid(v)
-            h = v * gate
-            hidden[rows, :] = h.astype(BF)
-            back = back * (gate * (1.0 + v - h))
+            back = back * slope[rows, :]
             mean = jnp.mean(back, axis=-1, keepdims=True)
             tilt = jnp.mean(back * v, axis=-1, keepdims=True)
             pre = (factor[rows, :] * (back - mean - v * tilt)).astype(BF)
@@ -315,14 +346,16 @@
 
         if start == 0:
             wait_role(role, pairs[:1], sems, 0)
-        p2 = step(dot_nt(ge, w_out[...]), n2, f2, h2_s, p2_s)
+        p2 = step(dot_nt(ge, w_out[...]), n2, f2, s2, p2_s)
         if start == 0:
             wait_role(role, pairs[1:], sems, 1)
-        step(dot_nt(p2, w_mid[...]), n1, f1, h1_s, p1_s)
-    tall = 256
-    unit = lax.broadcasted_iota(jnp.int32, (tall, tall), 1)
-    origin = (unit // 4 % 8) * 32 + unit // 64 * 8 + (unit // 32 % 2) * 4 + unit % 4
-    order = jnp.where(lax.broadcasted_iota(jnp.int32, (tall, tall), 0) == origin, 1.0, 0.0).astype(BF)
+        step(dot_nt(p2, w_mid[...]), n1, f1, s1, p1_s)
+    tall = TALL
+    order = unit_order(tall)
+
+    def slot(y, x_at):
+        return jnp.where(role == 0, y, x_at), jnp.where(role == 0, x_at, y)
+
     line = lax.broadcasted_iota(jnp.int32, (tall, LANES), 0)
     lane = lax.broadcasted_iota(jnp.int32, (tall, LANES), 1)
     wanted = lane // 16 == (line // 32 % 2) * 4 + line % 4
@@ -334,22 +367,23 @@
     for start in range(0, HID, tall):
         span = slice(start, start + tall)
         xh, half = start // tall // 2, start // tall % 2
-        for left, right, tile in ((h1_s, p2_s, 0), (h2_s, ge_s, 8), (p1_s, x, 10)):
-            units = dot_nn(left[:, span], order).astype(BF)
-            value = dot_tn(units, right[:, : right.shape[1] // EMB * EMB])
+        for left, right, tile in ((h1, p2_s, 0), (h2, ge_s, 8), (None, x, 10)):
+            units = turned(order, p1_s[:, span]) if left is None else left[span, :]
+            value = dot_nn(units, right[:, : right.shape[1] // EMB * EMB])
             for k in range(value.shape[1] // LANES):
                 for part in range(8):
                     piece = value[part * 32 : part * 32 + 32, k * LANES : (k + 1) * LANES]
                     at = (tile + k) * 64 + half * 32
-                    dest = part // 2 * 4 + xh * 2 + part % 2
-                    grads[dest, at : at + 32, :] = piece.astype(BF)
+                    first, second = slot(part // 2, xh * 2 + part % 2)
+                    grads[first, second, at : at + 32, :] = piece.astype(BF)
             if tile == 10:
-                value = jnp.where(wanted, dot_tn(units, x[:, EMB:]), 0.0).astype(BF)
+                value = jnp.where(wanted, dot_nn(units, x[:, EMB:]), 0.0).astype(BF)
                 packed.append(dot_nn(pack, value))
-    for dest in range(16):
-        y, xh = dest // 4, dest // 2 % 2
+    for part in range(16):
+        y, xh = part // 4, part // 2 % 2
+        first, second = slot(y, part % 4)
         two = [packed[2 * xh + half][y * 8 : y * 8 + 8] for half in range(2)]
-        grads[dest, TILES * 64 : TILES * 64 + 16, :] = jnp.concatenate(two, axis=0).astype(BF)
+        grads[first, second, TILES * 64 : TILES * 64 + 16, :] = jnp.concatenate(two, axis=0).astype(BF)
 
 
 def plus(parts, rows):
@@ -357,6 +391,14 @@
     for k in range(1, parts.shape[0]):
         value = value + parts[k, rows, :].astype(F32)
     return value
+
+
+def add_kernel(parts, out):
+    for dest in range(parts.shape[1]):
+        value = parts[0, dest].astype(F32)
+        for k in range(1, parts.shape[0]):
+            value = value + parts[k, dest].astype(F32)
+        out[dest] = value.astype(BF)
 
 
 def sum_kernel(parts, out):
@@ -475,6 +517,13 @@
         expo, part, total = scores(unit, theirs, steps[k], prev, k == n_z // 2, factor)
         expos.append(expo)
         prev = (part, total)
+        if k == 1:
+            s1, h1 = slopes(n1)
+            part, s1, h1 = lax.optimization_barrier((part, s1, h1))
+        if k == 2:
+            s2, h2 = slopes(n2)
+            part, s2, h2 = lax.optimization_barrier((part, s2, h2))
+        prev = (part, total)
         if k < n_z // 2 - 1:
             ahead, back, part, total = lax.optimization_barrier((ahead, back, part, total))
             steps[-1] = [ahead, back]
@@ -506,21 +555,32 @@
     )(total, scaled, across, *expos)[0]
     grads = call(
         functools.partial(backward_kernel, coef),
-        [shape((16, TILES * 64 + 16, LANES), BF)],
-        [SMEM] + [VMEM] * 10 + [HBM] * 4,
+        [shape((4, 4, TILES * 64 + 16, LANES), BF)],
+        [SMEM] + [VMEM] * 14 + [HBM] * 4,
         scratch=[
             pltpu.VMEM((HID, HID), BF),
             pltpu.VMEM((HID, EMB), BF),
             pltpu.VMEM((CHIP, EMB), BF),
             pltpu.VMEM((CHIP, HID), BF),
             pltpu.VMEM((CHIP, HID), BF),
-            pltpu.VMEM((CHIP, HID), BF),
-            pltpu.VMEM((CHIP, HID), BF),
             pltpu.SemaphoreType.DMA((2,)),
         ],
-    )(place, own, added, other, embed, inv, n1, f1, n2, f2, x, sa_mid, sa_out, goal_mid, goal_out)[0]
-
-    grads = lax.all_to_all(grads, ("y", "xh", "xl"), 0, 0)
+    )(
+        place, own, added, other, embed, inv, n1, f1, s1, h1, n2, f2, s2, h2, x,
+        sa_mid, sa_out, goal_mid, goal_out,
+    )[0]
+
+    along_y = [[y * 4 + x_at for y in range(4)] for x_at in range(4)]
+    along_x = [[y * 4 + x_at for x_at in range(4)] for y in range(4)]
+
+    def exchange(parts, low, high):
+        groups = low + [[16 + member for member in group] for group in high]
+        return lax.all_to_all(parts, ("c", "y", "xh", "xl"), 0, 0, axis_index_groups=groups)
+
+    height = TILES * 64 + 16
+    grads = exchange(grads, along_y, along_x)
+    grads = call(add_kernel, [shape((4, height, LANES), BF)], [VMEM])(grads)[0]
+    grads = exchange(grads, along_x, along_y)
     grads = call(sum_kernel, [shape((n_z, TILES * 8 + 16, LANES), BF)], [VMEM])(grads)[0]
     grads = lax.all_to_all(grads, "z", 0, 0)
     keep, send = call(

time: 157 us -> 148 us (0.943)
  blocking collectives: 77.1 us -> 70.4 us
  waiting for transfers between devices: 25.1 us -> 23.2 us
  Pallas kernels: 31.8 us -> 30.2 us
    all_to_all x1 -> x2, blocking collectives: 42.3 us -> 36.2 us  [exchange(): lax.all_to_all(parts, ('c', 'y', 'xh', 'xl'), 0, 0, axis_index_groups=gro...]
    ppermute x13, waiting for transfers between devices: 25.1 us -> 23.2 us  [shifted(): lax.ppermute(value, axis, [(k, (k + shift) % count) for k in range(count)])]
    pallas_call x1 -> x4, Pallas kernels: 11 us -> 9.66 us  [the longest x1 7.38 us: body(): call(functools.partial(backward_kernel, coef), [shape((4, 4, TILES * 64 +...]
  transfers between devices with their start and end apart: 13 -> 13, of which waited for: 11 -> 11; matrix products, arithmetic and copies ran while one was open for 0% -> 0% of each run, Pallas kernels for 4% -> 6%
where the time goes in v3:
time: 148 us
  blocking collectives  70.4 us (48%)
  Pallas kernels  30.2 us (20%)
  waiting for transfers between devices  23.2 us (16%)
  starting transfers between devices  22.9 us (15%)
    all_to_all x2, blocking collectives, exchange(): lax.all_to_all(parts, ('c', 'y', 'xh', 'xl'), 0, 0, axis_index_groups=gro...  36.2 us
    ppermute x13, waiting for transfers between devices, shifted(): lax.ppermute(value, axis, [(k, (k + shift) % count) for k in range(count)])  23.2 us
    ppermute x13, starting transfers between devices, shifted(): lax.ppermute(value, axis, [(k, (k + shift) % count) for k in range(count)])  22.9 us
    all_to_all x1, blocking collectives, body(): sums = lax.all_to_all(everyone, ('xh', 'z', 'c'), 0, 0)  20.6 us
    all_to_all x1, blocking collectives, body(): grads = lax.all_to_all(grads, 'z', 0, 0)  13.6 us
    pallas_call x1, Pallas kernels, body(): call(functools.partial(backward_kernel, coef), [shape((4, 4, TILES * 64 +...  7.38 us
    pallas_call x1, Pallas kernels, body(): call(forward_kernel, [shape((CHIP, WIDE), BF), shape((CHIP, HID), F32), s...  6.7 us
    pallas_call x5, Pallas kernels, scores(): return call(kernel, outs, [VMEM] * len(args), cost=cost)(*args)  6.1 us
  transfers between devices with their start and end apart: 13, of which 11 were waited for; matrix products, arithmetic and copies ran while one was open for 0% of the time, Pallas kernels for 6%

profile of v3, /device:TPU:1, one launch (start us, length us, event | category | flops | bytes accessed | tf_op | source)
XLA Modules:
  0.0 147.5 jit_solution(3225205254123682921)
XLA Ops:
  0.7 2.0 %shard_map.170 = (bf16[256,384]{1,0:T(8,128)(2,1)S(1)}, bf16[256,384]{1,0:T(8,128)(2,1)S(1)}) custom-call(s32[4]{0:T(128)S(1)} %pad_add_fusion.place, s32[1,256]{1,0:T(1,128)} %replay.1, s32[1,256]{1,0:T(1,128)} %offset.1, bf16[320,256]{1,0:T(8,128)(2,1)} %bitcast.11, bf16[16,320]{1,0:T(8,128)(2,1)} %bitcast.12), custom_call_target="tpu_custom_call" | custom-call | tf_op jit(solution)/shard_map/pallas_call | solution.py:470
  2.7 3.3 %collective-permute-start = (bf16[256,384]{1,0:T(8,128)(2,1)S(1)}, bf16[256,384]{1,0:T(8,128)(2,1)S(1)}, u32[]{:S(2)}, u32[]{:S(2)}) collective-permute-start(bf16[256,384]{1,0:T(8,128)(2,1)S(1)} %get-tuple-element.69), channel_id=1, source_target_pairs={{0,8},{8,0},{1,9},{9,1},{2,10},{10,2},{3,11},{11,3},{4,12},{12,4},... | collective-permute-start | bytes 589832 | tf_op jit(solution)/shard_map/ppermute | solution.py:441
  6.0 1.1 collective-permute-done.recv
  7.1 6.7 %shard_map.171 = (bf16[512,384]{1,0:T(8,128)(2,1)S(1)}, f32[512,1024]{1,0:T(8,128)S(1)}, f32[512,1]{1,0:T(8,128)S(1)}, f32[512,1024]{1,0:T(8,128)S(1)}, f32[512,...) custom-call(s32[4]{0:T(128)S(1)} %pad_add_fusion.place, ...), custom_call_target="tpu_custom_call" | custom-call | tf_op jit(solution)/shard_map/pallas_call | solution.py:483
  14.3 1.0 collective-permute-start.1
  15.5 5.4 %collective-permute-start.4 = (bf16[512,256]{1,0:T(8,128)(2,1)S(1)}, bf16[512,256]{1,0:T(8,128)(2,1)S(1)}, u32[]{:S(2)}, u32[]{:S(2)}) collective-permute-start(bf16[512,256]{1,0:T(8,128)(2,1)S(1)} %collective-permute-done.2.refs_2_.refs_5_.other), channel_id=1, source_target_pairs={{0,112},{16,0},{32,16},{48,32},{64,48},{80,64},{96,80},{112,96},{1... | collective-permute-start | bytes 786440 | tf_op jit(solution)/shard_map/ppermute | solution.py:441
  20.9 2.7 %collective-permute-done.1.refs_1_ = bf16[512,256]{1,0:T(8,128)(2,1)S(1)} collective-permute-done((bf16[512,256]{1,0:T(8,128)(2,1)S(1)}, bf16[512,256]{1,0:T(8,128)(2,1)S(1)}, u32[]{:S(2)}, u32[]{:S(2)}) %collective-permute-start.1) | collective-permute-done | bytes 262176 | tf_op jit(solution)/shard_map/ppermute | solution.py:441
  24.4 1.7 %collective-permute-done.4.refs_3_.refs_7_ = bf16[512,256]{1,0:T(8,128)(2,1)S(1)} collective-permute-done((bf16[512,256]{1,0:T(8,128)(2,1)S(1)}, bf16[512,256]{1,0:T(8,128)(2,1)S(1)}, u32[]{:S(2)}, u32[]{:S(2)}) %collective-permute-start.4) | collective-permute-done | bytes 262176 | tf_op jit(solution)/shard_map/ppermute | solution.py:441
  26.1 3.1 %collective-permute-done.3.refs_2_.refs_6_ = bf16[512,256]{1,0:T(8,128)(2,1)S(1)} collective-permute-done((bf16[512,256]{1,0:T(8,128)(2,1)S(1)}, bf16[512,256]{1,0:T(8,128)(2,1)S(1)}, u32[]{:S(2)}, u32[]{:S(2)}) %collective-permute-start.3) | collective-permute-done | bytes 262176 | tf_op jit(solution)/shard_map/ppermute | solution.py:441
  29.2 2.7 %collective-permute-start.6 = (bf16[512,256]{1,0:T(8,128)(2,1)S(1)}, bf16[512,256]{1,0:T(8,128)(2,1)S(1)}, u32[]{:S(2)}, u32[]{:S(2)}) collective-permute-start(bf16[512,256]{1,0:T(8,128)(2,1)S(1)} %collective-permute-done.4.refs_3_.refs_7_), channel_id=1, source_target_pairs={{0,112},{16,0},{32,16},{48,32},{64,48},{80,64},{96,80},{112,96},{1... | collective-permute-start | bytes 786440 | tf_op jit(solution)/shard_map/ppermute | solution.py:441
  31.9 0.9 shard_map.174
  32.9 1.4 shard_map.173
  34.3 2.4 %collective-permute-done.5.refs_2_.refs_8_ = bf16[512,256]{1,0:T(8,128)(2,1)S(1)} collective-permute-done((bf16[512,256]{1,0:T(8,128)(2,1)S(1)}, bf16[512,256]{1,0:T(8,128)(2,1)S(1)}, u32[]{:S(2)}, u32[]{:S(2)}) %collective-permute-start.5) | collective-permute-done | bytes 262176 | tf_op jit(solution)/shard_map/ppermute | solution.py:441
  36.7 2.7 %collective-permute-start.8 = (bf16[512,256]{1,0:T(8,128)(2,1)S(1)}, bf16[512,256]{1,0:T(8,128)(2,1)S(1)}, u32[]{:S(2)}, u32[]{:S(2)}) collective-permute-start(bf16[512,256]{1,0:T(8,128)(2,1)S(1)} %collective-permute-done.6.refs_3_.refs_9_), channel_id=1, source_target_pairs={{0,112},{16,0},{32,16},{48,32},{64,48},{80,64},{96,80},{112,96},{1... | collective-permute-start | bytes 786440 | tf_op jit(solution)/shard_map/ppermute | solution.py:441
  39.3 1.0 shard_map.176
  40.3 1.4 shard_map.175
  41.7 1.4 collective-permute-done.7.refs_2_.refs_10_
  43.1 2.7 %collective-permute-start.10 = (bf16[256,256]{1,0:T(8,128)(2,1)S(1)}, bf16[256,256]{1,0:T(8,128)(2,1)S(1)}, u32[]{:S(2)}, u32[]{:S(2)}) collective-permute-start(bf16[256,256]{1,0:T(8,128)(2,1)S(1)} %slice.7), channel_id=1, source_target_pairs={{0,112},{16,0},{32,16},{48,32},{64,48},{80,64},{96,80},{112,96},{1... | collective-permute-start | bytes 393224 | tf_op jit(solution)/shard_map/ppermute | solution.py:441
  45.9 1.4 shard_map.177
  47.8 3.1 %collective-permute-done.9.refs_2_.refs_12_ = bf16[256,256]{1,0:T(8,128)(2,1)S(1)} collective-permute-done((bf16[256,256]{1,0:T(8,128)(2,1)S(1)}, bf16[256,256]{1,0:T(8,128)(2,1)S(1)}, u32[]{:S(2)}, u32[]{:S(2)}) %collective-permute-start.9) | collective-permute-done | bytes 131104 | tf_op jit(solution)/shard_map/ppermute | solution.py:441
  50.9 1.0 shard_map.178
  52.0 20.6 %all_to_all.20.sums = f32[32,8,128]{2,1,0:T(8,128)S(1)} all-to-all(f32[32,8,128]{2,1,0:T(8,128)S(1)} %broadcast_in_dim.2), channel_id=1, replica_groups=mesh['xh'=2,'z'=8,'c'=2,'y'=4,'xl'=2] {'xh','z','c'}, dimensions={0} | all-to-all | bytes 262144 | tf_op jit(solution)/shard_map/all_to_all | solution.py:533
  72.6 2.5 %shard_map.179 = (bf16[512,256]{1,0:T(8,128)(2,1)S(1)}, bf16[4096,256]{1,0:T(8,128)(2,1)S(1)}, f32[128,128]{1,0:T(8,128)S(1)}, f32[1,256]{1,0:T(1,128)}) custom-call(s32[4]{0:T(128)S(1)} %pad_add_fusion.place, f32[32,8,128]{2,1,0:T(8,128)S(1)} %all_to_all.20.sums, f32[1024,256]{1,0:T(8,128)S(1)} %get-tuple-element.100.total, ...), custom_call_target="tpu_custom_call" | custom-call | tf_op jit(solution)/shard_map/pallas_call | solution.py:534
  75.2 1.2 shard_map.180.own
  76.5 6.2 %collective-permute-done.11.recv = bf16[512,256]{1,0:T(8,128)(2,1)S(1)} collective-permute-done((bf16[512,256]{1,0:T(8,128)(2,1)S(1)}, bf16[512,256]{1,0:T(8,128)(2,1)S(1)}, u32[]{:S(2)}, u32[]{:S(2)}) %collective-permute-start.11) | collective-permute-done | bytes 262176 | tf_op jit(solution)/shard_map/ppermute | solution.py:441
  82.7 7.4 %shard_map.181 = bf16[4,4,784,128]{3,2,1,0:T(8,128)(2,1)S(1)} custom-call(s32[4]{0:T(128)S(1)} %pad_add_fusion.place, f32[512,256]{1,0:T(8,128)S(1)} %shard_map.180.own, bf16[512,256]{1,0:T(8,128)(2,1)S(1)} %collective-permute-done.11.recv, bf16[512,256]{1,0:T(8,128)(2,1)S(1)} %collective-permute-done.2.refs_2_.refs_5_.other, ...), custom_call_target="tpu_custom_call" | custom-call | tf_op jit(solution)/shard_map/pallas_call | solution.py:556
  90.1 24.1 %all_to_all.21.parts = bf16[4,4,784,128]{3,2,1,0:T(8,128)(2,1)S(1)} all-to-all(bf16[4,4,784,128]{3,2,1,0:T(8,128)(2,1)S(1)} %shard_map.181), channel_id=1, replica_groups={{0,2,4,6},{1,3,5,7},{128,130,132,134},{129,131,133,135},{8,9,136,137},{..., dimensions={0} | all-to-all | bytes 6422528 | tf_op jit(solution)/shard_map/all_to_all | solution.py:578
  114.6 12.1 %all_to_all.22.parts = bf16[4,784,128]{2,1,0:T(8,128)(2,1)S(1)} all-to-all(bf16[4,784,128]{2,1,0:T(8,128)(2,1)S(1)} %shard_map.182), channel_id=1, replica_groups={{0,1,128,129},{2,3,130,131},{4,5,132,133},{6,7,134,135},{8,10,12,14},{9..., dimensions={0} | all-to-all | bytes 1605632 | tf_op jit(solution)/shard_map/all_to_all | solution.py:578
  126.8 13.6 %all_to_all.23.parts = bf16[8,112,128]{2,1,0:T(8,128)(2,1)S(1)} all-to-all(bf16[8,112,128]{2,1,0:T(8,128)(2,1)S(1)} %shard_map.183), channel_id=1, replica_groups=mesh['xh'=2,'z'=8,'c'=2,'y'=4,'xl'=2] {'z'}, dimensions={0} | all-to-all | bytes 458752 | tf_op jit(solution)/shard_map/all_to_all | solution.py:585
  141.0 4.4 %collective-permute-start.12 = (f32[56,128]{1,0:T(8,128)S(1)}, f32[56,128]{1,0:T(8,128)S(1)}, u32[]{:S(2)}, u32[]{:S(2)}) collective-permute-start(f32[56,128]{1,0:T(8,128)S(1)} %get-tuple-element.120), channel_id=1, source_target_pairs={{0,8},{8,0},{1,9},{9,1},{2,10},{10,2},{3,11},{11,3},{4,12},{12,4},... | collective-permute-start | bytes 86024 | tf_op jit(solution)/shard_map/ppermute | solution.py:441
  145.4 0.9 collective-permute-done.12.recv
  146.2 1.3 shard_map.185
  (18 shorter events, 3.4 us)
Async XLA Ops:
  2.7 4.4 %collective-permute-start = (bf16[256,384]{1,0:T(8,128)(2,1)S(1)}, bf16[256,384]{1,0:T(8,128)(2,1)S(1)}, u32[]{:S(2)}, u32[]{:S(2)}) collective-permute-start(bf16[256,384]{1,0:T(8,128)(2,1)S(1)} %get-tuple-element.69), channel_id=1, source_target_pairs={{0,8},{8,0},{1,9},{9,1},{2,10},{10,2},{3,11},{11,3},{4,12},{12,4},... | collective-permute-start | bytes 589832 | tf_op jit(solution)/shard_map/ppermute | solution.py:441
  13.8 1.6 %collective-permute-start.2 = (bf16[512,256]{1,0:T(8,128)(2,1)S(1)}, bf16[512,256]{1,0:T(8,128)(2,1)S(1)}, u32[]{:S(2)}, u32[]{:S(2)}) collective-permute-start(bf16[512,256]{1,0:T(8,128)(2,1)S(1)} %get-tuple-element.70.refs_0_.ours), channel_id=1, source_target_pairs={{0,8},{8,0},{1,9},{9,1},{2,10},{10,2},{3,11},{11,3},{4,12},{12,4},... | collective-permute-start | bytes 786440 | tf_op jit(solution)/shard_map/ppermute | solution.py:441
  14.3 9.3 %collective-permute-start.1 = (bf16[512,256]{1,0:T(8,128)(2,1)S(1)}, bf16[512,256]{1,0:T(8,128)(2,1)S(1)}, u32[]{:S(2)}, u32[]{:S(2)}) collective-permute-start(bf16[512,256]{1,0:T(8,128)(2,1)S(1)} %get-tuple-element.70.refs_0_.ours), channel_id=1, source_target_pairs={{0,128},{128,0},{1,129},{129,1},{2,130},{130,2},{3,131},{131,3},{4... | collective-permute-start | bytes 786440 | tf_op jit(solution)/shard_map/ppermute | solution.py:441
  15.5 10.7 %collective-permute-start.4 = (bf16[512,256]{1,0:T(8,128)(2,1)S(1)}, bf16[512,256]{1,0:T(8,128)(2,1)S(1)}, u32[]{:S(2)}, u32[]{:S(2)}) collective-permute-start(bf16[512,256]{1,0:T(8,128)(2,1)S(1)} %collective-permute-done.2.refs_2_.refs_5_.other), channel_id=1, source_target_pairs={{0,112},{16,0},{32,16},{48,32},{64,48},{80,64},{96,80},{112,96},{1... | collective-permute-start | bytes 786440 | tf_op jit(solution)/shard_map/ppermute | solution.py:441
  20.9 8.3 %collective-permute-start.3 = (bf16[512,256]{1,0:T(8,128)(2,1)S(1)}, bf16[512,256]{1,0:T(8,128)(2,1)S(1)}, u32[]{:S(2)}, u32[]{:S(2)}) collective-permute-start(bf16[512,256]{1,0:T(8,128)(2,1)S(1)} %collective-permute-done.2.refs_2_.refs_5_.other), channel_id=1, source_target_pairs={{0,16},{16,32},{32,48},{48,64},{64,80},{80,96},{96,112},{112,0},{1... | collective-permute-start | bytes 786440 | tf_op jit(solution)/shard_map/ppermute | solution.py:441
  29.2 7.4 %collective-permute-start.5 = (bf16[512,256]{1,0:T(8,128)(2,1)S(1)}, bf16[512,256]{1,0:T(8,128)(2,1)S(1)}, u32[]{:S(2)}, u32[]{:S(2)}) collective-permute-start(bf16[512,256]{1,0:T(8,128)(2,1)S(1)} %collective-permute-done.3.refs_2_.refs_6_), channel_id=1, source_target_pairs={{0,16},{16,32},{32,48},{48,64},{64,80},{80,96},{96,112},{112,0},{1... | collective-permute-start | bytes 786440 | tf_op jit(solution)/shard_map/ppermute | solution.py:441
  29.2 7.4 %collective-permute-start.6 = (bf16[512,256]{1,0:T(8,128)(2,1)S(1)}, bf16[512,256]{1,0:T(8,128)(2,1)S(1)}, u32[]{:S(2)}, u32[]{:S(2)}) collective-permute-start(bf16[512,256]{1,0:T(8,128)(2,1)S(1)} %collective-permute-done.4.refs_3_.refs_7_), channel_id=1, source_target_pairs={{0,112},{16,0},{32,16},{48,32},{64,48},{80,64},{96,80},{112,96},{1... | collective-permute-start | bytes 786440 | tf_op jit(solution)/shard_map/ppermute | solution.py:441
  36.7 6.4 %collective-permute-start.7 = (bf16[512,256]{1,0:T(8,128)(2,1)S(1)}, bf16[512,256]{1,0:T(8,128)(2,1)S(1)}, u32[]{:S(2)}, u32[]{:S(2)}) collective-permute-start(bf16[512,256]{1,0:T(8,128)(2,1)S(1)} %collective-permute-done.5.refs_2_.refs_8_), channel_id=1, source_target_pairs={{0,16},{16,32},{32,48},{48,64},{64,80},{80,96},{96,112},{112,0},{1... | collective-permute-start | bytes 786440 | tf_op jit(solution)/shard_map/ppermute | solution.py:441
  36.7 6.4 %collective-permute-start.8 = (bf16[512,256]{1,0:T(8,128)(2,1)S(1)}, bf16[512,256]{1,0:T(8,128)(2,1)S(1)}, u32[]{:S(2)}, u32[]{:S(2)}) collective-permute-start(bf16[512,256]{1,0:T(8,128)(2,1)S(1)} %collective-permute-done.6.refs_3_.refs_9_), channel_id=1, source_target_pairs={{0,112},{16,0},{32,16},{48,32},{64,48},{80,64},{96,80},{112,96},{1... | collective-permute-start | bytes 786440 | tf_op jit(solution)/shard_map/ppermute | solution.py:441
  43.1 4.7 %collective-permute-start.10 = (bf16[256,256]{1,0:T(8,128)(2,1)S(1)}, bf16[256,256]{1,0:T(8,128)(2,1)S(1)}, u32[]{:S(2)}, u32[]{:S(2)}) collective-permute-start(bf16[256,256]{1,0:T(8,128)(2,1)S(1)} %slice.7), channel_id=1, source_target_pairs={{0,112},{16,0},{32,16},{48,32},{64,48},{80,64},{96,80},{112,96},{1... | collective-permute-start | bytes 393224 | tf_op jit(solution)/shard_map/ppermute | solution.py:441
  45.9 5.0 %collective-permute-start.9 = (bf16[256,256]{1,0:T(8,128)(2,1)S(1)}, bf16[256,256]{1,0:T(8,128)(2,1)S(1)}, u32[]{:S(2)}, u32[]{:S(2)}) collective-permute-start(bf16[256,256]{1,0:T(8,128)(2,1)S(1)} %slice.6), channel_id=1, source_target_pairs={{0,16},{16,32},{32,48},{48,64},{64,80},{80,96},{96,112},{112,0},{1... | collective-permute-start | bytes 393224 | tf_op jit(solution)/shard_map/ppermute | solution.py:441
  75.0 7.7 %collective-permute-start.11 = (bf16[512,256]{1,0:T(8,128)(2,1)S(1)}, bf16[512,256]{1,0:T(8,128)(2,1)S(1)}, u32[]{:S(2)}, u32[]{:S(2)}) collective-permute-start(bf16[512,256]{1,0:T(8,128)(2,1)S(1)} %get-tuple-element.109), channel_id=1, source_target_pairs={{0,128},{128,0},{1,129},{129,1},{2,130},{130,2},{3,131},{131,3},{4... | collective-permute-start | bytes 786440 | tf_op jit(solution)/shard_map/ppermute | solution.py:441
  141.0 5.2 %collective-permute-start.12 = (f32[56,128]{1,0:T(8,128)S(1)}, f32[56,128]{1,0:T(8,128)S(1)}, u32[]{:S(2)}, u32[]{:S(2)}) collective-permute-start(f32[56,128]{1,0:T(8,128)S(1)} %get-tuple-element.120), channel_id=1, source_target_pairs={{0,8},{8,0},{1,9},{9,1},{2,10},{10,2},{3,11},{11,3},{4,12},{12,4},... | collective-permute-start | bytes 86024 | tf_op jit(solution)/shard_map/ppermute | solution.py:441

commit v4 on v3

--- a/solution.py
+++ b/solution.py
@@ -125,8 +125,8 @@
     other = pl.multiple_of((1 - role) * ROWS, ROWS)
     x[pl.ds(own, ROWS), :] = keep[...]
     x[pl.ds(other, ROWS), :] = recv[...]
-    for start in range(0, CHIP, LANES):
-        rows = pl.ds(start, LANES)
+    for start in range(0, CHIP, ROWS):
+        rows = pl.ds(start, ROWS)
 
         def norm(values, normed, factor):
             center = values - jnp.mean(values, axis=-1, keepdims=True)
@@ -222,7 +222,7 @@
 
 
 def send_kernel(n_z, logit, place, sums, total, ours, *refs):
-    n_exp = n_z // 2 + 1
+    n_exp = 3
     expos = refs[:n_exp]
     blocks = refs[n_exp : n_exp + n_z + 1]
     send, scaled, across, loss = refs[n_exp + n_z + 1 : n_exp + n_z + 5]
@@ -230,9 +230,9 @@
     xh, z, role = place[0], place[1], place[2]
 
     def full(x_at, z_at, side):
-        mine = sums[(x_at * n_z + z_at) * 2 + side]
-        partner = sums[((1 - x_at) * n_z + z_at) * 2 + side]
-        return mine[:4] + partner[4:]
+        mine = sums[x_at * n_z + z_at]
+        partner = sums[(1 - x_at) * n_z + z_at]
+        return mine[side * 8 : side * 8 + 4] + partner[side * 8 + 4 : side * 8 + 8]
 
     order = [0]
     for k in range(1, n_z // 2):
@@ -240,10 +240,10 @@
     order.append(n_z // 2)
     lines[...] = jnp.ones((LANES, LANES), F32)
     for k, shift in enumerate(order):
-        lines[4 * k : 4 * k + 4, :] = 1.0 / full(xh, lax.rem(z + shift, n_z), 1 - role)
-    mine = full(xh, z, role)
+        lines[4 * k : 4 * k + 4, :] = 1.0 / full(xh, lax.rem(z + shift, n_z), 1)
+    mine = full(xh, z, 0)
     lines[4 * n_z : 4 * n_z + 4, :] = 1.0 / mine
-    lines[4 * n_z + 4 : 4 * n_z + 8, :] = 1.0 / full(1 - xh, z, role)
+    lines[4 * n_z + 4 : 4 * n_z + 8, :] = 1.0 / full(1 - xh, z, 0)
     columns = lines[...].T
     across[...] = columns
 
@@ -261,7 +261,7 @@
     for start in range(CHIP, 2 * CHIP, ROWS):
         mix_rows(expos, scaled, total, columns, 4 * n_z, start, write)
 
-    logs = jnp.log(mine) + jnp.log(full(xh, z, 1 - role))
+    logs = jnp.log(mine) + jnp.log(full(xh, z, 1))
     logs = jnp.where(role == 0, logs[:2], logs[2:])
     at = pl.multiple_of(role * ROWS, ROWS)
     both = ours[pl.ds(at, ROWS), :].astype(F32) * blocks[0][pl.ds(at, ROWS), :].astype(F32)
@@ -356,9 +356,9 @@
     def slot(y, x_at):
         return jnp.where(role == 0, y, x_at), jnp.where(role == 0, x_at, y)
 
-    line = lax.broadcasted_iota(jnp.int32, (tall, LANES), 0)
+    row = lax.broadcasted_iota(jnp.int32, (tall, LANES), 0)
     lane = lax.broadcasted_iota(jnp.int32, (tall, LANES), 1)
-    wanted = lane // 16 == (line // 32 % 2) * 4 + line % 4
+    wanted = lane // 16 == (row // 32 % 2) * 4 + row % 4
     pack_row = lax.broadcasted_iota(jnp.int32, (32, tall), 0)
     pack_col = lax.broadcasted_iota(jnp.int32, (32, tall), 1)
     pack = (pack_col // 64 == pack_row // 8) & (pack_col // 4 % 8 == pack_row % 8)
@@ -370,20 +370,39 @@
         for left, right, tile in ((h1, p2_s, 0), (h2, ge_s, 8), (None, x, 10)):
             units = turned(order, p1_s[:, span]) if left is None else left[span, :]
             value = dot_nn(units, right[:, : right.shape[1] // EMB * EMB])
-            for k in range(value.shape[1] // LANES):
-                for part in range(8):
-                    piece = value[part * 32 : part * 32 + 32, k * LANES : (k + 1) * LANES]
-                    at = (tile + k) * 64 + half * 32
-                    first, second = slot(part // 2, xh * 2 + part % 2)
-                    grads[first, second, at : at + 32, :] = piece.astype(BF)
+            for part in range(8):
+                first, second = slot(part // 2, xh * 2 + part % 2)
+                for z in range(4):
+                    line = part * 32 + z * 8
+                    base = second * (4 * TILES * 8) + (half * 2 + z // 2) * TILES * 8
+                    for k in range(0, value.shape[1] // LANES, 2):
+                        two = [
+                            value[line : line + 8, at * LANES : (at + 1) * LANES] for at in (k, k + 1)
+                        ]
+                        at = pl.multiple_of(base + (tile + k) * 8, 16)
+                        piece = jnp.concatenate(two, axis=0).astype(BF)
+                        grads[first * 2 + z % 2, pl.ds(at, 16), :] = piece
             if tile == 10:
                 value = jnp.where(wanted, dot_nn(units, x[:, EMB:]), 0.0).astype(BF)
                 packed.append(dot_nn(pack, value))
-    for part in range(16):
-        y, xh = part // 4, part // 2 % 2
-        first, second = slot(y, part % 4)
-        two = [packed[2 * xh + half][y * 8 : y * 8 + 8] for half in range(2)]
-        grads[first, second, TILES * 64 : TILES * 64 + 16, :] = jnp.concatenate(two, axis=0).astype(BF)
+    halves = {}
+    for y in range(4):
+        for xh in range(2):
+            pieces = [packed[2 * xh + half][y * 8 : y * 8 + 8] for half in range(2)]
+            for parity in range(2):
+                rows = [p[z * 4 + parity * 2 :][:2] for p in pieces for z in range(2)]
+                for xl in range(2):
+                    halves[y, xh * 2 + xl, parity] = jnp.concatenate(rows, axis=0)
+    low = 16 * TILES * 8
+    for first in range(4):
+        for parity in range(2):
+            for pair in (0, 2):
+                rows = [
+                    jnp.where(role == 0, halves[first, at, parity], halves[at, first, parity])
+                    for at in (pair, pair + 1)
+                ]
+                piece = jnp.concatenate(rows, axis=0).astype(BF)
+                grads[first * 2 + parity, low + pair * 8 : low + pair * 8 + 16, :] = piece
 
 
 def plus(parts, rows):
@@ -393,20 +412,12 @@
     return value
 
 
-def add_kernel(parts, out):
-    for dest in range(parts.shape[1]):
-        value = parts[0, dest].astype(F32)
-        for k in range(1, parts.shape[0]):
-            value = value + parts[k, dest].astype(F32)
-        out[dest] = value.astype(BF)
-
-
 def sum_kernel(parts, out):
-    tiles = [plus(parts, pl.ds(k * 64, 64)) for k in range(TILES)]
-    extra = plus(parts, pl.ds(TILES * 64, 16))
-    for z in range(out.shape[0]):
-        rows = [tile[z * 8 : z * 8 + 8] for tile in tiles] + [extra]
-        out[z] = jnp.concatenate(rows, axis=0).astype(BF)
+    height = TILES * 8
+    for part in range(16):
+        extra = pl.ds(16 * height + part // 8 * 16, 16)
+        out[part, :height, :] = plus(parts, pl.ds(part * height, height)).astype(BF)
+        out[part, height:, :] = plus(parts, extra).astype(BF)
 
 
 def split_kernel(place, parts, keep, send, extra):
@@ -418,8 +429,9 @@
         keep[k * 4 : k * 4 + 4, :] = jnp.where(role == 0, low, high)
         send[k * 4 : k * 4 + 4, :] = jnp.where(role == 0, high, low)
     blank = jnp.zeros((8, LANES), F32)
+    part = (place[0] * 2 + place[3]) % 2 * 4 + place[1] // 2
     for out, side in ((keep, role), (send, 1 - role)):
-        out[TILES * 4 :, :] = blank + extra[pl.ds(place[1] * 2 + side, 1), :]
+        out[TILES * 4 :, :] = blank + extra[pl.ds(part * 2 + side, 1), :]
 
 
 def last_kernel(place, keep, recv, obs_a, act_a, mid_a, out_a, obs_b, mid_b, out_b):
@@ -501,36 +513,33 @@
         ],
     )(place, keep, recv, sa_obs, sa_act, sa_mid, sa_out, goal_obs, goal_mid, goal_out)
 
-    other = shifted(unit, "c", 1)
-    ahead = back = other
-    theirs = shifted(unit, "xh", 1)
-    steps = [[other]]
+    def crossed(value, shift):
+        hop = [((k + shift) % n_z * 2 + 1 - c) for k in range(n_z) for c in range(2)]
+        return lax.ppermute(value, ("z", "c"), list(enumerate(hop)))
+
+    ahead, back = crossed(unit, 1), crossed(unit, -1)
+    s1, h1 = slopes(n1)
+    s2, h2 = slopes(n2)
+    ahead, back, s1, h1, s2, h2, late = lax.optimization_barrier((ahead, back, s1, h1, s2, h2, unit))
+    steps = [[ahead, back]]
+    for k in range(2, n_z // 2 - 1):
+        ahead, back = shifted(ahead, "z", 1), shifted(back, "z", -1)
+        steps.append([ahead, back])
+    other, theirs = shifted(late, "c", 1), shifted(late, "xh", 1)
+    early = [other] + [block for step in steps for block in step]
+    ahead, back = shifted(ahead, "z", 1), shifted(back, "z", -1)
     factor = logit * math.log2(math.e)
-    expos = []
-    prev = None
-    for k in range(n_z // 2 + 1):
-        if k < n_z // 2 - 1:
-            ahead, back = shifted(ahead, "z", 1), shifted(back, "z", -1)
-            steps.append([ahead, back])
-        elif k == n_z // 2 - 1:
-            steps.append([shifted(ahead[:ROWS], "z", 1), shifted(back[ROWS:], "z", -1)])
-        expo, part, total = scores(unit, theirs, steps[k], prev, k == n_z // 2, factor)
+    expo, part, total = scores(unit, theirs, early, None, False, factor)
+    ahead, back, part, total = lax.optimization_barrier((ahead, back, part, total))
+    last = [shifted(ahead[:ROWS], "z", 1), shifted(back[ROWS:], "z", -1)]
+    expos = [expo]
+    for final, step in enumerate(([ahead, back], last)):
+        expo, part, total = scores(unit, theirs, step, (part, total), final == 1, factor)
         expos.append(expo)
-        prev = (part, total)
-        if k == 1:
-            s1, h1 = slopes(n1)
-            part, s1, h1 = lax.optimization_barrier((part, s1, h1))
-        if k == 2:
-            s2, h2 = slopes(n2)
-            part, s2, h2 = lax.optimization_barrier((part, s2, h2))
-        prev = (part, total)
-        if k < n_z // 2 - 1:
-            ahead, back, part, total = lax.optimization_barrier((ahead, back, part, total))
-            steps[-1] = [ahead, back]
-            prev = (part, total)
-    blocks = [block for step in steps for block in step]
-    everyone = jnp.broadcast_to(part[None], (4 * n_z, 8, LANES))
-    sums = lax.all_to_all(everyone, ("xh", "z", "c"), 0, 0)
+    blocks = early + [ahead, back] + last
+    both = jnp.concatenate([part, shifted(part, "c", 1)], axis=0)
+    everyone = jnp.broadcast_to(both[None], (2 * n_z, 16, LANES))
+    sums = lax.all_to_all(everyone, ("xh", "z"), 0, 0)
     partial, scaled, across, loss = call(
         functools.partial(send_kernel, n_z, logit),
         [
@@ -555,7 +564,7 @@
     )(total, scaled, across, *expos)[0]
     grads = call(
         functools.partial(backward_kernel, coef),
-        [shape((4, 4, TILES * 64 + 16, LANES), BF)],
+        [shape((8, 16 * TILES * 8 + 32, LANES), BF)],
         [SMEM] + [VMEM] * 14 + [HBM] * 4,
         scratch=[
             pltpu.VMEM((HID, HID), BF),
@@ -570,19 +579,27 @@
         sa_mid, sa_out, goal_mid, goal_out,
     )[0]
 
-    along_y = [[y * 4 + x_at for y in range(4)] for x_at in range(4)]
-    along_x = [[y * 4 + x_at for x_at in range(4)] for y in range(4)]
-
-    def exchange(parts, low, high):
-        groups = low + [[16 + member for member in group] for group in high]
-        return lax.all_to_all(parts, ("c", "y", "xh", "xl"), 0, 0, axis_index_groups=groups)
-
-    height = TILES * 64 + 16
-    grads = exchange(grads, along_y, along_x)
-    grads = call(add_kernel, [shape((4, height, LANES), BF)], [VMEM])(grads)[0]
-    grads = exchange(grads, along_x, along_y)
-    grads = call(sum_kernel, [shape((n_z, TILES * 8 + 16, LANES), BF)], [VMEM])(grads)[0]
-    grads = lax.all_to_all(grads, "z", 0, 0)
+    def member(c, first, second, z):
+        y, x_at = (first, second) if c == 0 else (second, first)
+        return ((c * 4 + y) * 4 + x_at) * n_z + z % n_z
+
+    half = n_z // 2
+    near = [
+        [member(c, a, b, 2 * q + p if c == 0 or p else 2 * q + 2) for a in range(4) for p in range(2)]
+        for c in range(2)
+        for b in range(4)
+        for q in range(half)
+    ]
+    far = [
+        [member(c, a, b, 2 * q + p) for b in range(4) for q in range(half)]
+        for c in range(2)
+        for a in range(4)
+        for p in range(2)
+    ]
+    axes = ("c", "y", "xh", "xl", "z")
+    grads = lax.all_to_all(grads, axes, 0, 0, axis_index_groups=near)
+    grads = call(sum_kernel, [shape((16, TILES * 8 + 16, LANES), BF)], [VMEM])(grads)[0]
+    grads = lax.all_to_all(grads, axes, 0, 0, axis_index_groups=far)
     keep, send = call(
         split_kernel,
         [shape((TILES * 4 + 8, LANES), F32)] * 2,

time: 148 us -> 141 us (0.953)
  blocking collectives: 70.4 us -> 63.9 us
  Pallas kernels: 30.2 us -> 28.6 us
    ppermute x0 -> x2, waiting for transfers between devices: none -> 7.36 us  [crossed(): return lax.ppermute(value, ('z', 'c'), list(enumerate(hop)))]
    all_to_all x4 -> x3, blocking collectives: 70.4 us -> 63.9 us  [the longest x1 25.9 us: body(): grads = lax.all_to_all(grads, axes, 0, 0, axis_index_groups=near)]
    ppermute x13 -> x12, waiting for transfers between devices: 23.2 us -> 16.7 us  [shifted(): lax.ppermute(value, axis, [(k, (k + shift) % count) for k in range(count)])]
    ppermute x0 -> x2, starting transfers between devices: none -> 4.17 us  [crossed(): return lax.ppermute(value, ('z', 'c'), list(enumerate(hop)))]
    ppermute x13 -> x12, starting transfers between devices: 22.9 us -> 19.3 us  [shifted(): lax.ppermute(value, axis, [(k, (k + shift) % count) for k in range(count)])]
    pallas_call x5 -> x3, Pallas kernels: 6.1 us -> 5.74 us  [scores(): return call(kernel, outs, [VMEM] * len(args), cost=cost)(*args)]
    pallas_call x3 -> x2, Pallas kernels: 7.87 us -> 7.86 us  [the longest x1 7.43 us: body(): call(functools.partial(backward_kernel, coef), [shape((8, 16 * TILES * 8...]
  transfers between devices with their start and end apart: 13 -> 14, of which waited for: 11 -> 11; matrix products, arithmetic and copies ran while one was open for 0% -> 0% of each run, Pallas kernels for 6% -> 6%
where the time goes in v4:
time: 141 us
  blocking collectives  63.9 us (45%)
  Pallas kernels  28.6 us (20%)
  waiting for transfers between devices  24.1 us (17%)
  starting transfers between devices  23.5 us (17%)
    all_to_all x1, blocking collectives, body(): grads = lax.all_to_all(grads, axes, 0, 0, axis_index_groups=near)  25.9 us
    all_to_all x1, blocking collectives, body(): grads = lax.all_to_all(grads, axes, 0, 0, axis_index_groups=far)  24.2 us
    ppermute x12, starting transfers between devices, shifted(): lax.ppermute(value, axis, [(k, (k + shift) % count) for k in range(count)])  19.3 us
    ppermute x12, waiting for transfers between devices, shifted(): lax.ppermute(value, axis, [(k, (k + shift) % count) for k in range(count)])  16.7 us
    all_to_all x1, blocking collectives, body(): sums = lax.all_to_all(everyone, ('xh', 'z'), 0, 0)  13.8 us
    pallas_call x1, Pallas kernels, body(): call(functools.partial(backward_kernel, coef), [shape((8, 16 * TILES * 8...  7.43 us
    ppermute x2, waiting for transfers between devices, crossed(): return lax.ppermute(value, ('z', 'c'), list(enumerate(hop)))  7.36 us
    pallas_call x3, Pallas kernels, scores(): return call(kernel, outs, [VMEM] * len(args), cost=cost)(*args)  5.74 us
  transfers between devices with their start and end apart: 14, of which 11 were waited for; matrix products, arithmetic and copies ran while one was open for 0% of the time, Pallas kernels for 6%

profile of v4, /device:TPU:1, one launch (start us, length us, event | category | flops | bytes accessed | tf_op | source)
XLA Modules:
  0.0 140.9 jit_solution(6521844192799010817)
XLA Ops:
  0.7 2.0 %shard_map.170 = (bf16[256,384]{1,0:T(8,128)(2,1)S(1)}, bf16[256,384]{1,0:T(8,128)(2,1)S(1)}) custom-call(s32[4]{0:T(128)S(1)} %pad_add_fusion.place, s32[1,256]{1,0:T(1,128)} %replay.1, s32[1,256]{1,0:T(1,128)} %offset.1, bf16[320,256]{1,0:T(8,128)(2,1)} %bitcast.11, bf16[16,320]{1,0:T(8,128)(2,1)} %bitcast.12), custom_call_target="tpu_custom_call" | custom-call | tf_op jit(solution)/shard_map/pallas_call | solution.py:482
  2.7 3.3 %collective-permute-start = (bf16[256,384]{1,0:T(8,128)(2,1)S(1)}, bf16[256,384]{1,0:T(8,128)(2,1)S(1)}, u32[]{:S(2)}, u32[]{:S(2)}) collective-permute-start(bf16[256,384]{1,0:T(8,128)(2,1)S(1)} %get-tuple-element.56), channel_id=1, source_target_pairs={{0,8},{8,0},{1,9},{9,1},{2,10},{10,2},{3,11},{11,3},{4,12},{12,4},... | collective-permute-start | bytes 589832 | tf_op jit(solution)/shard_map/ppermute | solution.py:453
  6.0 1.1 collective-permute-done.recv
  7.1 5.5 %shard_map.171 = (bf16[512,384]{1,0:T(8,128)(2,1)S(1)}, f32[512,1024]{1,0:T(8,128)S(1)}, f32[512,1]{1,0:T(8,128)S(1)}, f32[512,1024]{1,0:T(8,128)S(1)}, f32[512,...) custom-call(s32[4]{0:T(128)S(1)} %pad_add_fusion.place, ...), custom_call_target="tpu_custom_call" | custom-call | tf_op jit(solution)/shard_map/pallas_call | solution.py:495
  12.6 4.2 %collective-permute-start.2 = (bf16[512,256]{1,0:T(8,128)(2,1)S(1)}, bf16[512,256]{1,0:T(8,128)(2,1)S(1)}, u32[]{:S(2)}, u32[]{:S(2)}) collective-permute-start(bf16[512,256]{1,0:T(8,128)(2,1)S(1)} %get-tuple-element.64.refs_0_.ours), channel_id=1, source_target_pairs={{0,120},{8,112},{16,8},{24,0},{32,24},{40,16},{48,40},{56,32},{64,... | collective-permute-start | bytes 786440 | tf_op jit(solution)/shard_map/ppermute | solution.py:518
  16.8 1.0 shard_map.172
  17.8 1.0 shard_map.173
  18.7 3.9 %collective-permute-done.2.refs_4_.refs_5_ = bf16[512,256]{1,0:T(8,128)(2,1)S(1)} collective-permute-done((bf16[512,256]{1,0:T(8,128)(2,1)S(1)}, bf16[512,256]{1,0:T(8,128)(2,1)S(1)}, u32[]{:S(2)}, u32[]{:S(2)}) %collective-permute-start.2) | collective-permute-done | bytes 262176 | tf_op jit(solution)/shard_map/ppermute | solution.py:518
  22.6 3.5 %collective-permute-done.1.refs_3_.refs_4_ = bf16[512,256]{1,0:T(8,128)(2,1)S(1)} collective-permute-done((bf16[512,256]{1,0:T(8,128)(2,1)S(1)}, bf16[512,256]{1,0:T(8,128)(2,1)S(1)}, u32[]{:S(2)}, u32[]{:S(2)}) %collective-permute-start.1) | collective-permute-done | bytes 262176 | tf_op jit(solution)/shard_map/ppermute | solution.py:518
  26.1 2.7 %collective-permute-start.6 = (bf16[512,256]{1,0:T(8,128)(2,1)S(1)}, bf16[512,256]{1,0:T(8,128)(2,1)S(1)}, u32[]{:S(2)}, u32[]{:S(2)}) collective-permute-start(bf16[512,256]{1,0:T(8,128)(2,1)S(1)} %collective-permute-done.2.refs_4_.refs_5_), channel_id=1, source_target_pairs={{0,112},{16,0},{32,16},{48,32},{64,48},{80,64},{96,80},{112,96},{1... | collective-permute-start | bytes 786440 | tf_op jit(solution)/shard_map/ppermute | solution.py:453
  28.8 0.8 collective-permute-start.8
  29.5 2.8 %collective-permute-start.3 = (bf16[512,256]{1,0:T(8,128)(2,1)S(1)}, bf16[512,256]{1,0:T(8,128)(2,1)S(1)}, u32[]{:S(2)}, u32[]{:S(2)}) collective-permute-start(bf16[512,256]{1,0:T(8,128)(2,1)S(1)} %get-tuple-element.64.refs_0_.ours), channel_id=1, source_target_pairs={{0,128},{128,0},{1,129},{129,1},{2,130},{130,2},{3,131},{131,3},{4... | collective-permute-start | bytes 786440 | tf_op jit(solution)/shard_map/ppermute | solution.py:453
  32.3 2.7 %collective-permute-done.4.refs_5_.refs_6_ = bf16[512,256]{1,0:T(8,128)(2,1)S(1)} collective-permute-done((bf16[512,256]{1,0:T(8,128)(2,1)S(1)}, bf16[512,256]{1,0:T(8,128)(2,1)S(1)}, u32[]{:S(2)}, u32[]{:S(2)}) %collective-permute-start.4) | collective-permute-done | bytes 262176 | tf_op jit(solution)/shard_map/ppermute | solution.py:453
  35.0 2.7 %collective-permute-start.7 = (bf16[512,256]{1,0:T(8,128)(2,1)S(1)}, bf16[512,256]{1,0:T(8,128)(2,1)S(1)}, u32[]{:S(2)}, u32[]{:S(2)}) collective-permute-start(bf16[512,256]{1,0:T(8,128)(2,1)S(1)} %collective-permute-done.6.refs_6_.refs_7_), channel_id=1, source_target_pairs={{0,112},{16,0},{32,16},{48,32},{64,48},{80,64},{96,80},{112,96},{1... | collective-permute-start | bytes 786440 | tf_op jit(solution)/shard_map/ppermute | solution.py:453
  37.7 1.3 collective-permute-done.3.refs_1_
  39.0 3.3 %shard_map.174 = (bf16[1024,2560]{1,0:T(8,128)(2,1)S(1)}, f32[1024,128]{1,0:T(8,128)S(1)}, f32[1024,256]{1,0:T(8,128)S(1)}) custom-call(bf16[512,256]{1,0:T(8,128)(2,1)S(1)} %get-tuple-element.64.refs_0_.ours, bf16[512,256]{1,0:T(8,128)(2,1)S(1)} %collective-permute-done.3.refs_1_, bf16[512,256]{1,0:T(8,128)(2,1)S(1)} %collective-permute-done.8.refs_2_.refs_3_.other, ...), custom_call_target="tpu_custom_call" | custom-call | flops 2684354560 | bytes 6291456 | tf_op jit(solution)/shard_map/pallas_call | solution.py:207
  43.0 2.5 %collective-permute-start.10 = (bf16[256,256]{1,0:T(8,128)(2,1)S(1)}, bf16[256,256]{1,0:T(8,128)(2,1)S(1)}, u32[]{:S(2)}, u32[]{:S(2)}) collective-permute-start(bf16[256,256]{1,0:T(8,128)(2,1)S(1)} %slice.7), channel_id=1, source_target_pairs={{0,112},{16,0},{32,16},{48,32},{64,48},{80,64},{96,80},{112,96},{1... | collective-permute-start | bytes 393224 | tf_op jit(solution)/shard_map/ppermute | solution.py:453
  45.5 1.4 %shard_map.175 = (bf16[1024,1024]{1,0:T(8,128)(2,1)S(1)}, f32[1024,128]{1,0:T(8,128)S(1)}, f32[1024,256]{1,0:T(8,128)S(1)}) custom-call(bf16[512,256]{1,0:T(8,128)(2,1)S(1)} %get-tuple-element.64.refs_0_.ours, bf16[512,256]{1,0:T(8,128)(2,1)S(1)} %collective-permute-done.3.refs_1_, bf16[512,256]{1,0:T(8,128)(2,1)S(1)} %collective-permute-done.5.refs_2_.refs_8_, ...), custom_call_target="tpu_custom_call" | custom-call | flops 1073741824 | bytes 3145728 | tf_op jit(solution)/shard_map/pallas_call | solution.py:207
  47.5 3.1 %collective-permute-done.9.refs_2_.refs_10_ = bf16[256,256]{1,0:T(8,128)(2,1)S(1)} collective-permute-done((bf16[256,256]{1,0:T(8,128)(2,1)S(1)}, bf16[256,256]{1,0:T(8,128)(2,1)S(1)}, u32[]{:S(2)}, u32[]{:S(2)}) %collective-permute-start.9) | collective-permute-done | bytes 131104 | tf_op jit(solution)/shard_map/ppermute | solution.py:453
  50.5 1.0 shard_map.176
  51.6 3.7 %collective-permute-start.11 = (f32[8,128]{1,0:T(8,128)S(1)}, f32[8,128]{1,0:T(8,128)S(1)}, u32[]{:S(2)}, u32[]{:S(2)}) collective-permute-start(f32[8,128]{1,0:T(8,128)S(1)} %get-tuple-element.75), channel_id=1, source_target_pairs={{0,8},{8,0},{1,9},{9,1},{2,10},{10,2},{3,11},{11,3},{4,12},{12,4},... | collective-permute-start | bytes 12296 | tf_op jit(solution)/shard_map/ppermute | solution.py:453
  55.3 0.8 collective-permute-done.11
  56.2 13.8 %all_to_all.15.sums = f32[16,16,128]{2,1,0:T(8,128)S(1)} all-to-all(f32[16,16,128]{2,1,0:T(8,128)S(1)} %broadcast_in_dim.2), channel_id=1, replica_groups=mesh['xh'=2,'z'=8,'c'=2,'y'=4,'xl'=2] {'xh','z'}, dimensions={0} | all-to-all | bytes 262144 | tf_op jit(solution)/shard_map/all_to_all | solution.py:542
  70.0 2.5 %shard_map.177 = (bf16[512,256]{1,0:T(8,128)(2,1)S(1)}, bf16[4096,256]{1,0:T(8,128)(2,1)S(1)}, f32[128,128]{1,0:T(8,128)S(1)}, f32[1,256]{1,0:T(1,128)}) custom-call(s32[4]{0:T(128)S(1)} %pad_add_fusion.place, f32[16,16,128]{2,1,0:T(8,128)S(1)} %all_to_all.15.sums, f32[1024,256]{1,0:T(8,128)S(1)} %get-tuple-element.76.total, ...), custom_call_target="tpu_custom_call" | custom-call | tf_op jit(solution)/shard_map/pallas_call | solution.py:543
  72.4 0.8 collective-permute-start.12
  73.3 1.2 shard_map.178.own
  74.5 5.3 %collective-permute-done.12.recv = bf16[512,256]{1,0:T(8,128)(2,1)S(1)} collective-permute-done((bf16[512,256]{1,0:T(8,128)(2,1)S(1)}, bf16[512,256]{1,0:T(8,128)(2,1)S(1)}, u32[]{:S(2)}, u32[]{:S(2)}) %collective-permute-start.12) | collective-permute-done | bytes 262176 | tf_op jit(solution)/shard_map/ppermute | solution.py:453
  79.8 7.4 %shard_map.179 = bf16[8,1568,128]{2,1,0:T(8,128)(2,1)S(1)} custom-call(s32[4]{0:T(128)S(1)} %pad_add_fusion.place, f32[512,256]{1,0:T(8,128)S(1)} %shard_map.178.own, bf16[512,256]{1,0:T(8,128)(2,1)S(1)} %collective-permute-done.12.recv, bf16[512,256]{1,0:T(8,128)(2,1)S(1)} %collective-permute-done.8.refs_2_.refs_3_.other, ...), custom_call_target="tpu_custom_call" | custom-call | tf_op jit(solution)/shard_map/pallas_call | solution.py:565
  87.2 25.9 %all_to_all.16.parts = bf16[8,1568,128]{2,1,0:T(8,128)(2,1)S(1)} all-to-all(bf16[8,1568,128]{2,1,0:T(8,128)(2,1)S(1)} %shard_map.179), channel_id=1, replica_groups={{0,16,2,18,4,20,6,22},{32,48,34,50,36,52,38,54},{64,80,66,82,68,84,70,8..., dimensions={0} | all-to-all | bytes 6422528 | tf_op jit(solution)/shard_map/all_to_all | solution.py:600
  113.6 24.2 %all_to_all.17.parts = bf16[16,112,128]{2,1,0:T(8,128)(2,1)S(1)} all-to-all(bf16[16,112,128]{2,1,0:T(8,128)(2,1)S(1)} %shard_map.180), channel_id=1, replica_groups={{0,32,64,96,1,33,65,97,128,160,192,224,129,161,193,225},{16,48,80,112,1..., dimensions={0} | all-to-all | bytes 917504 | tf_op jit(solution)/shard_map/all_to_all | solution.py:602
  138.5 1.2 collective-permute-done.13.recv
  139.6 1.3 shard_map.182
  (17 shorter events, 2.5 us)
Async XLA Ops:
  2.7 4.4 %collective-permute-start = (bf16[256,384]{1,0:T(8,128)(2,1)S(1)}, bf16[256,384]{1,0:T(8,128)(2,1)S(1)}, u32[]{:S(2)}, u32[]{:S(2)}) collective-permute-start(bf16[256,384]{1,0:T(8,128)(2,1)S(1)} %get-tuple-element.56), channel_id=1, source_target_pairs={{0,8},{8,0},{1,9},{9,1},{2,10},{10,2},{3,11},{11,3},{4,12},{12,4},... | collective-permute-start | bytes 589832 | tf_op jit(solution)/shard_map/ppermute | solution.py:453
  12.6 10.0 %collective-permute-start.2 = (bf16[512,256]{1,0:T(8,128)(2,1)S(1)}, bf16[512,256]{1,0:T(8,128)(2,1)S(1)}, u32[]{:S(2)}, u32[]{:S(2)}) collective-permute-start(bf16[512,256]{1,0:T(8,128)(2,1)S(1)} %get-tuple-element.64.refs_0_.ours), channel_id=1, source_target_pairs={{0,120},{8,112},{16,8},{24,0},{32,24},{40,16},{48,40},{56,32},{64,... | collective-permute-start | bytes 786440 | tf_op jit(solution)/shard_map/ppermute | solution.py:518
  16.8 9.3 %collective-permute-start.1 = (bf16[512,256]{1,0:T(8,128)(2,1)S(1)}, bf16[512,256]{1,0:T(8,128)(2,1)S(1)}, u32[]{:S(2)}, u32[]{:S(2)}) collective-permute-start(bf16[512,256]{1,0:T(8,128)(2,1)S(1)} %get-tuple-element.64.refs_0_.ours), channel_id=1, source_target_pairs={{0,24},{8,16},{16,40},{24,32},{32,56},{40,48},{48,72},{56,64},{64,... | collective-permute-start | bytes 786440 | tf_op jit(solution)/shard_map/ppermute | solution.py:518
  26.1 8.9 %collective-permute-start.4 = (bf16[512,256]{1,0:T(8,128)(2,1)S(1)}, bf16[512,256]{1,0:T(8,128)(2,1)S(1)}, u32[]{:S(2)}, u32[]{:S(2)}) collective-permute-start(bf16[512,256]{1,0:T(8,128)(2,1)S(1)} %collective-permute-done.1.refs_3_.refs_4_), channel_id=1, source_target_pairs={{0,16},{16,32},{32,48},{48,64},{64,80},{80,96},{96,112},{112,0},{1... | collective-permute-start | bytes 786440 | tf_op jit(solution)/shard_map/ppermute | solution.py:453
  26.1 8.9 %collective-permute-start.6 = (bf16[512,256]{1,0:T(8,128)(2,1)S(1)}, bf16[512,256]{1,0:T(8,128)(2,1)S(1)}, u32[]{:S(2)}, u32[]{:S(2)}) collective-permute-start(bf16[512,256]{1,0:T(8,128)(2,1)S(1)} %collective-permute-done.2.refs_4_.refs_5_), channel_id=1, source_target_pairs={{0,112},{16,0},{32,16},{48,32},{64,48},{80,64},{96,80},{112,96},{1... | collective-permute-start | bytes 786440 | tf_op jit(solution)/shard_map/ppermute | solution.py:453
  28.8 8.9 %collective-permute-start.8 = (bf16[512,256]{1,0:T(8,128)(2,1)S(1)}, bf16[512,256]{1,0:T(8,128)(2,1)S(1)}, u32[]{:S(2)}, u32[]{:S(2)}) collective-permute-start(bf16[512,256]{1,0:T(8,128)(2,1)S(1)} %get-tuple-element.64.refs_0_.ours), channel_id=1, source_target_pairs={{0,8},{8,0},{1,9},{9,1},{2,10},{10,2},{3,11},{11,3},{4,12},{12,4},... | collective-permute-start | bytes 786440 | tf_op jit(solution)/shard_map/ppermute | solution.py:453
  29.5 9.4 %collective-permute-start.3 = (bf16[512,256]{1,0:T(8,128)(2,1)S(1)}, bf16[512,256]{1,0:T(8,128)(2,1)S(1)}, u32[]{:S(2)}, u32[]{:S(2)}) collective-permute-start(bf16[512,256]{1,0:T(8,128)(2,1)S(1)} %get-tuple-element.64.refs_0_.ours), channel_id=1, source_target_pairs={{0,128},{128,0},{1,129},{129,1},{2,130},{130,2},{3,131},{131,3},{4... | collective-permute-start | bytes 786440 | tf_op jit(solution)/shard_map/ppermute | solution.py:453
  35.0 8.0 %collective-permute-start.5 = (bf16[512,256]{1,0:T(8,128)(2,1)S(1)}, bf16[512,256]{1,0:T(8,128)(2,1)S(1)}, u32[]{:S(2)}, u32[]{:S(2)}) collective-permute-start(bf16[512,256]{1,0:T(8,128)(2,1)S(1)} %collective-permute-done.4.refs_5_.refs_6_), channel_id=1, source_target_pairs={{0,16},{16,32},{32,48},{48,64},{64,80},{80,96},{96,112},{112,0},{1... | collective-permute-start | bytes 786440 | tf_op jit(solution)/shard_map/ppermute | solution.py:453
  35.0 8.0 %collective-permute-start.7 = (bf16[512,256]{1,0:T(8,128)(2,1)S(1)}, bf16[512,256]{1,0:T(8,128)(2,1)S(1)}, u32[]{:S(2)}, u32[]{:S(2)}) collective-permute-start(bf16[512,256]{1,0:T(8,128)(2,1)S(1)} %collective-permute-done.6.refs_6_.refs_7_), channel_id=1, source_target_pairs={{0,112},{16,0},{32,16},{48,32},{64,48},{80,64},{96,80},{112,96},{1... | collective-permute-start | bytes 786440 | tf_op jit(solution)/shard_map/ppermute | solution.py:453
  43.0 4.4 %collective-permute-start.10 = (bf16[256,256]{1,0:T(8,128)(2,1)S(1)}, bf16[256,256]{1,0:T(8,128)(2,1)S(1)}, u32[]{:S(2)}, u32[]{:S(2)}) collective-permute-start(bf16[256,256]{1,0:T(8,128)(2,1)S(1)} %slice.7), channel_id=1, source_target_pairs={{0,112},{16,0},{32,16},{48,32},{64,48},{80,64},{96,80},{112,96},{1... | collective-permute-start | bytes 393224 | tf_op jit(solution)/shard_map/ppermute | solution.py:453
  45.5 5.0 %collective-permute-start.9 = (bf16[256,256]{1,0:T(8,128)(2,1)S(1)}, bf16[256,256]{1,0:T(8,128)(2,1)S(1)}, u32[]{:S(2)}, u32[]{:S(2)}) collective-permute-start(bf16[256,256]{1,0:T(8,128)(2,1)S(1)} %slice.6), channel_id=1, source_target_pairs={{0,16},{16,32},{32,48},{48,64},{64,80},{80,96},{96,112},{112,0},{1... | collective-permute-start | bytes 393224 | tf_op jit(solution)/shard_map/ppermute | solution.py:453
  51.6 4.6 %collective-permute-start.11 = (f32[8,128]{1,0:T(8,128)S(1)}, f32[8,128]{1,0:T(8,128)S(1)}, u32[]{:S(2)}, u32[]{:S(2)}) collective-permute-start(f32[8,128]{1,0:T(8,128)S(1)} %get-tuple-element.75), channel_id=1, source_target_pairs={{0,8},{8,0},{1,9},{9,1},{2,10},{10,2},{3,11},{11,3},{4,12},{12,4},... | collective-permute-start | bytes 12296 | tf_op jit(solution)/shard_map/ppermute | solution.py:453
  72.4 7.4 %collective-permute-start.12 = (bf16[512,256]{1,0:T(8,128)(2,1)S(1)}, bf16[512,256]{1,0:T(8,128)(2,1)S(1)}, u32[]{:S(2)}, u32[]{:S(2)}) collective-permute-start(bf16[512,256]{1,0:T(8,128)(2,1)S(1)} %get-tuple-element.83), channel_id=1, source_target_pairs={{0,128},{128,0},{1,129},{129,1},{2,130},{130,2},{3,131},{131,3},{4... | collective-permute-start | bytes 786440 | tf_op jit(solution)/shard_map/ppermute | solution.py:453
  138.4 1.3 collective-permute-start.13

commit v5 on v4

--- a/solution.py
+++ b/solution.py
@@ -364,17 +364,20 @@
     pack = (pack_col // 64 == pack_row // 8) & (pack_col // 4 % 8 == pack_row % 8)
     pack = jnp.where(pack, 1.0, 0.0).astype(BF)
     packed = []
-    for start in range(0, HID, tall):
-        span = slice(start, start + tall)
-        xh, half = start // tall // 2, start // tall % 2
+    for xh in range(2):
+        start = xh * CHIP
         for left, right, tile in ((h1, p2_s, 0), (h2, ge_s, 8), (None, x, 10)):
-            units = turned(order, p1_s[:, span]) if left is None else left[span, :]
+            if left is None:
+                spans = [slice(start + half * tall, start + (half + 1) * tall) for half in range(2)]
+                units = jnp.concatenate([turned(order, p1_s[:, span]) for span in spans], axis=0)
+            else:
+                units = left[start : start + CHIP, :]
             value = dot_nn(units, right[:, : right.shape[1] // EMB * EMB])
             for part in range(8):
                 first, second = slot(part // 2, xh * 2 + part % 2)
-                for z in range(4):
-                    line = part * 32 + z * 8
-                    base = second * (4 * TILES * 8) + (half * 2 + z // 2) * TILES * 8
+                for z in range(8):
+                    line = z // 4 * tall + part * 32 + z % 4 * 8
+                    base = second * (4 * TILES * 8) + z // 2 * TILES * 8
                     for k in range(0, value.shape[1] // LANES, 2):
                         two = [
                             value[line : line + 8, at * LANES : (at + 1) * LANES] for at in (k, k + 1)
@@ -383,8 +386,10 @@
                         piece = jnp.concatenate(two, axis=0).astype(BF)
                         grads[first * 2 + z % 2, pl.ds(at, 16), :] = piece
             if tile == 10:
-                value = jnp.where(wanted, dot_nn(units, x[:, EMB:]), 0.0).astype(BF)
-                packed.append(dot_nn(pack, value))
+                value = dot_nn(units, x[:, EMB:])
+                for half in range(2):
+                    mine = jnp.where(wanted, value[half * tall : (half + 1) * tall], 0.0)
+                    packed.append(dot_nn(pack, mine.astype(BF)))
     halves = {}
     for y in range(4):
         for xh in range(2):
@@ -520,7 +525,7 @@
     ahead, back = crossed(unit, 1), crossed(unit, -1)
     s1, h1 = slopes(n1)
     s2, h2 = slopes(n2)
-    ahead, back, s1, h1, s2, h2, late = lax.optimization_barrier((ahead, back, s1, h1, s2, h2, unit))
+    back, ahead, s1, h1, s2, h2, late = lax.optimization_barrier((back, ahead, s1, h1, s2, h2, unit))
     steps = [[ahead, back]]
     for k in range(2, n_z // 2 - 1):
         ahead, back = shifted(ahead, "z", 1), shifted(back, "z", -1)
@@ -531,7 +536,7 @@
     factor = logit * math.log2(math.e)
     expo, part, total = scores(unit, theirs, early, None, False, factor)
     ahead, back, part, total = lax.optimization_barrier((ahead, back, part, total))
-    last = [shifted(ahead[:ROWS], "z", 1), shifted(back[ROWS:], "z", -1)]
+    last = [shifted(back[:ROWS], "z", -1), shifted(ahead[ROWS:], "z", 1)]
     expos = [expo]
     for final, step in enumerate(([ahead, back], last)):
         expo, part, total = scores(unit, theirs, step, (part, total), final == 1, factor)

time: 141 us -> 138 us (0.979)
  waiting for transfers between devices: 24.1 us -> 18.8 us
  blocking collectives: 63.9 us -> 66.9 us
    ppermute x2, waiting for transfers between devices: 7.36 us -> 4.31 us  [crossed(): return lax.ppermute(value, ('z', 'c'), list(enumerate(hop)))]
    all_to_all x1, blocking collectives: 13.8 us -> 16.8 us  [body(): sums = lax.all_to_all(everyone, ('xh', 'z'), 0, 0)]
    ppermute x12, waiting for transfers between devices: 16.7 us -> 14.5 us  [shifted(): lax.ppermute(value, axis, [(k, (k + shift) % count) for k in range(count)])]
  transfers between devices with their start and end apart: 14 -> 14, of which waited for: 11 -> 9; matrix products, arithmetic and copies ran while one was open for 0% -> 0% of each run, Pallas kernels for 6% -> 6%
where the time goes in v5:
time: 138 us
  blocking collectives  66.9 us (48%)
  Pallas kernels  28.3 us (21%)
  starting transfers between devices  23.4 us (17%)
  waiting for transfers between devices  18.8 us (14%)
    all_to_all x1, blocking collectives, body(): grads = lax.all_to_all(grads, axes, 0, 0, axis_index_groups=near)  25.9 us
    all_to_all x1, blocking collectives, body(): grads = lax.all_to_all(grads, axes, 0, 0, axis_index_groups=far)  24.2 us
    ppermute x12, starting transfers between devices, shifted(): lax.ppermute(value, axis, [(k, (k + shift) % count) for k in range(count)])  19.1 us
    all_to_all x1, blocking collectives, body(): sums = lax.all_to_all(everyone, ('xh', 'z'), 0, 0)  16.8 us
    ppermute x12, waiting for transfers between devices, shifted(): lax.ppermute(value, axis, [(k, (k + shift) % count) for k in range(count)])  14.5 us
    pallas_call x1, Pallas kernels, body(): call(functools.partial(backward_kernel, coef), [shape((8, 16 * TILES * 8...  7.04 us
    pallas_call x3, Pallas kernels, scores(): return call(kernel, outs, [VMEM] * len(args), cost=cost)(*args)  5.74 us
    pallas_call x1, Pallas kernels, body(): call(forward_kernel, [shape((CHIP, WIDE), BF), shape((CHIP, HID), F32), s...  5.53 us
  transfers between devices with their start and end apart: 14, of which 9 were waited for; matrix products, arithmetic and copies ran while one was open for 0% of the time, Pallas kernels for 6%

profile of v5, /device:TPU:1, one launch (start us, length us, event | category | flops | bytes accessed | tf_op | source)
XLA Modules:
  0.0 138.2 jit_solution(11374194586357888920)
XLA Ops:
  0.7 2.0 %shard_map.170 = (bf16[256,384]{1,0:T(8,128)(2,1)S(1)}, bf16[256,384]{1,0:T(8,128)(2,1)S(1)}) custom-call(s32[4]{0:T(128)S(1)} %pad_add_fusion.place, s32[1,256]{1,0:T(1,128)} %replay.1, s32[1,256]{1,0:T(1,128)} %offset.1, bf16[320,256]{1,0:T(8,128)(2,1)} %bitcast.11, bf16[16,320]{1,0:T(8,128)(2,1)} %bitcast.12), custom_call_target="tpu_custom_call" | custom-call | tf_op jit(solution)/shard_map/pallas_call | solution.py:487
  2.7 3.3 %collective-permute-start = (bf16[256,384]{1,0:T(8,128)(2,1)S(1)}, bf16[256,384]{1,0:T(8,128)(2,1)S(1)}, u32[]{:S(2)}, u32[]{:S(2)}) collective-permute-start(bf16[256,384]{1,0:T(8,128)(2,1)S(1)} %get-tuple-element.56), channel_id=1, source_target_pairs={{0,8},{8,0},{1,9},{9,1},{2,10},{10,2},{3,11},{11,3},{4,12},{12,4},... | collective-permute-start | bytes 589832 | tf_op jit(solution)/shard_map/ppermute | solution.py:458
  6.0 1.1 collective-permute-done.recv
  7.1 5.5 %shard_map.171 = (bf16[512,384]{1,0:T(8,128)(2,1)S(1)}, f32[512,1024]{1,0:T(8,128)S(1)}, f32[512,1]{1,0:T(8,128)S(1)}, f32[512,1024]{1,0:T(8,128)S(1)}, f32[512,...) custom-call(s32[4]{0:T(128)S(1)} %pad_add_fusion.place, ...), custom_call_target="tpu_custom_call" | custom-call | tf_op jit(solution)/shard_map/pallas_call | solution.py:500
  12.9 4.0 %collective-permute-start.1 = (bf16[512,256]{1,0:T(8,128)(2,1)S(1)}, bf16[512,256]{1,0:T(8,128)(2,1)S(1)}, u32[]{:S(2)}, u32[]{:S(2)}) collective-permute-start(bf16[512,256]{1,0:T(8,128)(2,1)S(1)} %get-tuple-element.64.refs_0_.ours), channel_id=1, source_target_pairs={{0,120},{8,112},{16,8},{24,0},{32,24},{40,16},{48,40},{56,32},{64,... | collective-permute-start | bytes 786440 | tf_op jit(solution)/shard_map/ppermute | solution.py:523
  16.9 0.9 shard_map.172
  17.9 1.0 shard_map.173
  18.8 4.3 %collective-permute-done.2.refs_3_.refs_4_ = bf16[512,256]{1,0:T(8,128)(2,1)S(1)} collective-permute-done((bf16[512,256]{1,0:T(8,128)(2,1)S(1)}, bf16[512,256]{1,0:T(8,128)(2,1)S(1)}, u32[]{:S(2)}, u32[]{:S(2)}) %collective-permute-start.2) | collective-permute-done | bytes 262176 | tf_op jit(solution)/shard_map/ppermute | solution.py:523
  23.1 3.0 %collective-permute-start.6 = (bf16[512,256]{1,0:T(8,128)(2,1)S(1)}, bf16[512,256]{1,0:T(8,128)(2,1)S(1)}, u32[]{:S(2)}, u32[]{:S(2)}) collective-permute-start(bf16[512,256]{1,0:T(8,128)(2,1)S(1)} %collective-permute-done.1.refs_4_.refs_5_), channel_id=1, source_target_pairs={{0,112},{16,0},{32,16},{48,32},{64,48},{80,64},{96,80},{112,96},{1... | collective-permute-start | bytes 786440 | tf_op jit(solution)/shard_map/ppermute | solution.py:458
  26.8 2.7 %collective-permute-start.3 = (bf16[512,256]{1,0:T(8,128)(2,1)S(1)}, bf16[512,256]{1,0:T(8,128)(2,1)S(1)}, u32[]{:S(2)}, u32[]{:S(2)}) collective-permute-start(bf16[512,256]{1,0:T(8,128)(2,1)S(1)} %get-tuple-element.64.refs_0_.ours), channel_id=1, source_target_pairs={{0,128},{128,0},{1,129},{129,1},{2,130},{130,2},{3,131},{131,3},{4... | collective-permute-start | bytes 786440 | tf_op jit(solution)/shard_map/ppermute | solution.py:458
  29.5 3.0 %collective-permute-done.4.refs_5_.refs_6_ = bf16[512,256]{1,0:T(8,128)(2,1)S(1)} collective-permute-done((bf16[512,256]{1,0:T(8,128)(2,1)S(1)}, bf16[512,256]{1,0:T(8,128)(2,1)S(1)}, u32[]{:S(2)}, u32[]{:S(2)}) %collective-permute-start.4) | collective-permute-done | bytes 262176 | tf_op jit(solution)/shard_map/ppermute | solution.py:458
  32.5 2.7 %collective-permute-start.7 = (bf16[512,256]{1,0:T(8,128)(2,1)S(1)}, bf16[512,256]{1,0:T(8,128)(2,1)S(1)}, u32[]{:S(2)}, u32[]{:S(2)}) collective-permute-start(bf16[512,256]{1,0:T(8,128)(2,1)S(1)} %collective-permute-done.6.refs_6_.refs_7_), channel_id=1, source_target_pairs={{0,112},{16,0},{32,16},{48,32},{64,48},{80,64},{96,80},{112,96},{1... | collective-permute-start | bytes 786440 | tf_op jit(solution)/shard_map/ppermute | solution.py:458
  35.2 1.0 collective-permute-done.3.refs_1_
  36.2 3.3 %shard_map.174 = (bf16[1024,2560]{1,0:T(8,128)(2,1)S(1)}, f32[1024,128]{1,0:T(8,128)S(1)}, f32[1024,256]{1,0:T(8,128)S(1)}) custom-call(bf16[512,256]{1,0:T(8,128)(2,1)S(1)} %get-tuple-element.64.refs_0_.ours, bf16[512,256]{1,0:T(8,128)(2,1)S(1)} %collective-permute-done.3.refs_1_, bf16[512,256]{1,0:T(8,128)(2,1)S(1)} %collective-permute-done.8.refs_2_.refs_3_.other, ...), custom_call_target="tpu_custom_call" | custom-call | flops 2684354560 | bytes 6291456 | tf_op jit(solution)/shard_map/pallas_call | solution.py:207
  39.5 1.1 collective-permute-done.5.refs_2_.refs_8_
  40.7 0.7 collective-permute-start.10
  41.4 2.1 %collective-permute-start.9 = (bf16[256,256]{1,0:T(8,128)(2,1)S(1)}, bf16[256,256]{1,0:T(8,128)(2,1)S(1)}, u32[]{:S(2)}, u32[]{:S(2)}) collective-permute-start(bf16[256,256]{1,0:T(8,128)(2,1)S(1)} %slice.6), channel_id=1, source_target_pairs={{0,112},{16,0},{32,16},{48,32},{64,48},{80,64},{96,80},{112,96},{1... | collective-permute-start | bytes 393224 | tf_op jit(solution)/shard_map/ppermute | solution.py:458
  43.5 1.4 %shard_map.175 = (bf16[1024,1024]{1,0:T(8,128)(2,1)S(1)}, f32[1024,128]{1,0:T(8,128)S(1)}, f32[1024,256]{1,0:T(8,128)S(1)}) custom-call(bf16[512,256]{1,0:T(8,128)(2,1)S(1)} %get-tuple-element.64.refs_0_.ours, bf16[512,256]{1,0:T(8,128)(2,1)S(1)} %collective-permute-done.3.refs_1_, bf16[512,256]{1,0:T(8,128)(2,1)S(1)} %collective-permute-done.5.refs_2_.refs_8_, ...), custom_call_target="tpu_custom_call" | custom-call | flops 1073741824 | bytes 3145728 | tf_op jit(solution)/shard_map/pallas_call | solution.py:207
  44.9 0.9 collective-permute-done.10.refs_3_.refs_11_
  45.8 1.0 shard_map.176
  46.9 3.0 %collective-permute-start.11 = (f32[8,128]{1,0:T(8,128)S(1)}, f32[8,128]{1,0:T(8,128)S(1)}, u32[]{:S(2)}, u32[]{:S(2)}) collective-permute-start(f32[8,128]{1,0:T(8,128)S(1)} %get-tuple-element.75), channel_id=1, source_target_pairs={{0,8},{8,0},{1,9},{9,1},{2,10},{10,2},{3,11},{11,3},{4,12},{12,4},... | collective-permute-start | bytes 12296 | tf_op jit(solution)/shard_map/ppermute | solution.py:458
  49.9 0.8 collective-permute-done.11
  50.7 16.8 %all_to_all.15.sums = f32[16,16,128]{2,1,0:T(8,128)S(1)} all-to-all(f32[16,16,128]{2,1,0:T(8,128)S(1)} %broadcast_in_dim.2), channel_id=1, replica_groups=mesh['xh'=2,'z'=8,'c'=2,'y'=4,'xl'=2] {'xh','z'}, dimensions={0} | all-to-all | bytes 262144 | tf_op jit(solution)/shard_map/all_to_all | solution.py:547
  67.6 2.5 %shard_map.177 = (bf16[512,256]{1,0:T(8,128)(2,1)S(1)}, bf16[4096,256]{1,0:T(8,128)(2,1)S(1)}, f32[128,128]{1,0:T(8,128)S(1)}, f32[1,256]{1,0:T(1,128)}) custom-call(s32[4]{0:T(128)S(1)} %pad_add_fusion.place, f32[16,16,128]{2,1,0:T(8,128)S(1)} %all_to_all.15.sums, f32[1024,256]{1,0:T(8,128)S(1)} %get-tuple-element.76.total, ...), custom_call_target="tpu_custom_call" | custom-call | tf_op jit(solution)/shard_map/pallas_call | solution.py:548
  70.0 0.8 collective-permute-start.12
  70.9 1.2 shard_map.178.own
  72.1 5.3 %collective-permute-done.12.recv = bf16[512,256]{1,0:T(8,128)(2,1)S(1)} collective-permute-done((bf16[512,256]{1,0:T(8,128)(2,1)S(1)}, bf16[512,256]{1,0:T(8,128)(2,1)S(1)}, u32[]{:S(2)}, u32[]{:S(2)}) %collective-permute-start.12) | collective-permute-done | bytes 262176 | tf_op jit(solution)/shard_map/ppermute | solution.py:458
  77.4 7.0 %shard_map.179 = bf16[8,1568,128]{2,1,0:T(8,128)(2,1)S(1)} custom-call(s32[4]{0:T(128)S(1)} %pad_add_fusion.place, f32[512,256]{1,0:T(8,128)S(1)} %shard_map.178.own, bf16[512,256]{1,0:T(8,128)(2,1)S(1)} %collective-permute-done.12.recv, bf16[512,256]{1,0:T(8,128)(2,1)S(1)} %collective-permute-done.8.refs_2_.refs_3_.other, ...), custom_call_target="tpu_custom_call" | custom-call | tf_op jit(solution)/shard_map/pallas_call | solution.py:570
  84.5 25.9 %all_to_all.16.parts = bf16[8,1568,128]{2,1,0:T(8,128)(2,1)S(1)} all-to-all(bf16[8,1568,128]{2,1,0:T(8,128)(2,1)S(1)} %shard_map.179), channel_id=1, replica_groups={{0,16,2,18,4,20,6,22},{32,48,34,50,36,52,38,54},{64,80,66,82,68,84,70,8..., dimensions={0} | all-to-all | bytes 6422528 | tf_op jit(solution)/shard_map/all_to_all | solution.py:605
  110.8 24.2 %all_to_all.17.parts = bf16[16,112,128]{2,1,0:T(8,128)(2,1)S(1)} all-to-all(bf16[16,112,128]{2,1,0:T(8,128)(2,1)S(1)} %shard_map.180), channel_id=1, replica_groups={{0,32,64,96,1,33,65,97,128,160,192,224,129,161,193,225},{16,48,80,112,1..., dimensions={0} | all-to-all | bytes 917504 | tf_op jit(solution)/shard_map/all_to_all | solution.py:607
  135.7 1.2 collective-permute-done.13.recv
  136.9 1.3 shard_map.182
  (17 shorter events, 2.1 us)
Async XLA Ops:
  2.7 4.4 %collective-permute-start = (bf16[256,384]{1,0:T(8,128)(2,1)S(1)}, bf16[256,384]{1,0:T(8,128)(2,1)S(1)}, u32[]{:S(2)}, u32[]{:S(2)}) collective-permute-start(bf16[256,384]{1,0:T(8,128)(2,1)S(1)} %get-tuple-element.56), channel_id=1, source_target_pairs={{0,8},{8,0},{1,9},{9,1},{2,10},{10,2},{3,11},{11,3},{4,12},{12,4},... | collective-permute-start | bytes 589832 | tf_op jit(solution)/shard_map/ppermute | solution.py:458
  12.6 10.5 %collective-permute-start.2 = (bf16[512,256]{1,0:T(8,128)(2,1)S(1)}, bf16[512,256]{1,0:T(8,128)(2,1)S(1)}, u32[]{:S(2)}, u32[]{:S(2)}) collective-permute-start(bf16[512,256]{1,0:T(8,128)(2,1)S(1)} %get-tuple-element.64.refs_0_.ours), channel_id=1, source_target_pairs={{0,24},{8,16},{16,40},{24,32},{32,56},{40,48},{48,72},{56,64},{64,... | collective-permute-start | bytes 786440 | tf_op jit(solution)/shard_map/ppermute | solution.py:523
  12.9 10.3 %collective-permute-start.1 = (bf16[512,256]{1,0:T(8,128)(2,1)S(1)}, bf16[512,256]{1,0:T(8,128)(2,1)S(1)}, u32[]{:S(2)}, u32[]{:S(2)}) collective-permute-start(bf16[512,256]{1,0:T(8,128)(2,1)S(1)} %get-tuple-element.64.refs_0_.ours), channel_id=1, source_target_pairs={{0,120},{8,112},{16,8},{24,0},{32,24},{40,16},{48,40},{56,32},{64,... | collective-permute-start | bytes 786440 | tf_op jit(solution)/shard_map/ppermute | solution.py:523
  23.1 9.4 %collective-permute-start.4 = (bf16[512,256]{1,0:T(8,128)(2,1)S(1)}, bf16[512,256]{1,0:T(8,128)(2,1)S(1)}, u32[]{:S(2)}, u32[]{:S(2)}) collective-permute-start(bf16[512,256]{1,0:T(8,128)(2,1)S(1)} %collective-permute-done.2.refs_3_.refs_4_), channel_id=1, source_target_pairs={{0,16},{16,32},{32,48},{48,64},{64,80},{80,96},{96,112},{112,0},{1... | collective-permute-start | bytes 786440 | tf_op jit(solution)/shard_map/ppermute | solution.py:458
  23.1 9.4 %collective-permute-start.6 = (bf16[512,256]{1,0:T(8,128)(2,1)S(1)}, bf16[512,256]{1,0:T(8,128)(2,1)S(1)}, u32[]{:S(2)}, u32[]{:S(2)}) collective-permute-start(bf16[512,256]{1,0:T(8,128)(2,1)S(1)} %collective-permute-done.1.refs_4_.refs_5_), channel_id=1, source_target_pairs={{0,112},{16,0},{32,16},{48,32},{64,48},{80,64},{96,80},{112,96},{1... | collective-permute-start | bytes 786440 | tf_op jit(solution)/shard_map/ppermute | solution.py:458
  26.2 9.1 %collective-permute-start.8 = (bf16[512,256]{1,0:T(8,128)(2,1)S(1)}, bf16[512,256]{1,0:T(8,128)(2,1)S(1)}, u32[]{:S(2)}, u32[]{:S(2)}) collective-permute-start(bf16[512,256]{1,0:T(8,128)(2,1)S(1)} %get-tuple-element.64.refs_0_.ours), channel_id=1, source_target_pairs={{0,8},{8,0},{1,9},{9,1},{2,10},{10,2},{3,11},{11,3},{4,12},{12,4},... | collective-permute-start | bytes 786440 | tf_op jit(solution)/shard_map/ppermute | solution.py:458
  26.8 9.4 %collective-permute-start.3 = (bf16[512,256]{1,0:T(8,128)(2,1)S(1)}, bf16[512,256]{1,0:T(8,128)(2,1)S(1)}, u32[]{:S(2)}, u32[]{:S(2)}) collective-permute-start(bf16[512,256]{1,0:T(8,128)(2,1)S(1)} %get-tuple-element.64.refs_0_.ours), channel_id=1, source_target_pairs={{0,128},{128,0},{1,129},{129,1},{2,130},{130,2},{3,131},{131,3},{4... | collective-permute-start | bytes 786440 | tf_op jit(solution)/shard_map/ppermute | solution.py:458
  32.5 8.1 %collective-permute-start.5 = (bf16[512,256]{1,0:T(8,128)(2,1)S(1)}, bf16[512,256]{1,0:T(8,128)(2,1)S(1)}, u32[]{:S(2)}, u32[]{:S(2)}) collective-permute-start(bf16[512,256]{1,0:T(8,128)(2,1)S(1)} %collective-permute-done.4.refs_5_.refs_6_), channel_id=1, source_target_pairs={{0,16},{16,32},{32,48},{48,64},{64,80},{80,96},{96,112},{112,0},{1... | collective-permute-start | bytes 786440 | tf_op jit(solution)/shard_map/ppermute | solution.py:458
  32.5 8.1 %collective-permute-start.7 = (bf16[512,256]{1,0:T(8,128)(2,1)S(1)}, bf16[512,256]{1,0:T(8,128)(2,1)S(1)}, u32[]{:S(2)}, u32[]{:S(2)}) collective-permute-start(bf16[512,256]{1,0:T(8,128)(2,1)S(1)} %collective-permute-done.6.refs_6_.refs_7_), channel_id=1, source_target_pairs={{0,112},{16,0},{32,16},{48,32},{64,48},{80,64},{96,80},{112,96},{1... | collective-permute-start | bytes 786440 | tf_op jit(solution)/shard_map/ppermute | solution.py:458
  40.7 5.1 %collective-permute-start.10 = (bf16[256,256]{1,0:T(8,128)(2,1)S(1)}, bf16[256,256]{1,0:T(8,128)(2,1)S(1)}, u32[]{:S(2)}, u32[]{:S(2)}) collective-permute-start(bf16[256,256]{1,0:T(8,128)(2,1)S(1)} %slice.7), channel_id=1, source_target_pairs={{0,16},{16,32},{32,48},{48,64},{64,80},{80,96},{96,112},{112,0},{1... | collective-permute-start | bytes 393224 | tf_op jit(solution)/shard_map/ppermute | solution.py:458
  41.4 4.4 %collective-permute-start.9 = (bf16[256,256]{1,0:T(8,128)(2,1)S(1)}, bf16[256,256]{1,0:T(8,128)(2,1)S(1)}, u32[]{:S(2)}, u32[]{:S(2)}) collective-permute-start(bf16[256,256]{1,0:T(8,128)(2,1)S(1)} %slice.6), channel_id=1, source_target_pairs={{0,112},{16,0},{32,16},{48,32},{64,48},{80,64},{96,80},{112,96},{1... | collective-permute-start | bytes 393224 | tf_op jit(solution)/shard_map/ppermute | solution.py:458
  46.9 3.8 %collective-permute-start.11 = (f32[8,128]{1,0:T(8,128)S(1)}, f32[8,128]{1,0:T(8,128)S(1)}, u32[]{:S(2)}, u32[]{:S(2)}) collective-permute-start(f32[8,128]{1,0:T(8,128)S(1)} %get-tuple-element.75), channel_id=1, source_target_pairs={{0,8},{8,0},{1,9},{9,1},{2,10},{10,2},{3,11},{11,3},{4,12},{12,4},... | collective-permute-start | bytes 12296 | tf_op jit(solution)/shard_map/ppermute | solution.py:458
  70.0 7.4 %collective-permute-start.12 = (bf16[512,256]{1,0:T(8,128)(2,1)S(1)}, bf16[512,256]{1,0:T(8,128)(2,1)S(1)}, u32[]{:S(2)}, u32[]{:S(2)}) collective-permute-start(bf16[512,256]{1,0:T(8,128)(2,1)S(1)} %get-tuple-element.83), channel_id=1, source_target_pairs={{0,128},{128,0},{1,129},{129,1},{2,130},{130,2},{3,131},{131,3},{4... | collective-permute-start | bytes 786440 | tf_op jit(solution)/shard_map/ppermute | solution.py:458
  135.6 1.3 collective-permute-start.13

commit v6 on v5

--- a/solution.py
+++ b/solution.py
@@ -125,8 +125,8 @@
     other = pl.multiple_of((1 - role) * ROWS, ROWS)
     x[pl.ds(own, ROWS), :] = keep[...]
     x[pl.ds(other, ROWS), :] = recv[...]
-    for start in range(0, CHIP, ROWS):
-        rows = pl.ds(start, ROWS)
+    for start in range(0, CHIP, CHIP):
+        rows = pl.ds(start, CHIP)
 
         def norm(values, normed, factor):
             center = values - jnp.mean(values, axis=-1, keepdims=True)
@@ -153,7 +153,14 @@
     return jnp.sum(values.T, axis=0, keepdims=True)
 
 
-def score_kernel(n_blocks, first, last, factor, *refs):
+def ring_order(n_z):
+    order = [0, n_z - 1, 1]
+    for k in range(2, n_z // 2):
+        order += [n_z - k, k]
+    return order + [n_z // 2]
+
+
+def score_kernel(n_blocks, first, last, factor, place, *refs):
     refs = list(refs)
     ours, theirs = refs[:2]
     blocks = refs[2 : 2 + n_blocks]
@@ -161,7 +168,11 @@
     if not first:
         old_sum, old_total = refs[:2]
         refs = refs[2:]
-    expo, part, total = refs[:3]
+    if last:
+        old_columns = refs[:-4]
+        refs = refs[-4:]
+    expo, part, total, columns = refs
+    down = [None] * n_blocks
     for start in range(0, 2 * CHIP, ROWS):
         source = ours if start < CHIP else theirs
         q = source[pl.ds(start % CHIP, ROWS), :]
@@ -169,13 +180,15 @@
         acc = None if first else old_total[rows, :]
         sums = None if first else old_sum[rows, :]
         at = 0
-        for block in blocks:
+        for n, block in enumerate(blocks):
             t = block[...]
             width = t.shape[0]
             e = jnp.exp2(dot_nt(q, t) * factor)
             for lane in range(0, width, LANES):
                 piece = e[:, lane : lane + LANES]
                 sums = piece if sums is None else sums + piece
+            fold = jnp.sum(e.reshape(ROWS // 8, 8, width), axis=0)
+            down[n] = fold if down[n] is None else down[n] + fold
             e16 = e.astype(BF)
             expo[rows, at : at + width] = e16
             add = dot_nn(e16, t)
@@ -188,23 +201,39 @@
                 part[line : line + 1, :] = to_lanes(sums[k * LANES : (k + 1) * LANES, :])
         else:
             part[rows, :] = sums
-
-
-def scores(ours, theirs, blocks, prev, last, factor):
+    lines = []
+    for fold in down:
+        whole = jnp.sum(fold, axis=0, keepdims=True)
+        lines += [whole[:, k : k + LANES] for k in range(0, whole.shape[1], LANES)]
+    if last:
+        n_z = columns.shape[0]
+        held = [ref[k : k + 4, :] for ref in old_columns for k in range(0, ref.shape[0], 4)]
+        held.append(jnp.concatenate(lines, axis=0))
+        for shift, value in zip(ring_order(n_z), held):
+            columns[lax.rem(place[1] + shift, n_z)] = value
+    else:
+        for k, line in enumerate(lines):
+            columns[k : k + 1, :] = line
+
+
+def scores(place, ours, theirs, blocks, prev, held, factor):
     width = sum(b.shape[0] for b in blocks)
+    last = held is not None
+    lines = (2 * sum(c.shape[0] for c in held) + 2 * width // LANES) // 8 if last else width // LANES
     outs = [
         shape((2 * CHIP, width), BF),
         shape((8, LANES) if last else (2 * CHIP, LANES), F32),
         shape((2 * CHIP, EMB), F32),
+        shape((lines, 4, LANES) if last else (lines, LANES), F32),
     ]
-    args = [ours, theirs, *blocks] + list(prev or ())
+    args = [place, ours, theirs, *blocks] + list(prev or ()) + list(held or ())
     kernel = functools.partial(score_kernel, len(blocks), prev is None, last, factor)
     cost = pl.CostEstimate(
         flops=4 * 2 * CHIP * width * EMB,
         bytes_accessed=2 * 2 * CHIP * width + 4 * 2 * CHIP * EMB,
         transcendentals=2 * CHIP * width,
     )
-    return call(kernel, outs, [VMEM] * len(args), cost=cost)(*args)
+    return call(kernel, outs, [SMEM] + [VMEM] * (len(args) - 1), cost=cost)(*args)
 
 
 def mix_rows(expos, scaled, total, columns, line, start, write):
@@ -221,29 +250,24 @@
         write(start + k * LANES, value + acc[k * LANES : (k + 1) * LANES, :])
 
 
-def send_kernel(n_z, logit, place, sums, total, ours, *refs):
+def send_kernel(n_z, logit, place, sums, part, partner, total, ours, *refs):
     n_exp = 3
     expos = refs[:n_exp]
     blocks = refs[n_exp : n_exp + n_z + 1]
     send, scaled, across, loss = refs[n_exp + n_z + 1 : n_exp + n_z + 5]
-    lines = refs[n_exp + n_z + 5]
-    xh, z, role = place[0], place[1], place[2]
-
-    def full(x_at, z_at, side):
-        mine = sums[x_at * n_z + z_at]
-        partner = sums[(1 - x_at) * n_z + z_at]
-        return mine[side * 8 : side * 8 + 4] + partner[side * 8 + 4 : side * 8 + 8]
-
-    order = [0]
-    for k in range(1, n_z // 2):
-        order += [n_z - k, k]
-    order.append(n_z // 2)
+    lines, whole = refs[n_exp + n_z + 5 :]
+    z, role = place[1], place[2]
+    column = sums[0]
+    for k in range(1, n_z):
+        column = column + sums[k]
+    whole[...] = column
+    mine = part[:4, :] + partner[4:, :]
+    theirs = part[4:, :] + partner[:4, :]
     lines[...] = jnp.ones((LANES, LANES), F32)
-    for k, shift in enumerate(order):
-        lines[4 * k : 4 * k + 4, :] = 1.0 / full(xh, lax.rem(z + shift, n_z), 1)
-    mine = full(xh, z, 0)
+    for k, shift in enumerate(ring_order(n_z)):
+        lines[4 * k : 4 * k + 4, :] = 1.0 / whole[lax.rem(z + shift, n_z)]
     lines[4 * n_z : 4 * n_z + 4, :] = 1.0 / mine
-    lines[4 * n_z + 4 : 4 * n_z + 8, :] = 1.0 / full(1 - xh, z, 0)
+    lines[4 * n_z + 4 : 4 * n_z + 8, :] = 1.0 / theirs
     columns = lines[...].T
     across[...] = columns
 
@@ -261,7 +285,7 @@
     for start in range(CHIP, 2 * CHIP, ROWS):
         mix_rows(expos, scaled, total, columns, 4 * n_z, start, write)
 
-    logs = jnp.log(mine) + jnp.log(full(xh, z, 1))
+    logs = jnp.log(mine) + jnp.log(whole[z])
     logs = jnp.where(role == 0, logs[:2], logs[2:])
     at = pl.multiple_of(role * ROWS, ROWS)
     both = ours[pl.ds(at, ROWS), :].astype(F32) * blocks[0][pl.ds(at, ROWS), :].astype(F32)
@@ -324,8 +348,8 @@
     role = place[2]
     pairs = [((sa_out, goal_out), w_out), ((sa_mid, goal_mid), w_mid)]
     by_role(role, pairs, sems)
-    for start in range(0, CHIP, ROWS):
-        rows = pl.ds(start, ROWS)
+    for start in range(0, CHIP, CHIP):
+        rows = pl.ds(start, CHIP)
         grad = coef * (
             own[rows, :] + recv[rows, :].astype(F32) - 2.0 * other[rows, :].astype(F32)
         )
@@ -534,17 +558,19 @@
     early = [other] + [block for step in steps for block in step]
     ahead, back = shifted(ahead, "z", 1), shifted(back, "z", -1)
     factor = logit * math.log2(math.e)
-    expo, part, total = scores(unit, theirs, early, None, False, factor)
+    expo, part, total, columns = scores(place, unit, theirs, early, None, None, factor)
+    held = [columns]
     ahead, back, part, total = lax.optimization_barrier((ahead, back, part, total))
     last = [shifted(back[:ROWS], "z", -1), shifted(ahead[ROWS:], "z", 1)]
     expos = [expo]
-    for final, step in enumerate(([ahead, back], last)):
-        expo, part, total = scores(unit, theirs, step, (part, total), final == 1, factor)
-        expos.append(expo)
+    expo, part, total, columns = scores(place, unit, theirs, [ahead, back], (part, total), None, factor)
+    expos.append(expo)
+    held.append(columns)
+    expo, part, total, columns = scores(place, unit, theirs, last, (part, total), held, factor)
+    expos.append(expo)
     blocks = early + [ahead, back] + last
-    both = jnp.concatenate([part, shifted(part, "c", 1)], axis=0)
-    everyone = jnp.broadcast_to(both[None], (2 * n_z, 16, LANES))
-    sums = lax.all_to_all(everyone, ("xh", "z"), 0, 0)
+    partner = shifted(part, "xh", 1)
+    sums = lax.all_to_all(jnp.broadcast_to(columns[None], (n_z, n_z, 4, LANES)), "z", 0, 0)
     partial, scaled, across, loss = call(
         functools.partial(send_kernel, n_z, logit),
         [
@@ -553,9 +579,9 @@
             shape((LANES, LANES), F32),
             shape((1, ROWS), F32),
         ],
-        [SMEM] + [VMEM] * (3 + len(expos) + len(blocks)),
-        scratch=[pltpu.VMEM((LANES, LANES), F32)],
-    )(place, sums, total, unit, *expos, *blocks)
+        [SMEM] + [VMEM] * (5 + len(expos) + len(blocks)),
+        scratch=[pltpu.VMEM((LANES, LANES), F32), pltpu.VMEM((n_z, 4, LANES), F32)],
+    )(place, sums, part, partner, total, unit, *expos, *blocks)
     added = shifted(partial, "xh", 1)
     own = call(
         functools.partial(own_kernel, n_z),

time: 138 us -> 156 us (1.13)
  local copies, waits for them, and re-layouts: 0.03 us -> 29 us
  blocking collectives: 66.9 us -> 47.6 us
  starting transfers between devices: 23.4 us -> 33.5 us
  waiting for transfers between devices: 18.8 us -> 14.8 us
    unnamed x0 -> x102, local copies, waits for them, and re-layouts: none -> 28.3 us
    all_to_all x1 -> x0, blocking collectives: 16.8 us -> none  [body(): sums = lax.all_to_all(everyone, ('xh', 'z'), 0, 0)]
    all_to_all x0 -> x1, starting transfers between devices: none -> 5.63 us  [body(): lax.all_to_all(jnp.broadcast_to(columns[None], (n_z, n_z, 4, LANES)), 'z'...]
    ppermute x12, waiting for transfers between devices: 14.5 us -> 9.75 us  [shifted(): lax.ppermute(value, axis, [(k, (k + shift) % count) for k in range(count)])]
    ppermute x12, starting transfers between devices: 19.1 us -> 23.8 us  [shifted(): lax.ppermute(value, axis, [(k, (k + shift) % count) for k in range(count)])]
    all_to_all x0 -> x1, waiting for transfers between devices: none -> 3.97 us  [body(): lax.all_to_all(jnp.broadcast_to(columns[None], (n_z, n_z, 4, LANES)), 'z'...]
    all_to_all x1, blocking collectives: 24.2 us -> 20.5 us  [body(): grads = lax.all_to_all(grads, axes, 0, 0, axis_index_groups=far)]
    ppermute x2, waiting for transfers between devices: 4.31 us -> 1.1 us  [crossed(): return lax.ppermute(value, ('z', 'c'), list(enumerate(hop)))]
  transfers between devices with their start and end apart: 14 -> 15, of which waited for: 9 -> 8; matrix products, arithmetic and copies ran while one was open for 0% -> 0% of each run, Pallas kernels for 6% -> 6%
where the time goes in v6:
time: 156 us
  blocking collectives  47.6 us (31%)
  starting transfers between devices  33.5 us (21%)
  Pallas kernels  29.4 us (19%)
  local copies, waits for them, and re-layouts  29 us (19%)
  waiting for transfers between devices  14.8 us (9%)
    unnamed x102, local copies, waits for them, and re-layouts  28.3 us
    all_to_all x1, blocking collectives, body(): grads = lax.all_to_all(grads, axes, 0, 0, axis_index_groups=near)  27.1 us
    ppermute x12, starting transfers between devices, shifted(): lax.ppermute(value, axis, [(k, (k + shift) % count) for k in range(count)])  23.8 us
    all_to_all x1, blocking collectives, body(): grads = lax.all_to_all(grads, axes, 0, 0, axis_index_groups=far)  20.5 us
    ppermute x12, waiting for transfers between devices, shifted(): lax.ppermute(value, axis, [(k, (k + shift) % count) for k in range(count)])  9.75 us
    pallas_call x3, Pallas kernels, scores(): call(kernel, outs, [SMEM] + [VMEM] * (len(args) - 1), cost=cost)(*args)  7.3 us
    pallas_call x1, Pallas kernels, body(): call(functools.partial(backward_kernel, coef), [shape((8, 16 * TILES * 8...  6.73 us
    all_to_all x1, starting transfers between devices, body(): lax.all_to_all(jnp.broadcast_to(columns[None], (n_z, n_z, 4, LANES)), 'z'...  5.63 us
  transfers between devices with their start and end apart: 15, of which 8 were waited for; matrix products, arithmetic and copies ran while one was open for 0% of the time, Pallas kernels for 6%

profile of v6, /device:TPU:1, one launch (start us, length us, event | category | flops | bytes accessed | tf_op | source)
XLA Modules:
  0.0 155.5 jit_solution(1526362933258088212)
XLA Ops:
  0.7 2.0 %shard_map.170 = (bf16[256,384]{1,0:T(8,128)(2,1)S(1)}, bf16[256,384]{1,0:T(8,128)(2,1)S(1)}) custom-call(s32[4]{0:T(128)S(1)} %pad_add_fusion.place, s32[1,256]{1,0:T(1,128)} %replay.1, s32[1,256]{1,0:T(1,128)} %offset.1, bf16[320,256]{1,0:T(8,128)(2,1)} %bitcast.13, bf16[16,320]{1,0:T(8,128)(2,1)} %bitcast.14), custom_call_target="tpu_custom_call" | custom-call | tf_op jit(solution)/shard_map/pallas_call | solution.py:511
  2.7 3.3 %collective-permute-start = (bf16[256,384]{1,0:T(8,128)(2,1)S(1)}, bf16[256,384]{1,0:T(8,128)(2,1)S(1)}, u32[]{:S(2)}, u32[]{:S(2)}) collective-permute-start(bf16[256,384]{1,0:T(8,128)(2,1)S(1)} %get-tuple-element.59), channel_id=1, source_target_pairs={{0,8},{8,0},{1,9},{9,1},{2,10},{10,2},{3,11},{11,3},{4,12},{12,4},... | collective-permute-start | bytes 589832 | tf_op jit(solution)/shard_map/ppermute | solution.py:482
  7.1 5.4 %shard_map.171 = (bf16[512,384]{1,0:T(8,128)(2,1)S(1)}, f32[512,1024]{1,0:T(8,128)S(1)}, f32[512,1]{1,0:T(8,128)S(1)}, f32[512,1024]{1,0:T(8,128)S(1)}, f32[512,...) custom-call(s32[4]{0:T(128)S(1)} %pad_add_fusion.place, ...), custom_call_target="tpu_custom_call" | custom-call | tf_op jit(solution)/shard_map/pallas_call | solution.py:524
  16.3 3.9 %collective-permute-start.1 = (bf16[512,256]{1,0:T(8,128)(2,1)S(1)}, bf16[512,256]{1,0:T(8,128)(2,1)S(1)}, u32[]{:S(2)}, u32[]{:S(2)}) collective-permute-start(bf16[512,256]{1,0:T(8,128)(2,1)S(1)} %get-tuple-element.67.refs_0_.ours), channel_id=1, source_target_pairs={{0,120},{8,112},{16,8},{24,0},{32,24},{40,16},{48,40},{56,32},{64,... | collective-permute-start | bytes 786440 | tf_op jit(solution)/shard_map/ppermute | solution.py:547
  23.2 1.3 copy-done.15
  26.7 2.8 %collective-permute-start.6 = (bf16[512,256]{1,0:T(8,128)(2,1)S(1)}, bf16[512,256]{1,0:T(8,128)(2,1)S(1)}, u32[]{:S(2)}, u32[]{:S(2)}) collective-permute-start(bf16[512,256]{1,0:T(8,128)(2,1)S(1)} %collective-permute-done.1.refs_4_.refs_5_), channel_id=1, source_target_pairs={{0,112},{16,0},{32,16},{48,32},{64,48},{80,64},{96,80},{112,96},{1... | collective-permute-start | bytes 786440 | tf_op jit(solution)/shard_map/ppermute | solution.py:482
  30.2 2.7 %collective-permute-start.3 = (bf16[512,256]{1,0:T(8,128)(2,1)S(1)}, bf16[512,256]{1,0:T(8,128)(2,1)S(1)}, u32[]{:S(2)}, u32[]{:S(2)}) collective-permute-start(bf16[512,256]{1,0:T(8,128)(2,1)S(1)} %get-tuple-element.67.refs_0_.ours), channel_id=1, source_target_pairs={{0,128},{128,0},{1,129},{129,1},{2,130},{130,2},{3,131},{131,3},{4... | collective-permute-start | bytes 786440 | tf_op jit(solution)/shard_map/ppermute | solution.py:482
  32.9 3.0 %collective-permute-done.4.refs_5_.refs_6_ = bf16[512,256]{1,0:T(8,128)(2,1)S(1)} collective-permute-done((bf16[512,256]{1,0:T(8,128)(2,1)S(1)}, bf16[512,256]{1,0:T(8,128)(2,1)S(1)}, u32[]{:S(2)}, u32[]{:S(2)}) %collective-permute-start.4) | collective-permute-done | bytes 262176 | tf_op jit(solution)/shard_map/ppermute | solution.py:482
  35.9 2.7 %collective-permute-start.7 = (bf16[512,256]{1,0:T(8,128)(2,1)S(1)}, bf16[512,256]{1,0:T(8,128)(2,1)S(1)}, u32[]{:S(2)}, u32[]{:S(2)}) collective-permute-start(bf16[512,256]{1,0:T(8,128)(2,1)S(1)} %collective-permute-done.6.refs_6_.refs_7_), channel_id=1, source_target_pairs={{0,112},{16,0},{32,16},{48,32},{64,48},{80,64},{96,80},{112,96},{1... | collective-permute-start | bytes 786440 | tf_op jit(solution)/shard_map/ppermute | solution.py:482
  39.6 3.7 %shard_map.174 = (bf16[1024,2560]{1,0:T(8,128)(2,1)S(1)}, f32[1024,128]{1,0:T(8,128)S(1)}, f32[1024,256]{1,0:T(8,128)S(1)}, f32[20,128]{1,0:T(8,128)S(1)}) custom-call(s32[4]{0:T(128)S(1)} %pad_add_fusion.place, bf16[512,256]{1,0:T(8,128)(2,1)S(1)} %get-tuple-element.67.refs_0_.ours, bf16[512,256]{1,0:T(8,128)(2,1)S(1)} %collective-permute-done.3.refs_1_, ...), custom_call_target="tpu_custom_call" | custom-call | flops 2684354560 | bytes 6291456 | tf_op jit(solution)/shard_map/pallas_call | solution.py:236
  43.4 2.3 %copy-done = bf16[1024,2560]{1,0:T(8,128)(2,1)} copy-done((bf16[1024,2560]{1,0:T(8,128)(2,1)}, bf16[1024,2560]{1,0:T(8,128)(2,1)S(1)}, u32[]{:S(2)}) %copy-start) | copy-done | bytes 5242904
  45.9 2.7 %collective-permute-start.9 = (bf16[256,256]{1,0:T(8,128)(2,1)S(1)}, bf16[256,256]{1,0:T(8,128)(2,1)S(1)}, u32[]{:S(2)}, u32[]{:S(2)}) collective-permute-start(bf16[256,256]{1,0:T(8,128)(2,1)S(1)} %slice.6), channel_id=1, source_target_pairs={{0,112},{16,0},{32,16},{48,32},{64,48},{80,64},{96,80},{112,96},{1... | collective-permute-start | bytes 393224 | tf_op jit(solution)/shard_map/ppermute | solution.py:482
  48.6 2.0 %shard_map.175 = (bf16[1024,1024]{1,0:T(8,128)(2,1)S(1)}, f32[1024,128]{1,0:T(8,128)S(1)}, f32[1024,256]{1,0:T(8,128)S(1)}, f32[8,128]{1,0:T(8,128)S(1)}) custom-call(s32[4]{0:T(128)S(1)} %pad_add_fusion.place, bf16[512,256]{1,0:T(8,128)(2,1)S(1)} %get-tuple-element.67.refs_0_.ours, bf16[512,256]{1,0:T(8,128)(2,1)S(1)} %collective-permute-done.3.refs_1_, ...), custom_call_target="tpu_custom_call" | custom-call | flops 1073741824 | bytes 3145728 | tf_op jit(solution)/shard_map/pallas_call | solution.py:236
  50.6 1.3 copy-done.4
  51.9 1.6 %shard_map.176 = (bf16[1024,512]{1,0:T(8,128)(2,1)S(1)}, f32[8,128]{1,0:T(8,128)S(1)}, f32[1024,256]{1,0:T(8,128)S(1)}, f32[8,4,128]{2,1,0:T(4,128)S(1)}) custom-call(s32[4]{0:T(128)S(1)} %pad_add_fusion.place, bf16[512,256]{1,0:T(8,128)(2,1)S(1)} %get-tuple-element.67.refs_0_.ours, bf16[512,256]{1,0:T(8,128)(2,1)S(1)} %collective-permute-done.3.refs_1_, ...), custom_call_target="tpu_custom_call" | custom-call | flops 536870912 | bytes 2097152 | tf_op jit(solution)/shard_map/pallas_call | solution.py:236
  56.9 5.6 %all-to-all-start = ((f32[8,8,4,128]{3,2,1,0:T(4,128)}), f32[8,8,4,128]{3,2,1,0:T(4,128)S(1)}, u32[]{:S(2)}, u32[]{:S(2)}) async-start(f32[8,8,4,128]{3,2,1,0:T(4,128)} %broadcast_in_dim.2), calls=%async_computation | async-start | bytes 262144 | tf_op jit(solution)/shard_map/all_to_all | solution.py:573
  62.5 2.7 %collective-permute-start.11 = (f32[8,128]{1,0:T(8,128)S(1)}, f32[8,128]{1,0:T(8,128)S(1)}, u32[]{:S(2)}, u32[]{:S(2)}) collective-permute-start(f32[8,128]{1,0:T(8,128)S(1)} %get-tuple-element.81.part), channel_id=1, source_target_pairs={{0,128},{128,0},{1,129},{129,1},{2,130},{130,2},{3,131},{131,3},{4... | collective-permute-start | bytes 12296 | tf_op jit(solution)/shard_map/ppermute | solution.py:482
  65.3 1.2 collective-permute-done.11.partner
  66.5 4.0 %all-to-all-done.sums = f32[8,8,4,128]{3,2,1,0:T(4,128)S(1)} async-done(((f32[8,8,4,128]{3,2,1,0:T(4,128)}), f32[8,8,4,128]{3,2,1,0:T(4,128)S(1)}, u32[]{:S(2)}, u32[]{:S(2)}) %all-to-all-start) | async-done | bytes 131104 | tf_op jit(solution)/shard_map/all_to_all | solution.py:573
  70.4 2.5 %copy-done.1 = bf16[1024,2560]{1,0:T(8,128)(2,1)S(1)} copy-done((bf16[1024,2560]{1,0:T(8,128)(2,1)S(1)}, bf16[1024,2560]{1,0:T(8,128)(2,1)}, u32[]{:S(2)}) %copy-start.1) | copy-done | bytes 5242904
  72.9 1.6 %copy-done.5 = bf16[1024,1024]{1,0:T(8,128)(2,1)S(1)} copy-done((bf16[1024,1024]{1,0:T(8,128)(2,1)S(1)}, bf16[1024,1024]{1,0:T(8,128)(2,1)}, u32[]{:S(2)}) %copy-start.5) | copy-done | bytes 2097176
  74.5 1.2 copy-done.8
  75.7 1.2 copy-done.11
  85.4 2.5 %shard_map.177 = (bf16[512,256]{1,0:T(8,128)(2,1)S(1)}, bf16[4096,256]{1,0:T(8,128)(2,1)S(1)}, f32[128,128]{1,0:T(8,128)S(1)}, f32[1,256]{1,0:T(1,128)}) custom-call(s32[4]{0:T(128)S(1)} %pad_add_fusion.place, f32[8,8,4,128]{3,2,1,0:T(4,128)S(1)} %all-to-all-done.sums, f32[8,128]{1,0:T(8,128)S(1)} %get-tuple-element.81.part, ...), custom_call_target="tpu_custom_call" | custom-call | tf_op jit(solution)/shard_map/pallas_call | solution.py:574
  87.9 2.7 %collective-permute-start.12 = (bf16[512,256]{1,0:T(8,128)(2,1)S(1)}, bf16[512,256]{1,0:T(8,128)(2,1)S(1)}, u32[]{:S(2)}, u32[]{:S(2)}) collective-permute-start(bf16[512,256]{1,0:T(8,128)(2,1)S(1)} %get-tuple-element.89), channel_id=1, source_target_pairs={{0,128},{128,0},{1,129},{129,1},{2,130},{130,2},{3,131},{131,3},{4... | collective-permute-start | bytes 786440 | tf_op jit(solution)/shard_map/ppermute | solution.py:482
  90.8 1.2 shard_map.178.own
  92.1 2.6 %collective-permute-done.12.recv = bf16[512,256]{1,0:T(8,128)(2,1)S(1)} collective-permute-done((bf16[512,256]{1,0:T(8,128)(2,1)S(1)}, bf16[512,256]{1,0:T(8,128)(2,1)S(1)}, u32[]{:S(2)}, u32[]{:S(2)}) %collective-permute-start.12) | collective-permute-done | bytes 262176 | tf_op jit(solution)/shard_map/ppermute | solution.py:482
  94.7 6.7 %shard_map.179 = bf16[8,1568,128]{2,1,0:T(8,128)(2,1)S(1)} custom-call(s32[4]{0:T(128)S(1)} %pad_add_fusion.place, f32[512,256]{1,0:T(8,128)S(1)} %shard_map.178.own, bf16[512,256]{1,0:T(8,128)(2,1)S(1)} %collective-permute-done.12.recv, bf16[512,256]{1,0:T(8,128)(2,1)S(1)} %collective-permute-done.8.refs_2_.refs_3_.other, f32[512,256]{1,0:T(8,128)S(1)} %copy-done.28, ...), custom_call_target="tpu_custom_call" | custom-call | tf_op jit(solution)/shard_map/pallas_call | solution.py:596
  101.5 27.1 %all_to_all.15.parts = bf16[8,1568,128]{2,1,0:T(8,128)(2,1)S(1)} all-to-all(bf16[8,1568,128]{2,1,0:T(8,128)(2,1)S(1)} %shard_map.179), channel_id=1, replica_groups={{0,16,2,18,4,20,6,22},{32,48,34,50,36,52,38,54},{64,80,66,82,68,84,70,8..., dimensions={0} | all-to-all | bytes 6422528 | tf_op jit(solution)/shard_map/all_to_all | solution.py:631
  129.0 20.5 %all_to_all.16.parts = bf16[16,112,128]{2,1,0:T(8,128)(2,1)S(1)} all-to-all(bf16[16,112,128]{2,1,0:T(8,128)(2,1)S(1)} %shard_map.180), channel_id=1, replica_groups={{0,32,64,96,1,33,65,97,128,160,192,224,129,161,193,225},{16,48,80,112,1..., dimensions={0} | all-to-all | bytes 917504 | tf_op jit(solution)/shard_map/all_to_all | solution.py:633
  150.1 3.2 %collective-permute-start.13 = (f32[56,128]{1,0:T(8,128)S(1)}, f32[56,128]{1,0:T(8,128)S(1)}, u32[]{:S(2)}, u32[]{:S(2)}) collective-permute-start(f32[56,128]{1,0:T(8,128)S(1)} %get-tuple-element.100), channel_id=1, source_target_pairs={{0,8},{8,0},{1,9},{9,1},{2,10},{10,2},{3,11},{11,3},{4,12},{12,4},... | collective-permute-start | bytes 86024 | tf_op jit(solution)/shard_map/ppermute | solution.py:482
  154.2 1.3 shard_map.182
  (120 shorter events, 25.6 us)
Async XLA Ops:
  2.7 4.4 %collective-permute-start = (bf16[256,384]{1,0:T(8,128)(2,1)S(1)}, bf16[256,384]{1,0:T(8,128)(2,1)S(1)}, u32[]{:S(2)}, u32[]{:S(2)}) collective-permute-start(bf16[256,384]{1,0:T(8,128)(2,1)S(1)} %get-tuple-element.59), channel_id=1, source_target_pairs={{0,8},{8,0},{1,9},{9,1},{2,10},{10,2},{3,11},{11,3},{4,12},{12,4},... | collective-permute-start | bytes 589832 | tf_op jit(solution)/shard_map/ppermute | solution.py:482
  16.2 7.0 %copy-start.2 = (f32[512,1024]{1,0:T(8,128)}, f32[512,1024]{1,0:T(8,128)S(1)}, u32[]{:S(2)}) copy-start(f32[512,1024]{1,0:T(8,128)S(1)} %get-tuple-element.64.normed.n2) | copy-start | bytes 6291460
  16.2 10.4 %collective-permute-start.2 = (bf16[512,256]{1,0:T(8,128)(2,1)S(1)}, bf16[512,256]{1,0:T(8,128)(2,1)S(1)}, u32[]{:S(2)}, u32[]{:S(2)}) collective-permute-start(bf16[512,256]{1,0:T(8,128)(2,1)S(1)} %get-tuple-element.67.refs_0_.ours), channel_id=1, source_target_pairs={{0,24},{8,16},{16,40},{24,32},{32,56},{40,48},{48,72},{56,64},{64,... | collective-permute-start | bytes 786440 | tf_op jit(solution)/shard_map/ppermute | solution.py:547
  16.3 10.3 %collective-permute-start.1 = (bf16[512,256]{1,0:T(8,128)(2,1)S(1)}, bf16[512,256]{1,0:T(8,128)(2,1)S(1)}, u32[]{:S(2)}, u32[]{:S(2)}) collective-permute-start(bf16[512,256]{1,0:T(8,128)(2,1)S(1)} %get-tuple-element.67.refs_0_.ours), channel_id=1, source_target_pairs={{0,120},{8,112},{16,8},{24,0},{32,24},{40,16},{48,40},{56,32},{64,... | collective-permute-start | bytes 786440 | tf_op jit(solution)/shard_map/ppermute | solution.py:547
  22.2 16.4 %copy-start.13 = (f32[512,1024]{1,0:T(8,128)}, f32[512,1024]{1,0:T(8,128)S(1)}, u32[]{:S(2)}) copy-start(f32[512,1024]{1,0:T(8,128)S(1)} %get-tuple-element.93.s1) | copy-start | bytes 6291460
  26.6 16.8 %copy-start.41 = (bf16[512,256]{1,0:T(8,128)(2,1)}, bf16[512,256]{1,0:T(8,128)(2,1)S(1)}, u32[]{:S(2)}) copy-start(bf16[512,256]{1,0:T(8,128)(2,1)S(1)} %collective-permute-done.2.refs_3_.refs_4_) | copy-start | bytes 786436
  26.6 16.8 %copy-start.43 = (bf16[512,256]{1,0:T(8,128)(2,1)}, bf16[512,256]{1,0:T(8,128)(2,1)S(1)}, u32[]{:S(2)}) copy-start(bf16[512,256]{1,0:T(8,128)(2,1)S(1)} %collective-permute-done.1.refs_4_.refs_5_) | copy-start | bytes 786436
  26.6 9.3 %collective-permute-start.4 = (bf16[512,256]{1,0:T(8,128)(2,1)S(1)}, bf16[512,256]{1,0:T(8,128)(2,1)S(1)}, u32[]{:S(2)}, u32[]{:S(2)}) collective-permute-start(bf16[512,256]{1,0:T(8,128)(2,1)S(1)} %collective-permute-done.2.refs_3_.refs_4_), channel_id=1, source_target_pairs={{0,16},{16,32},{32,48},{48,64},{64,80},{80,96},{96,112},{112,0},{1... | collective-permute-start | bytes 786440 | tf_op jit(solution)/shard_map/ppermute | solution.py:482
  26.7 9.2 %collective-permute-start.6 = (bf16[512,256]{1,0:T(8,128)(2,1)S(1)}, bf16[512,256]{1,0:T(8,128)(2,1)S(1)}, u32[]{:S(2)}, u32[]{:S(2)}) collective-permute-start(bf16[512,256]{1,0:T(8,128)(2,1)S(1)} %collective-permute-done.1.refs_4_.refs_5_), channel_id=1, source_target_pairs={{0,112},{16,0},{32,16},{48,32},{64,48},{80,64},{96,80},{112,96},{1... | collective-permute-start | bytes 786440 | tf_op jit(solution)/shard_map/ppermute | solution.py:482
  29.5 9.1 %collective-permute-start.8 = (bf16[512,256]{1,0:T(8,128)(2,1)S(1)}, bf16[512,256]{1,0:T(8,128)(2,1)S(1)}, u32[]{:S(2)}, u32[]{:S(2)}) collective-permute-start(bf16[512,256]{1,0:T(8,128)(2,1)S(1)} %get-tuple-element.67.refs_0_.ours), channel_id=1, source_target_pairs={{0,8},{8,0},{1,9},{9,1},{2,10},{10,2},{3,11},{11,3},{4,12},{12,4},... | collective-permute-start | bytes 786440 | tf_op jit(solution)/shard_map/ppermute | solution.py:482
  30.2 9.4 %collective-permute-start.3 = (bf16[512,256]{1,0:T(8,128)(2,1)S(1)}, bf16[512,256]{1,0:T(8,128)(2,1)S(1)}, u32[]{:S(2)}, u32[]{:S(2)}) collective-permute-start(bf16[512,256]{1,0:T(8,128)(2,1)S(1)} %get-tuple-element.67.refs_0_.ours), channel_id=1, source_target_pairs={{0,128},{128,0},{1,129},{129,1},{2,130},{130,2},{3,131},{131,3},{4... | collective-permute-start | bytes 786440 | tf_op jit(solution)/shard_map/ppermute | solution.py:482
  35.9 7.5 %copy-start.45 = (bf16[512,256]{1,0:T(8,128)(2,1)}, bf16[512,256]{1,0:T(8,128)(2,1)S(1)}, u32[]{:S(2)}) copy-start(bf16[512,256]{1,0:T(8,128)(2,1)S(1)} %collective-permute-done.4.refs_5_.refs_6_) | copy-start | bytes 786436
  35.9 9.8 %collective-permute-start.5 = (bf16[512,256]{1,0:T(8,128)(2,1)S(1)}, bf16[512,256]{1,0:T(8,128)(2,1)S(1)}, u32[]{:S(2)}, u32[]{:S(2)}) collective-permute-start(bf16[512,256]{1,0:T(8,128)(2,1)S(1)} %collective-permute-done.4.refs_5_.refs_6_), channel_id=1, source_target_pairs={{0,16},{16,32},{32,48},{48,64},{64,80},{80,96},{96,112},{112,0},{1... | collective-permute-start | bytes 786440 | tf_op jit(solution)/shard_map/ppermute | solution.py:482
  35.9 7.5 %copy-start.47 = (bf16[512,256]{1,0:T(8,128)(2,1)}, bf16[512,256]{1,0:T(8,128)(2,1)S(1)}, u32[]{:S(2)}) copy-start(bf16[512,256]{1,0:T(8,128)(2,1)S(1)} %collective-permute-done.6.refs_6_.refs_7_) | copy-start | bytes 786436
  35.9 9.8 %collective-permute-start.7 = (bf16[512,256]{1,0:T(8,128)(2,1)S(1)}, bf16[512,256]{1,0:T(8,128)(2,1)S(1)}, u32[]{:S(2)}, u32[]{:S(2)}) collective-permute-start(bf16[512,256]{1,0:T(8,128)(2,1)S(1)} %collective-permute-done.6.refs_6_.refs_7_), channel_id=1, source_target_pairs={{0,112},{16,0},{32,16},{48,32},{64,48},{80,64},{96,80},{112,96},{1... | collective-permute-start | bytes 786440 | tf_op jit(solution)/shard_map/ppermute | solution.py:482
  45.8 4.8 %copy-start.23 = (bf16[512,256]{1,0:T(8,128)(2,1)}, bf16[512,256]{1,0:T(8,128)(2,1)S(1)}, u32[]{:S(2)}) copy-start(bf16[512,256]{1,0:T(8,128)(2,1)S(1)} %collective-permute-done.5.refs_2_.refs_8_) | copy-start | bytes 786436
  45.8 4.8 %copy-start.25 = (bf16[512,256]{1,0:T(8,128)(2,1)}, bf16[512,256]{1,0:T(8,128)(2,1)S(1)}, u32[]{:S(2)}) copy-start(bf16[512,256]{1,0:T(8,128)(2,1)S(1)} %collective-permute-done.7.refs_3_.refs_9_) | copy-start | bytes 786436
  45.8 6.1 %collective-permute-start.10 = (bf16[256,256]{1,0:T(8,128)(2,1)S(1)}, bf16[256,256]{1,0:T(8,128)(2,1)S(1)}, u32[]{:S(2)}, u32[]{:S(2)}) collective-permute-start(bf16[256,256]{1,0:T(8,128)(2,1)S(1)} %slice.7), channel_id=1, source_target_pairs={{0,16},{16,32},{32,48},{48,64},{64,80},{80,96},{96,112},{112,0},{1... | collective-permute-start | bytes 393224 | tf_op jit(solution)/shard_map/ppermute | solution.py:482
  45.9 6.0 %collective-permute-start.9 = (bf16[256,256]{1,0:T(8,128)(2,1)S(1)}, bf16[256,256]{1,0:T(8,128)(2,1)S(1)}, u32[]{:S(2)}, u32[]{:S(2)}) collective-permute-start(bf16[256,256]{1,0:T(8,128)(2,1)S(1)} %slice.6), channel_id=1, source_target_pairs={{0,112},{16,0},{32,16},{48,32},{64,48},{80,64},{96,80},{112,96},{1... | collective-permute-start | bytes 393224 | tf_op jit(solution)/shard_map/ppermute | solution.py:482
  51.9 4.3 %copy-start.31 = (bf16[256,256]{1,0:T(8,128)(2,1)}, bf16[256,256]{1,0:T(8,128)(2,1)S(1)}, u32[]{:S(2)}) copy-start(bf16[256,256]{1,0:T(8,128)(2,1)S(1)} %collective-permute-done.9.refs_2_.refs_10_) | copy-start | bytes 393220
  51.9 38.8 %slice-start = ((s8[5242880]{0:T(1024)(128)(4,1)}), s8[1048576]{0:T(1024)(128)(4,1)S(1)}, s32[]{:S(2)}) async-start(s8[5242880]{0:T(1024)(128)(4,1)} %bitcast.11), calls=%async_computation.3 | async-start | bytes 2097152
  56.9 13.6 %all-to-all-start = ((f32[8,8,4,128]{3,2,1,0:T(4,128)}), f32[8,8,4,128]{3,2,1,0:T(4,128)S(1)}, u32[]{:S(2)}, u32[]{:S(2)}) async-start(f32[8,8,4,128]{3,2,1,0:T(4,128)} %broadcast_in_dim.2), calls=%async_computation | async-start | bytes 262144 | tf_op jit(solution)/shard_map/all_to_all | solution.py:573
  62.5 4.0 %collective-permute-start.11 = (f32[8,128]{1,0:T(8,128)S(1)}, f32[8,128]{1,0:T(8,128)S(1)}, u32[]{:S(2)}, u32[]{:S(2)}) collective-permute-start(f32[8,128]{1,0:T(8,128)S(1)} %get-tuple-element.81.part), channel_id=1, source_target_pairs={{0,128},{128,0},{1,129},{129,1},{2,130},{130,2},{3,131},{131,3},{4... | collective-permute-start | bytes 12296 | tf_op jit(solution)/shard_map/ppermute | solution.py:482
  85.4 5.3 %slice-start.1 = ((s8[5242880]{0:T(1024)(128)(4,1)}), s8[4194304]{0:T(1024)(128)(4,1)S(1)}, s32[]{:S(2)}) async-start(s8[5242880]{0:T(1024)(128)(4,1)} %bitcast.11), calls=%async_computation.4 | async-start | bytes 8388608
  85.4 5.3 %copy-start.6 = (bf16[1024,1024]{1,0:T(8,128)(2,1)S(1)}, bf16[1024,1024]{1,0:T(8,128)(2,1)}, u32[]{:S(2)}) copy-start(bf16[1024,1024]{1,0:T(8,128)(2,1)} %copy-done.4) | copy-start | bytes 6291460
  85.4 5.3 %copy-start.9 = (bf16[1024,512]{1,0:T(8,128)(2,1)S(1)}, bf16[1024,512]{1,0:T(8,128)(2,1)}, u32[]{:S(2)}) copy-start(bf16[1024,512]{1,0:T(8,128)(2,1)} %copy-done.7) | copy-start | bytes 3145732
  85.4 5.3 %copy-start.12 = (f32[1024,256]{1,0:T(8,128)S(1)}, f32[1024,256]{1,0:T(8,128)}, u32[]{:S(2)}) copy-start(f32[1024,256]{1,0:T(8,128)} %copy-done.10) | copy-start | bytes 3145732
  87.9 6.7 %collective-permute-start.12 = (bf16[512,256]{1,0:T(8,128)(2,1)S(1)}, bf16[512,256]{1,0:T(8,128)(2,1)S(1)}, u32[]{:S(2)}, u32[]{:S(2)}) collective-permute-start(bf16[512,256]{1,0:T(8,128)(2,1)S(1)} %get-tuple-element.89), channel_id=1, source_target_pairs={{0,128},{128,0},{1,129},{129,1},{2,130},{130,2},{3,131},{131,3},{4... | collective-permute-start | bytes 786440 | tf_op jit(solution)/shard_map/ppermute | solution.py:482
  90.7 3.9 %copy-start.3 = (f32[512,1024]{1,0:T(8,128)S(1)}, f32[512,1024]{1,0:T(8,128)}, u32[]{:S(2)}) copy-start(f32[512,1024]{1,0:T(8,128)} %copy-done.2) | copy-start | bytes 6291460
  90.7 3.9 %copy-start.14 = (f32[512,1024]{1,0:T(8,128)S(1)}, f32[512,1024]{1,0:T(8,128)}, u32[]{:S(2)}) copy-start(f32[512,1024]{1,0:T(8,128)} %copy-done.13) | copy-start | bytes 6291460
  90.7 3.9 %copy-start.16 = (f32[512,1024]{1,0:T(8,128)S(1)}, f32[512,1024]{1,0:T(8,128)}, u32[]{:S(2)}) copy-start(f32[512,1024]{1,0:T(8,128)} %copy-done.15) | copy-start | bytes 6291460
  150.1 4.1 %collective-permute-start.13 = (f32[56,128]{1,0:T(8,128)S(1)}, f32[56,128]{1,0:T(8,128)S(1)}, u32[]{:S(2)}, u32[]{:S(2)}) collective-permute-start(f32[56,128]{1,0:T(8,128)S(1)} %get-tuple-element.100), channel_id=1, source_target_pairs={{0,8},{8,0},{1,9},{9,1},{2,10},{10,2},{3,11},{11,3},{4,12},{12,4},... | collective-permute-start | bytes 86024 | tf_op jit(solution)/shard_map/ppermute | solution.py:482
  (34 other events, 57.4 us)

commit v7 on v6

--- a/solution.py
+++ b/solution.py
@@ -570,6 +570,7 @@
     expos.append(expo)
     blocks = early + [ahead, back] + last
     partner = shifted(part, "xh", 1)
+    partner, columns = lax.optimization_barrier((partner, columns))
     sums = lax.all_to_all(jnp.broadcast_to(columns[None], (n_z, n_z, 4, LANES)), "z", 0, 0)
     partial, scaled, across, loss = call(
         functools.partial(send_kernel, n_z, logit),

time: 156 us -> 137 us (0.88)
  local copies, waits for them, and re-layouts: 29 us -> 0.04 us
  blocking collectives: 47.6 us -> 58.5 us
    unnamed x102 -> x0, local copies, waits for them, and re-layouts: 28.3 us -> none
    all_to_all x0 -> x1, blocking collectives: none -> 13 us  [body(): lax.all_to_all(jnp.broadcast_to(columns[None], (n_z, n_z, 4, LANES)), 'z'...]
    all_to_all x1 -> x0, starting transfers between devices: 5.63 us -> none  [body(): lax.all_to_all(jnp.broadcast_to(columns[None], (n_z, n_z, 4, LANES)), 'z'...]
    ppermute x12, starting transfers between devices: 23.8 us -> 28.2 us  [shifted(): lax.ppermute(value, axis, [(k, (k + shift) % count) for k in range(count)])]
    all_to_all x1 -> x0, waiting for transfers between devices: 3.97 us -> none  [body(): lax.all_to_all(jnp.broadcast_to(columns[None], (n_z, n_z, 4, LANES)), 'z'...]
    ppermute x2, waiting for transfers between devices: 1.1 us -> 4.32 us  [crossed(): return lax.ppermute(value, ('z', 'c'), list(enumerate(hop)))]
    all_to_all x1, blocking collectives: 20.5 us -> 18.4 us  [body(): grads = lax.all_to_all(grads, axes, 0, 0, axis_index_groups=far)]
  transfers between devices with their start and end apart: 15 -> 14, of which waited for: 8 -> 9; matrix products, arithmetic and copies ran while one was open for 0% -> 0% of each run, Pallas kernels for 6% -> 7%
where the time goes in v7:
time: 137 us; the launch traced here: 136 us
  blocking collectives  58.5 us (43%)
  starting transfers between devices  32.4 us (24%)
  Pallas kernels  29.7 us (22%)
  waiting for transfers between devices  15.1 us (11%)
    ppermute x12, starting transfers between devices, shifted(): lax.ppermute(value, axis, [(k, (k + shift) % count) for k in range(count)])  28.2 us
    all_to_all x1, blocking collectives, body(): grads = lax.all_to_all(grads, axes, 0, 0, axis_index_groups=near)  27.1 us
    all_to_all x1, blocking collectives, body(): grads = lax.all_to_all(grads, axes, 0, 0, axis_index_groups=far)  18.4 us
    all_to_all x1, blocking collectives, body(): lax.all_to_all(jnp.broadcast_to(columns[None], (n_z, n_z, 4, LANES)), 'z'...  13 us
    ppermute x12, waiting for transfers between devices, shifted(): lax.ppermute(value, axis, [(k, (k + shift) % count) for k in range(count)])  10.8 us
    pallas_call x3, Pallas kernels, scores(): call(kernel, outs, [SMEM] + [VMEM] * (len(args) - 1), cost=cost)(*args)  7.52 us
    pallas_call x1, Pallas kernels, body(): call(functools.partial(backward_kernel, coef), [shape((8, 16 * TILES * 8...  6.76 us
    pallas_call x1, Pallas kernels, body(): call(forward_kernel, [shape((CHIP, WIDE), BF), shape((CHIP, HID), F32), s...  5.41 us
  transfers between devices with their start and end apart: 14, of which 9 were waited for; matrix products, arithmetic and copies ran while one was open for 0% of the time, Pallas kernels for 7%

profile of v7, /device:TPU:1, one launch (start us, length us, event | category | flops | bytes accessed | tf_op | source)
XLA Modules:
  0.0 136.5 jit_solution(3765206465137549099)
XLA Ops:
  0.7 2.0 %shard_map.170 = (bf16[256,384]{1,0:T(8,128)(2,1)S(1)}, bf16[256,384]{1,0:T(8,128)(2,1)S(1)}) custom-call(s32[4]{0:T(128)S(1)} %pad_add_fusion.place, s32[1,256]{1,0:T(1,128)} %replay.1, s32[1,256]{1,0:T(1,128)} %offset.1, bf16[320,256]{1,0:T(8,128)(2,1)} %bitcast.11, bf16[16,320]{1,0:T(8,128)(2,1)} %bitcast.12), custom_call_target="tpu_custom_call" | custom-call | tf_op jit(solution)/shard_map/pallas_call | solution.py:511
  2.7 3.3 %collective-permute-start = (bf16[256,384]{1,0:T(8,128)(2,1)S(1)}, bf16[256,384]{1,0:T(8,128)(2,1)S(1)}, u32[]{:S(2)}, u32[]{:S(2)}) collective-permute-start(bf16[256,384]{1,0:T(8,128)(2,1)S(1)} %get-tuple-element.61), channel_id=1, source_target_pairs={{0,8},{8,0},{1,9},{9,1},{2,10},{10,2},{3,11},{11,3},{4,12},{12,4},... | collective-permute-start | bytes 589832 | tf_op jit(solution)/shard_map/ppermute | solution.py:482
  6.0 1.1 collective-permute-done.recv
  7.1 5.4 %shard_map.171 = (bf16[512,384]{1,0:T(8,128)(2,1)S(1)}, f32[512,1024]{1,0:T(8,128)S(1)}, f32[512,1]{1,0:T(8,128)S(1)}, f32[512,1024]{1,0:T(8,128)S(1)}, f32[512,...) custom-call(s32[4]{0:T(128)S(1)} %pad_add_fusion.place, ...), custom_call_target="tpu_custom_call" | custom-call | tf_op jit(solution)/shard_map/pallas_call | solution.py:524
  12.8 4.0 %collective-permute-start.1 = (bf16[512,256]{1,0:T(8,128)(2,1)S(1)}, bf16[512,256]{1,0:T(8,128)(2,1)S(1)}, u32[]{:S(2)}, u32[]{:S(2)}) collective-permute-start(bf16[512,256]{1,0:T(8,128)(2,1)S(1)} %get-tuple-element.69.refs_0_.ours), channel_id=1, source_target_pairs={{0,120},{8,112},{16,8},{24,0},{32,24},{40,16},{48,40},{56,32},{64,... | collective-permute-start | bytes 786440 | tf_op jit(solution)/shard_map/ppermute | solution.py:547
  16.8 0.9 shard_map.172
  17.7 1.0 shard_map.173
  18.7 4.3 %collective-permute-done.2.refs_3_.refs_4_ = bf16[512,256]{1,0:T(8,128)(2,1)S(1)} collective-permute-done((bf16[512,256]{1,0:T(8,128)(2,1)S(1)}, bf16[512,256]{1,0:T(8,128)(2,1)S(1)}, u32[]{:S(2)}, u32[]{:S(2)}) %collective-permute-start.2) | collective-permute-done | bytes 262176 | tf_op jit(solution)/shard_map/ppermute | solution.py:547
  23.0 3.0 %collective-permute-start.6 = (bf16[512,256]{1,0:T(8,128)(2,1)S(1)}, bf16[512,256]{1,0:T(8,128)(2,1)S(1)}, u32[]{:S(2)}, u32[]{:S(2)}) collective-permute-start(bf16[512,256]{1,0:T(8,128)(2,1)S(1)} %collective-permute-done.1.refs_4_.refs_5_), channel_id=1, source_target_pairs={{0,112},{16,0},{32,16},{48,32},{64,48},{80,64},{96,80},{112,96},{1... | collective-permute-start | bytes 786440 | tf_op jit(solution)/shard_map/ppermute | solution.py:482
  26.0 0.6 collective-permute-start.8
  26.7 2.7 %collective-permute-start.3 = (bf16[512,256]{1,0:T(8,128)(2,1)S(1)}, bf16[512,256]{1,0:T(8,128)(2,1)S(1)}, u32[]{:S(2)}, u32[]{:S(2)}) collective-permute-start(bf16[512,256]{1,0:T(8,128)(2,1)S(1)} %get-tuple-element.69.refs_0_.ours), channel_id=1, source_target_pairs={{0,128},{128,0},{1,129},{129,1},{2,130},{130,2},{3,131},{131,3},{4... | collective-permute-start | bytes 786440 | tf_op jit(solution)/shard_map/ppermute | solution.py:482
  29.4 3.0 %collective-permute-done.4.refs_5_.refs_6_ = bf16[512,256]{1,0:T(8,128)(2,1)S(1)} collective-permute-done((bf16[512,256]{1,0:T(8,128)(2,1)S(1)}, bf16[512,256]{1,0:T(8,128)(2,1)S(1)}, u32[]{:S(2)}, u32[]{:S(2)}) %collective-permute-start.4) | collective-permute-done | bytes 262176 | tf_op jit(solution)/shard_map/ppermute | solution.py:482
  32.4 2.7 %collective-permute-start.7 = (bf16[512,256]{1,0:T(8,128)(2,1)S(1)}, bf16[512,256]{1,0:T(8,128)(2,1)S(1)}, u32[]{:S(2)}, u32[]{:S(2)}) collective-permute-start(bf16[512,256]{1,0:T(8,128)(2,1)S(1)} %collective-permute-done.6.refs_6_.refs_7_), channel_id=1, source_target_pairs={{0,112},{16,0},{32,16},{48,32},{64,48},{80,64},{96,80},{112,96},{1... | collective-permute-start | bytes 786440 | tf_op jit(solution)/shard_map/ppermute | solution.py:482
  35.1 1.0 collective-permute-done.3.refs_1_
  36.1 3.9 %shard_map.174 = (bf16[1024,2560]{1,0:T(8,128)(2,1)S(1)}, f32[1024,128]{1,0:T(8,128)S(1)}, f32[1024,256]{1,0:T(8,128)S(1)}, f32[20,128]{1,0:T(8,128)S(1)}) custom-call(s32[4]{0:T(128)S(1)} %pad_add_fusion.place, bf16[512,256]{1,0:T(8,128)(2,1)S(1)} %get-tuple-element.69.refs_0_.ours, bf16[512,256]{1,0:T(8,128)(2,1)S(1)} %collective-permute-done.3.refs_1_, ...), custom_call_target="tpu_custom_call" | custom-call | flops 2684354560 | bytes 6291456 | tf_op jit(solution)/shard_map/pallas_call | solution.py:236
  40.6 0.7 collective-permute-start.10
  41.3 2.1 %collective-permute-start.9 = (bf16[256,256]{1,0:T(8,128)(2,1)S(1)}, bf16[256,256]{1,0:T(8,128)(2,1)S(1)}, u32[]{:S(2)}, u32[]{:S(2)}) collective-permute-start(bf16[256,256]{1,0:T(8,128)(2,1)S(1)} %slice.6), channel_id=1, source_target_pairs={{0,112},{16,0},{32,16},{48,32},{64,48},{80,64},{96,80},{112,96},{1... | collective-permute-start | bytes 393224 | tf_op jit(solution)/shard_map/ppermute | solution.py:482
  43.4 2.0 %shard_map.175 = (bf16[1024,1024]{1,0:T(8,128)(2,1)S(1)}, f32[1024,128]{1,0:T(8,128)S(1)}, f32[1024,256]{1,0:T(8,128)S(1)}, f32[8,128]{1,0:T(8,128)S(1)}) custom-call(s32[4]{0:T(128)S(1)} %pad_add_fusion.place, bf16[512,256]{1,0:T(8,128)(2,1)S(1)} %get-tuple-element.69.refs_0_.ours, bf16[512,256]{1,0:T(8,128)(2,1)S(1)} %collective-permute-done.3.refs_1_, ...), custom_call_target="tpu_custom_call" | custom-call | flops 1073741824 | bytes 3145728 | tf_op jit(solution)/shard_map/pallas_call | solution.py:236
  45.7 1.6 %shard_map.176 = (bf16[1024,512]{1,0:T(8,128)(2,1)S(1)}, f32[8,128]{1,0:T(8,128)S(1)}, f32[1024,256]{1,0:T(8,128)S(1)}, f32[8,4,128]{2,1,0:T(4,128)S(1)}) custom-call(s32[4]{0:T(128)S(1)} %pad_add_fusion.place, bf16[512,256]{1,0:T(8,128)(2,1)S(1)} %get-tuple-element.69.refs_0_.ours, bf16[512,256]{1,0:T(8,128)(2,1)S(1)} %collective-permute-done.3.refs_1_, ...), custom_call_target="tpu_custom_call" | custom-call | flops 536870912 | bytes 2097152 | tf_op jit(solution)/shard_map/pallas_call | solution.py:236
  47.3 2.8 %collective-permute-start.11 = (f32[8,128]{1,0:T(8,128)S(1)}, f32[8,128]{1,0:T(8,128)S(1)}, u32[]{:S(2)}, u32[]{:S(2)}) collective-permute-start(f32[8,128]{1,0:T(8,128)S(1)} %get-tuple-element.82.part), channel_id=1, source_target_pairs={{0,128},{128,0},{1,129},{129,1},{2,130},{130,2},{3,131},{131,3},{4... | collective-permute-start | bytes 12296 | tf_op jit(solution)/shard_map/ppermute | solution.py:482
  50.1 1.2 collective-permute-done.11.partner
  51.4 13.0 %all_to_all.15.sums = f32[8,8,4,128]{3,2,1,0:T(4,128)S(1)} all-to-all(f32[8,8,4,128]{3,2,1,0:T(4,128)S(1)} %broadcast_in_dim.2), channel_id=1, replica_groups=mesh['xh'=2,'z'=8,'c'=2,'y'=4,'xl'=2] {'z'}, dimensions={0} | all-to-all | bytes 262144 | tf_op jit(solution)/shard_map/all_to_all | solution.py:574
  64.4 2.5 %shard_map.177 = (bf16[512,256]{1,0:T(8,128)(2,1)S(1)}, bf16[4096,256]{1,0:T(8,128)(2,1)S(1)}, f32[128,128]{1,0:T(8,128)S(1)}, f32[1,256]{1,0:T(1,128)}) custom-call(s32[4]{0:T(128)S(1)} %pad_add_fusion.place, f32[8,8,4,128]{3,2,1,0:T(4,128)S(1)} %all_to_all.15.sums, f32[8,128]{1,0:T(8,128)S(1)} %get-tuple-element.82.part, ...), custom_call_target="tpu_custom_call" | custom-call | tf_op jit(solution)/shard_map/pallas_call | solution.py:575
  66.9 2.7 %collective-permute-start.12 = (bf16[512,256]{1,0:T(8,128)(2,1)S(1)}, bf16[512,256]{1,0:T(8,128)(2,1)S(1)}, u32[]{:S(2)}, u32[]{:S(2)}) collective-permute-start(bf16[512,256]{1,0:T(8,128)(2,1)S(1)} %get-tuple-element.93), channel_id=1, source_target_pairs={{0,128},{128,0},{1,129},{129,1},{2,130},{130,2},{3,131},{131,3},{4... | collective-permute-start | bytes 786440 | tf_op jit(solution)/shard_map/ppermute | solution.py:482
  69.6 1.3 shard_map.178.own
  70.9 2.7 %collective-permute-done.12.recv = bf16[512,256]{1,0:T(8,128)(2,1)S(1)} collective-permute-done((bf16[512,256]{1,0:T(8,128)(2,1)S(1)}, bf16[512,256]{1,0:T(8,128)(2,1)S(1)}, u32[]{:S(2)}, u32[]{:S(2)}) %collective-permute-start.12) | collective-permute-done | bytes 262176 | tf_op jit(solution)/shard_map/ppermute | solution.py:482
  73.6 6.8 %shard_map.179 = bf16[8,1568,128]{2,1,0:T(8,128)(2,1)S(1)} custom-call(s32[4]{0:T(128)S(1)} %pad_add_fusion.place, f32[512,256]{1,0:T(8,128)S(1)} %shard_map.178.own, bf16[512,256]{1,0:T(8,128)(2,1)S(1)} %collective-permute-done.12.recv, bf16[512,256]{1,0:T(8,128)(2,1)S(1)} %collective-permute-done.8.refs_2_.refs_3_.other, ...), custom_call_target="tpu_custom_call" | custom-call | tf_op jit(solution)/shard_map/pallas_call | solution.py:597
  80.4 27.1 %all_to_all.16.parts = bf16[8,1568,128]{2,1,0:T(8,128)(2,1)S(1)} all-to-all(bf16[8,1568,128]{2,1,0:T(8,128)(2,1)S(1)} %shard_map.179), channel_id=1, replica_groups={{0,16,2,18,4,20,6,22},{32,48,34,50,36,52,38,54},{64,80,66,82,68,84,70,8..., dimensions={0} | all-to-all | bytes 6422528 | tf_op jit(solution)/shard_map/all_to_all | solution.py:632
  107.9 18.4 %all_to_all.17.parts = bf16[16,112,128]{2,1,0:T(8,128)(2,1)S(1)} all-to-all(bf16[16,112,128]{2,1,0:T(8,128)(2,1)S(1)} %shard_map.180), channel_id=1, replica_groups={{0,32,64,96,1,33,65,97,128,160,192,224,129,161,193,225},{16,48,80,112,1..., dimensions={0} | all-to-all | bytes 917504 | tf_op jit(solution)/shard_map/all_to_all | solution.py:634
  126.9 7.4 %collective-permute-start.13 = (f32[56,128]{1,0:T(8,128)S(1)}, f32[56,128]{1,0:T(8,128)S(1)}, u32[]{:S(2)}, u32[]{:S(2)}) collective-permute-start(f32[56,128]{1,0:T(8,128)S(1)} %get-tuple-element.104), channel_id=1, source_target_pairs={{0,8},{8,0},{1,9},{9,1},{2,10},{10,2},{3,11},{11,3},{4,12},{12,4},... | collective-permute-start | bytes 86024 | tf_op jit(solution)/shard_map/ppermute | solution.py:482
  134.3 0.9 collective-permute-done.13.recv
  135.2 1.3 shard_map.182
  (16 shorter events, 2.3 us)
Async XLA Ops:
  2.7 4.4 %collective-permute-start = (bf16[256,384]{1,0:T(8,128)(2,1)S(1)}, bf16[256,384]{1,0:T(8,128)(2,1)S(1)}, u32[]{:S(2)}, u32[]{:S(2)}) collective-permute-start(bf16[256,384]{1,0:T(8,128)(2,1)S(1)} %get-tuple-element.61), channel_id=1, source_target_pairs={{0,8},{8,0},{1,9},{9,1},{2,10},{10,2},{3,11},{11,3},{4,12},{12,4},... | collective-permute-start | bytes 589832 | tf_op jit(solution)/shard_map/ppermute | solution.py:482
  12.5 10.5 %collective-permute-start.2 = (bf16[512,256]{1,0:T(8,128)(2,1)S(1)}, bf16[512,256]{1,0:T(8,128)(2,1)S(1)}, u32[]{:S(2)}, u32[]{:S(2)}) collective-permute-start(bf16[512,256]{1,0:T(8,128)(2,1)S(1)} %get-tuple-element.69.refs_0_.ours), channel_id=1, source_target_pairs={{0,24},{8,16},{16,40},{24,32},{32,56},{40,48},{48,72},{56,64},{64,... | collective-permute-start | bytes 786440 | tf_op jit(solution)/shard_map/ppermute | solution.py:547
  12.8 10.3 %collective-permute-start.1 = (bf16[512,256]{1,0:T(8,128)(2,1)S(1)}, bf16[512,256]{1,0:T(8,128)(2,1)S(1)}, u32[]{:S(2)}, u32[]{:S(2)}) collective-permute-start(bf16[512,256]{1,0:T(8,128)(2,1)S(1)} %get-tuple-element.69.refs_0_.ours), channel_id=1, source_target_pairs={{0,120},{8,112},{16,8},{24,0},{32,24},{40,16},{48,40},{56,32},{64,... | collective-permute-start | bytes 786440 | tf_op jit(solution)/shard_map/ppermute | solution.py:547
  23.0 9.4 %collective-permute-start.4 = (bf16[512,256]{1,0:T(8,128)(2,1)S(1)}, bf16[512,256]{1,0:T(8,128)(2,1)S(1)}, u32[]{:S(2)}, u32[]{:S(2)}) collective-permute-start(bf16[512,256]{1,0:T(8,128)(2,1)S(1)} %collective-permute-done.2.refs_3_.refs_4_), channel_id=1, source_target_pairs={{0,16},{16,32},{32,48},{48,64},{64,80},{80,96},{96,112},{112,0},{1... | collective-permute-start | bytes 786440 | tf_op jit(solution)/shard_map/ppermute | solution.py:482
  23.0 9.4 %collective-permute-start.6 = (bf16[512,256]{1,0:T(8,128)(2,1)S(1)}, bf16[512,256]{1,0:T(8,128)(2,1)S(1)}, u32[]{:S(2)}, u32[]{:S(2)}) collective-permute-start(bf16[512,256]{1,0:T(8,128)(2,1)S(1)} %collective-permute-done.1.refs_4_.refs_5_), channel_id=1, source_target_pairs={{0,112},{16,0},{32,16},{48,32},{64,48},{80,64},{96,80},{112,96},{1... | collective-permute-start | bytes 786440 | tf_op jit(solution)/shard_map/ppermute | solution.py:482
  26.0 9.1 %collective-permute-start.8 = (bf16[512,256]{1,0:T(8,128)(2,1)S(1)}, bf16[512,256]{1,0:T(8,128)(2,1)S(1)}, u32[]{:S(2)}, u32[]{:S(2)}) collective-permute-start(bf16[512,256]{1,0:T(8,128)(2,1)S(1)} %get-tuple-element.69.refs_0_.ours), channel_id=1, source_target_pairs={{0,8},{8,0},{1,9},{9,1},{2,10},{10,2},{3,11},{11,3},{4,12},{12,4},... | collective-permute-start | bytes 786440 | tf_op jit(solution)/shard_map/ppermute | solution.py:482
  26.7 9.4 %collective-permute-start.3 = (bf16[512,256]{1,0:T(8,128)(2,1)S(1)}, bf16[512,256]{1,0:T(8,128)(2,1)S(1)}, u32[]{:S(2)}, u32[]{:S(2)}) collective-permute-start(bf16[512,256]{1,0:T(8,128)(2,1)S(1)} %get-tuple-element.69.refs_0_.ours), channel_id=1, source_target_pairs={{0,128},{128,0},{1,129},{129,1},{2,130},{130,2},{3,131},{131,3},{4... | collective-permute-start | bytes 786440 | tf_op jit(solution)/shard_map/ppermute | solution.py:482
  32.4 8.2 %collective-permute-start.5 = (bf16[512,256]{1,0:T(8,128)(2,1)S(1)}, bf16[512,256]{1,0:T(8,128)(2,1)S(1)}, u32[]{:S(2)}, u32[]{:S(2)}) collective-permute-start(bf16[512,256]{1,0:T(8,128)(2,1)S(1)} %collective-permute-done.4.refs_5_.refs_6_), channel_id=1, source_target_pairs={{0,16},{16,32},{32,48},{48,64},{64,80},{80,96},{96,112},{112,0},{1... | collective-permute-start | bytes 786440 | tf_op jit(solution)/shard_map/ppermute | solution.py:482
  32.4 8.2 %collective-permute-start.7 = (bf16[512,256]{1,0:T(8,128)(2,1)S(1)}, bf16[512,256]{1,0:T(8,128)(2,1)S(1)}, u32[]{:S(2)}, u32[]{:S(2)}) collective-permute-start(bf16[512,256]{1,0:T(8,128)(2,1)S(1)} %collective-permute-done.6.refs_6_.refs_7_), channel_id=1, source_target_pairs={{0,112},{16,0},{32,16},{48,32},{64,48},{80,64},{96,80},{112,96},{1... | collective-permute-start | bytes 786440 | tf_op jit(solution)/shard_map/ppermute | solution.py:482
  40.6 5.1 %collective-permute-start.10 = (bf16[256,256]{1,0:T(8,128)(2,1)S(1)}, bf16[256,256]{1,0:T(8,128)(2,1)S(1)}, u32[]{:S(2)}, u32[]{:S(2)}) collective-permute-start(bf16[256,256]{1,0:T(8,128)(2,1)S(1)} %slice.7), channel_id=1, source_target_pairs={{0,16},{16,32},{32,48},{48,64},{64,80},{80,96},{96,112},{112,0},{1... | collective-permute-start | bytes 393224 | tf_op jit(solution)/shard_map/ppermute | solution.py:482
  41.3 4.4 %collective-permute-start.9 = (bf16[256,256]{1,0:T(8,128)(2,1)S(1)}, bf16[256,256]{1,0:T(8,128)(2,1)S(1)}, u32[]{:S(2)}, u32[]{:S(2)}) collective-permute-start(bf16[256,256]{1,0:T(8,128)(2,1)S(1)} %slice.6), channel_id=1, source_target_pairs={{0,112},{16,0},{32,16},{48,32},{64,48},{80,64},{96,80},{112,96},{1... | collective-permute-start | bytes 393224 | tf_op jit(solution)/shard_map/ppermute | solution.py:482
  47.3 4.0 %collective-permute-start.11 = (f32[8,128]{1,0:T(8,128)S(1)}, f32[8,128]{1,0:T(8,128)S(1)}, u32[]{:S(2)}, u32[]{:S(2)}) collective-permute-start(f32[8,128]{1,0:T(8,128)S(1)} %get-tuple-element.82.part), channel_id=1, source_target_pairs={{0,128},{128,0},{1,129},{129,1},{2,130},{130,2},{3,131},{131,3},{4... | collective-permute-start | bytes 12296 | tf_op jit(solution)/shard_map/ppermute | solution.py:482
  66.9 6.7 %collective-permute-start.12 = (bf16[512,256]{1,0:T(8,128)(2,1)S(1)}, bf16[512,256]{1,0:T(8,128)(2,1)S(1)}, u32[]{:S(2)}, u32[]{:S(2)}) collective-permute-start(bf16[512,256]{1,0:T(8,128)(2,1)S(1)} %get-tuple-element.93), channel_id=1, source_target_pairs={{0,128},{128,0},{1,129},{129,1},{2,130},{130,2},{3,131},{131,3},{4... | collective-permute-start | bytes 786440 | tf_op jit(solution)/shard_map/ppermute | solution.py:482
  126.9 8.3 %collective-permute-start.13 = (f32[56,128]{1,0:T(8,128)S(1)}, f32[56,128]{1,0:T(8,128)S(1)}, u32[]{:S(2)}, u32[]{:S(2)}) collective-permute-start(f32[56,128]{1,0:T(8,128)S(1)} %get-tuple-element.104), channel_id=1, source_target_pairs={{0,8},{8,0},{1,9},{9,1},{2,10},{10,2},{3,11},{11,3},{4,12},{12,4},... | collective-permute-start | bytes 86024 | tf_op jit(solution)/shard_map/ppermute | solution.py:482

commit v8 on v7

--- a/solution.py
+++ b/solution.py
@@ -153,11 +153,13 @@
     return jnp.sum(values.T, axis=0, keepdims=True)
 
 
-def ring_order(n_z):
-    order = [0, n_z - 1, 1]
-    for k in range(2, n_z // 2):
-        order += [n_z - k, k]
-    return order + [n_z // 2]
+def ring_order(place, n_z):
+    order = [0]
+    for k in range(1, n_z // 2):
+        order += [k, n_z - k]
+    order.append(n_z // 2)
+    z, role = place[1], place[2]
+    return [lax.rem(z + jnp.where(role == 0, shift, n_z - shift), n_z) for shift in order]
 
 
 def score_kernel(n_blocks, first, last, factor, place, *refs):
@@ -209,8 +211,8 @@
         n_z = columns.shape[0]
         held = [ref[k : k + 4, :] for ref in old_columns for k in range(0, ref.shape[0], 4)]
         held.append(jnp.concatenate(lines, axis=0))
-        for shift, value in zip(ring_order(n_z), held):
-            columns[lax.rem(place[1] + shift, n_z)] = value
+        for origin, value in zip(ring_order(place, n_z), held):
+            columns[origin] = value
     else:
         for k, line in enumerate(lines):
             columns[k : k + 1, :] = line
@@ -264,8 +266,8 @@
     mine = part[:4, :] + partner[4:, :]
     theirs = part[4:, :] + partner[:4, :]
     lines[...] = jnp.ones((LANES, LANES), F32)
-    for k, shift in enumerate(ring_order(n_z)):
-        lines[4 * k : 4 * k + 4, :] = 1.0 / whole[lax.rem(z + shift, n_z)]
+    for k, origin in enumerate(ring_order(place, n_z)):
+        lines[4 * k : 4 * k + 4, :] = 1.0 / whole[origin]
     lines[4 * n_z : 4 * n_z + 4, :] = 1.0 / mine
     lines[4 * n_z + 4 : 4 * n_z + 8, :] = 1.0 / theirs
     columns = lines[...].T
@@ -542,26 +544,30 @@
         ],
     )(place, keep, recv, sa_obs, sa_act, sa_mid, sa_out, goal_obs, goal_mid, goal_out)
 
-    def crossed(value, shift):
-        hop = [((k + shift) % n_z * 2 + 1 - c) for k in range(n_z) for c in range(2)]
-        return lax.ppermute(value, ("z", "c"), list(enumerate(hop)))
-
-    ahead, back = crossed(unit, 1), crossed(unit, -1)
+    def hop(value, way, cross=0):
+        pairs = []
+        for k in range(n_z):
+            for c in range(2):
+                to = c ^ cross
+                pairs.append((k * 2 + c, (k + (way if to else -way)) % n_z * 2 + to))
+        return lax.ppermute(value, ("z", "c"), pairs)
+
+    ahead, back = hop(unit, 1, 1), hop(unit, -1, 1)
     s1, h1 = slopes(n1)
     s2, h2 = slopes(n2)
     back, ahead, s1, h1, s2, h2, late = lax.optimization_barrier((back, ahead, s1, h1, s2, h2, unit))
     steps = [[ahead, back]]
     for k in range(2, n_z // 2 - 1):
-        ahead, back = shifted(ahead, "z", 1), shifted(back, "z", -1)
+        ahead, back = hop(ahead, 1), hop(back, -1)
         steps.append([ahead, back])
     other, theirs = shifted(late, "c", 1), shifted(late, "xh", 1)
     early = [other] + [block for step in steps for block in step]
-    ahead, back = shifted(ahead, "z", 1), shifted(back, "z", -1)
+    ahead, back = hop(ahead, 1), hop(back, -1)
     factor = logit * math.log2(math.e)
     expo, part, total, columns = scores(place, unit, theirs, early, None, None, factor)
     held = [columns]
     ahead, back, part, total = lax.optimization_barrier((ahead, back, part, total))
-    last = [shifted(back[:ROWS], "z", -1), shifted(ahead[ROWS:], "z", 1)]
+    last = [hop(back[:ROWS], -1), hop(ahead[ROWS:], 1)]
     expos = [expo]
     expo, part, total, columns = scores(place, unit, theirs, [ahead, back], (part, total), None, factor)
     expos.append(expo)

time: 137 us -> 137 us (level)
    ppermute x12 -> x6, starting transfers between devices: 28.2 us -> 17.8 us  [shifted(): lax.ppermute(value, axis, [(k, (k + shift) % count) for k in range(count)])]
    ppermute x2 -> x8, starting transfers between devices: 4.26 us -> 13.8 us  [hop(): return lax.ppermute(value, ('z', 'c'), pairs)]
    ppermute x2 -> x8, waiting for transfers between devices: 4.32 us -> 9.77 us  [hop(): return lax.ppermute(value, ('z', 'c'), pairs)]
    ppermute x12 -> x6, waiting for transfers between devices: 10.8 us -> 6.35 us  [shifted(): lax.ppermute(value, axis, [(k, (k + shift) % count) for k in range(count)])]
where the time goes in v8:
time: 137 us; the launch traced here: 136 us
  blocking collectives  58.1 us (42%)
  starting transfers between devices  31.7 us (23%)
  Pallas kernels  29.7 us (22%)
  waiting for transfers between devices  16.1 us (12%)
    all_to_all x1, blocking collectives, body(): grads = lax.all_to_all(grads, axes, 0, 0, axis_index_groups=near)  26.9 us
    all_to_all x1, blocking collectives, body(): grads = lax.all_to_all(grads, axes, 0, 0, axis_index_groups=far)  18.6 us
    ppermute x6, starting transfers between devices, shifted(): lax.ppermute(value, axis, [(k, (k + shift) % count) for k in range(count)])  17.8 us
    ppermute x8, starting transfers between devices, hop(): return lax.ppermute(value, ('z', 'c'), pairs)  13.8 us
    all_to_all x1, blocking collectives, body(): lax.all_to_all(jnp.broadcast_to(columns[None], (n_z, n_z, 4, LANES)), 'z'...  12.6 us
    ppermute x8, waiting for transfers between devices, hop(): return lax.ppermute(value, ('z', 'c'), pairs)  9.77 us
    pallas_call x3, Pallas kernels, scores(): call(kernel, outs, [SMEM] + [VMEM] * (len(args) - 1), cost=cost)(*args)  7.52 us
    pallas_call x1, Pallas kernels, body(): call(functools.partial(backward_kernel, coef), [shape((8, 16 * TILES * 8...  6.76 us
  transfers between devices with their start and end apart: 14, of which 9 were waited for; matrix products, arithmetic and copies ran while one was open for 0% of the time, Pallas kernels for 7%

profile of v8, /device:TPU:1, one launch (start us, length us, event | category | flops | bytes accessed | tf_op | source)
XLA Modules:
  0.0 136.5 jit_solution(7396598370364783738)
XLA Ops:
  0.7 2.0 %shard_map.170 = (bf16[256,384]{1,0:T(8,128)(2,1)S(1)}, bf16[256,384]{1,0:T(8,128)(2,1)S(1)}) custom-call(s32[4]{0:T(128)S(1)} %pad_add_fusion.place, s32[1,256]{1,0:T(1,128)} %replay.1, s32[1,256]{1,0:T(1,128)} %offset.1, bf16[320,256]{1,0:T(8,128)(2,1)} %bitcast.11, bf16[16,320]{1,0:T(8,128)(2,1)} %bitcast.12), custom_call_target="tpu_custom_call" | custom-call | tf_op jit(solution)/shard_map/pallas_call | solution.py:513
  2.7 3.3 %collective-permute-start = (bf16[256,384]{1,0:T(8,128)(2,1)S(1)}, bf16[256,384]{1,0:T(8,128)(2,1)S(1)}, u32[]{:S(2)}, u32[]{:S(2)}) collective-permute-start(bf16[256,384]{1,0:T(8,128)(2,1)S(1)} %get-tuple-element.61), channel_id=1, source_target_pairs={{0,8},{8,0},{1,9},{9,1},{2,10},{10,2},{3,11},{11,3},{4,12},{12,4},... | collective-permute-start | bytes 589832 | tf_op jit(solution)/shard_map/ppermute | solution.py:484
  6.0 1.1 collective-permute-done.recv
  7.1 5.4 %shard_map.171 = (bf16[512,384]{1,0:T(8,128)(2,1)S(1)}, f32[512,1024]{1,0:T(8,128)S(1)}, f32[512,1]{1,0:T(8,128)S(1)}, f32[512,1024]{1,0:T(8,128)S(1)}, f32[512,...) custom-call(s32[4]{0:T(128)S(1)} %pad_add_fusion.place, ...), custom_call_target="tpu_custom_call" | custom-call | tf_op jit(solution)/shard_map/pallas_call | solution.py:526
  12.5 4.2 %collective-permute-start.2 = (bf16[512,256]{1,0:T(8,128)(2,1)S(1)}, bf16[512,256]{1,0:T(8,128)(2,1)S(1)}, u32[]{:S(2)}, u32[]{:S(2)}) collective-permute-start(bf16[512,256]{1,0:T(8,128)(2,1)S(1)} %get-tuple-element.69.refs_0_.ours), channel_id=1, source_target_pairs={{0,24},{8,112},{16,40},{24,0},{32,56},{40,16},{48,72},{56,32},{64,... | collective-permute-start | bytes 786440 | tf_op jit(solution)/shard_map/ppermute | solution.py:553
  16.7 0.9 shard_map.172
  17.7 1.0 shard_map.173
  18.6 4.9 %collective-permute-done.2.refs_3_.refs_4_ = bf16[512,256]{1,0:T(8,128)(2,1)S(1)} collective-permute-done((bf16[512,256]{1,0:T(8,128)(2,1)S(1)}, bf16[512,256]{1,0:T(8,128)(2,1)S(1)}, u32[]{:S(2)}, u32[]{:S(2)}) %collective-permute-start.2) | collective-permute-done | bytes 262176 | tf_op jit(solution)/shard_map/ppermute | solution.py:553
  23.5 2.7 %collective-permute-start.6 = (bf16[512,256]{1,0:T(8,128)(2,1)S(1)}, bf16[512,256]{1,0:T(8,128)(2,1)S(1)}, u32[]{:S(2)}, u32[]{:S(2)}) collective-permute-start(bf16[512,256]{1,0:T(8,128)(2,1)S(1)} %collective-permute-done.1.refs_4_.refs_5_), channel_id=1, source_target_pairs={{0,16},{8,120},{16,32},{24,8},{32,48},{40,24},{48,64},{56,40},{64,... | collective-permute-start | bytes 786440 | tf_op jit(solution)/shard_map/ppermute | solution.py:553
  26.3 2.7 %collective-permute-start.3 = (bf16[512,256]{1,0:T(8,128)(2,1)S(1)}, bf16[512,256]{1,0:T(8,128)(2,1)S(1)}, u32[]{:S(2)}, u32[]{:S(2)}) collective-permute-start(bf16[512,256]{1,0:T(8,128)(2,1)S(1)} %get-tuple-element.69.refs_0_.ours), channel_id=1, source_target_pairs={{0,128},{128,0},{1,129},{129,1},{2,130},{130,2},{3,131},{131,3},{4... | collective-permute-start | bytes 786440 | tf_op jit(solution)/shard_map/ppermute | solution.py:484
  29.0 1.4 %collective-permute-done.4.refs_5_.refs_6_ = bf16[512,256]{1,0:T(8,128)(2,1)S(1)} collective-permute-done((bf16[512,256]{1,0:T(8,128)(2,1)S(1)}, bf16[512,256]{1,0:T(8,128)(2,1)S(1)}, u32[]{:S(2)}, u32[]{:S(2)}) %collective-permute-start.4) | collective-permute-done | bytes 262176 | tf_op jit(solution)/shard_map/ppermute | solution.py:553
  30.5 1.4 %collective-permute-done.6.refs_6_.refs_7_ = bf16[512,256]{1,0:T(8,128)(2,1)S(1)} collective-permute-done((bf16[512,256]{1,0:T(8,128)(2,1)S(1)}, bf16[512,256]{1,0:T(8,128)(2,1)S(1)}, u32[]{:S(2)}, u32[]{:S(2)}) %collective-permute-start.6) | collective-permute-done | bytes 262176 | tf_op jit(solution)/shard_map/ppermute | solution.py:553
  31.9 3.4 %collective-permute-start.7 = (bf16[512,256]{1,0:T(8,128)(2,1)S(1)}, bf16[512,256]{1,0:T(8,128)(2,1)S(1)}, u32[]{:S(2)}, u32[]{:S(2)}) collective-permute-start(bf16[512,256]{1,0:T(8,128)(2,1)S(1)} %collective-permute-done.6.refs_6_.refs_7_), channel_id=1, source_target_pairs={{0,16},{8,120},{16,32},{24,8},{32,48},{40,24},{48,64},{56,40},{64,... | collective-permute-start | bytes 786440 | tf_op jit(solution)/shard_map/ppermute | solution.py:553
  35.3 3.9 %shard_map.174 = (bf16[1024,2560]{1,0:T(8,128)(2,1)S(1)}, f32[1024,128]{1,0:T(8,128)S(1)}, f32[1024,256]{1,0:T(8,128)S(1)}, f32[20,128]{1,0:T(8,128)S(1)}) custom-call(s32[4]{0:T(128)S(1)} %pad_add_fusion.place, bf16[512,256]{1,0:T(8,128)(2,1)S(1)} %get-tuple-element.69.refs_0_.ours, bf16[512,256]{1,0:T(8,128)(2,1)S(1)} %collective-permute-done.3.refs_1_, ...), custom_call_target="tpu_custom_call" | custom-call | flops 2684354560 | bytes 6291456 | tf_op jit(solution)/shard_map/pallas_call | solution.py:238
  39.3 1.7 %collective-permute-done.7.refs_3_.refs_9_ = bf16[512,256]{1,0:T(8,128)(2,1)S(1)} collective-permute-done((bf16[512,256]{1,0:T(8,128)(2,1)S(1)}, bf16[512,256]{1,0:T(8,128)(2,1)S(1)}, u32[]{:S(2)}, u32[]{:S(2)}) %collective-permute-start.7) | collective-permute-done | bytes 262176 | tf_op jit(solution)/shard_map/ppermute | solution.py:553
  41.1 3.5 %collective-permute-start.9 = (bf16[256,256]{1,0:T(8,128)(2,1)S(1)}, bf16[256,256]{1,0:T(8,128)(2,1)S(1)}, u32[]{:S(2)}, u32[]{:S(2)}) collective-permute-start(bf16[256,256]{1,0:T(8,128)(2,1)S(1)} %slice.6), channel_id=1, source_target_pairs={{0,16},{8,120},{16,32},{24,8},{32,48},{40,24},{48,64},{56,40},{64,... | collective-permute-start | bytes 393224 | tf_op jit(solution)/shard_map/ppermute | solution.py:553
  44.6 2.0 %shard_map.175 = (bf16[1024,1024]{1,0:T(8,128)(2,1)S(1)}, f32[1024,128]{1,0:T(8,128)S(1)}, f32[1024,256]{1,0:T(8,128)S(1)}, f32[8,128]{1,0:T(8,128)S(1)}) custom-call(s32[4]{0:T(128)S(1)} %pad_add_fusion.place, bf16[512,256]{1,0:T(8,128)(2,1)S(1)} %get-tuple-element.69.refs_0_.ours, bf16[512,256]{1,0:T(8,128)(2,1)S(1)} %collective-permute-done.3.refs_1_, ...), custom_call_target="tpu_custom_call" | custom-call | flops 1073741824 | bytes 3145728 | tf_op jit(solution)/shard_map/pallas_call | solution.py:238
  46.9 1.6 %shard_map.176 = (bf16[1024,512]{1,0:T(8,128)(2,1)S(1)}, f32[8,128]{1,0:T(8,128)S(1)}, f32[1024,256]{1,0:T(8,128)S(1)}, f32[8,4,128]{2,1,0:T(4,128)S(1)}) custom-call(s32[4]{0:T(128)S(1)} %pad_add_fusion.place, bf16[512,256]{1,0:T(8,128)(2,1)S(1)} %get-tuple-element.69.refs_0_.ours, bf16[512,256]{1,0:T(8,128)(2,1)S(1)} %collective-permute-done.3.refs_1_, ...), custom_call_target="tpu_custom_call" | custom-call | flops 536870912 | bytes 2097152 | tf_op jit(solution)/shard_map/pallas_call | solution.py:238
  48.5 2.5 %collective-permute-start.11 = (f32[8,128]{1,0:T(8,128)S(1)}, f32[8,128]{1,0:T(8,128)S(1)}, u32[]{:S(2)}, u32[]{:S(2)}) collective-permute-start(f32[8,128]{1,0:T(8,128)S(1)} %get-tuple-element.82.part), channel_id=1, source_target_pairs={{0,128},{128,0},{1,129},{129,1},{2,130},{130,2},{3,131},{131,3},{4... | collective-permute-start | bytes 12296 | tf_op jit(solution)/shard_map/ppermute | solution.py:484
  51.0 1.6 %collective-permute-done.11.partner = f32[8,128]{1,0:T(8,128)S(1)} collective-permute-done((f32[8,128]{1,0:T(8,128)S(1)}, f32[8,128]{1,0:T(8,128)S(1)}, u32[]{:S(2)}, u32[]{:S(2)}) %collective-permute-start.11) | collective-permute-done | bytes 4128 | tf_op jit(solution)/shard_map/ppermute | solution.py:484
  52.6 12.6 %all_to_all.15.sums = f32[8,8,4,128]{3,2,1,0:T(4,128)S(1)} all-to-all(f32[8,8,4,128]{3,2,1,0:T(4,128)S(1)} %broadcast_in_dim.2), channel_id=1, replica_groups=mesh['xh'=2,'z'=8,'c'=2,'y'=4,'xl'=2] {'z'}, dimensions={0} | all-to-all | bytes 262144 | tf_op jit(solution)/shard_map/all_to_all | solution.py:580
  65.2 2.5 %shard_map.177 = (bf16[512,256]{1,0:T(8,128)(2,1)S(1)}, bf16[4096,256]{1,0:T(8,128)(2,1)S(1)}, f32[128,128]{1,0:T(8,128)S(1)}, f32[1,256]{1,0:T(1,128)}) custom-call(s32[4]{0:T(128)S(1)} %pad_add_fusion.place, f32[8,8,4,128]{3,2,1,0:T(4,128)S(1)} %all_to_all.15.sums, f32[8,128]{1,0:T(8,128)S(1)} %get-tuple-element.82.part, ...), custom_call_target="tpu_custom_call" | custom-call | tf_op jit(solution)/shard_map/pallas_call | solution.py:581
  67.7 2.6 %collective-permute-start.12 = (bf16[512,256]{1,0:T(8,128)(2,1)S(1)}, bf16[512,256]{1,0:T(8,128)(2,1)S(1)}, u32[]{:S(2)}, u32[]{:S(2)}) collective-permute-start(bf16[512,256]{1,0:T(8,128)(2,1)S(1)} %get-tuple-element.93), channel_id=1, source_target_pairs={{0,128},{128,0},{1,129},{129,1},{2,130},{130,2},{3,131},{131,3},{4... | collective-permute-start | bytes 786440 | tf_op jit(solution)/shard_map/ppermute | solution.py:484
  70.3 1.3 shard_map.178.own
  71.5 2.9 %collective-permute-done.12.recv = bf16[512,256]{1,0:T(8,128)(2,1)S(1)} collective-permute-done((bf16[512,256]{1,0:T(8,128)(2,1)S(1)}, bf16[512,256]{1,0:T(8,128)(2,1)S(1)}, u32[]{:S(2)}, u32[]{:S(2)}) %collective-permute-start.12) | collective-permute-done | bytes 262176 | tf_op jit(solution)/shard_map/ppermute | solution.py:484
  74.4 6.8 %shard_map.179 = bf16[8,1568,128]{2,1,0:T(8,128)(2,1)S(1)} custom-call(s32[4]{0:T(128)S(1)} %pad_add_fusion.place, f32[512,256]{1,0:T(8,128)S(1)} %shard_map.178.own, bf16[512,256]{1,0:T(8,128)(2,1)S(1)} %collective-permute-done.12.recv, bf16[512,256]{1,0:T(8,128)(2,1)S(1)} %collective-permute-done.8.refs_2_.refs_3_.other, ...), custom_call_target="tpu_custom_call" | custom-call | tf_op jit(solution)/shard_map/pallas_call | solution.py:603
  81.2 26.9 %all_to_all.16.parts = bf16[8,1568,128]{2,1,0:T(8,128)(2,1)S(1)} all-to-all(bf16[8,1568,128]{2,1,0:T(8,128)(2,1)S(1)} %shard_map.179), channel_id=1, replica_groups={{0,16,2,18,4,20,6,22},{32,48,34,50,36,52,38,54},{64,80,66,82,68,84,70,8..., dimensions={0} | all-to-all | bytes 6422528 | tf_op jit(solution)/shard_map/all_to_all | solution.py:638
  108.5 18.6 %all_to_all.17.parts = bf16[16,112,128]{2,1,0:T(8,128)(2,1)S(1)} all-to-all(bf16[16,112,128]{2,1,0:T(8,128)(2,1)S(1)} %shard_map.180), channel_id=1, replica_groups={{0,32,64,96,1,33,65,97,128,160,192,224,129,161,193,225},{16,48,80,112,1..., dimensions={0} | all-to-all | bytes 917504 | tf_op jit(solution)/shard_map/all_to_all | solution.py:640
  127.1 0.6 shard_map.181
  127.7 6.6 %collective-permute-start.13 = (f32[56,128]{1,0:T(8,128)S(1)}, f32[56,128]{1,0:T(8,128)S(1)}, u32[]{:S(2)}, u32[]{:S(2)}) collective-permute-start(f32[56,128]{1,0:T(8,128)S(1)} %get-tuple-element.104), channel_id=1, source_target_pairs={{0,8},{8,0},{1,9},{9,1},{2,10},{10,2},{3,11},{11,3},{4,12},{12,4},... | collective-permute-start | bytes 86024 | tf_op jit(solution)/shard_map/ppermute | solution.py:484
  134.3 0.9 collective-permute-done.13.recv
  135.2 1.3 shard_map.182
  (16 shorter events, 1.0 us)
Async XLA Ops:
  2.7 4.4 %collective-permute-start = (bf16[256,384]{1,0:T(8,128)(2,1)S(1)}, bf16[256,384]{1,0:T(8,128)(2,1)S(1)}, u32[]{:S(2)}, u32[]{:S(2)}) collective-permute-start(bf16[256,384]{1,0:T(8,128)(2,1)S(1)} %get-tuple-element.61), channel_id=1, source_target_pairs={{0,8},{8,0},{1,9},{9,1},{2,10},{10,2},{3,11},{11,3},{4,12},{12,4},... | collective-permute-start | bytes 589832 | tf_op jit(solution)/shard_map/ppermute | solution.py:484
  12.5 11.0 %collective-permute-start.2 = (bf16[512,256]{1,0:T(8,128)(2,1)S(1)}, bf16[512,256]{1,0:T(8,128)(2,1)S(1)}, u32[]{:S(2)}, u32[]{:S(2)}) collective-permute-start(bf16[512,256]{1,0:T(8,128)(2,1)S(1)} %get-tuple-element.69.refs_0_.ours), channel_id=1, source_target_pairs={{0,24},{8,112},{16,40},{24,0},{32,56},{40,16},{48,72},{56,32},{64,... | collective-permute-start | bytes 786440 | tf_op jit(solution)/shard_map/ppermute | solution.py:553
  16.7 6.8 %collective-permute-start.1 = (bf16[512,256]{1,0:T(8,128)(2,1)S(1)}, bf16[512,256]{1,0:T(8,128)(2,1)S(1)}, u32[]{:S(2)}, u32[]{:S(2)}) collective-permute-start(bf16[512,256]{1,0:T(8,128)(2,1)S(1)} %get-tuple-element.69.refs_0_.ours), channel_id=1, source_target_pairs={{0,120},{8,16},{16,8},{24,32},{32,24},{40,48},{48,40},{56,64},{64,... | collective-permute-start | bytes 786440 | tf_op jit(solution)/shard_map/ppermute | solution.py:553
  23.5 6.9 %collective-permute-start.4 = (bf16[512,256]{1,0:T(8,128)(2,1)S(1)}, bf16[512,256]{1,0:T(8,128)(2,1)S(1)}, u32[]{:S(2)}, u32[]{:S(2)}) collective-permute-start(bf16[512,256]{1,0:T(8,128)(2,1)S(1)} %collective-permute-done.2.refs_3_.refs_4_), channel_id=1, source_target_pairs={{0,112},{8,24},{16,0},{24,40},{32,16},{40,56},{48,32},{56,72},{64,... | collective-permute-start | bytes 786440 | tf_op jit(solution)/shard_map/ppermute | solution.py:553
  23.5 8.4 %collective-permute-start.6 = (bf16[512,256]{1,0:T(8,128)(2,1)S(1)}, bf16[512,256]{1,0:T(8,128)(2,1)S(1)}, u32[]{:S(2)}, u32[]{:S(2)}) collective-permute-start(bf16[512,256]{1,0:T(8,128)(2,1)S(1)} %collective-permute-done.1.refs_4_.refs_5_), channel_id=1, source_target_pairs={{0,16},{8,120},{16,32},{24,8},{32,48},{40,24},{48,64},{56,40},{64,... | collective-permute-start | bytes 786440 | tf_op jit(solution)/shard_map/ppermute | solution.py:553
  26.2 9.1 %collective-permute-start.8 = (bf16[512,256]{1,0:T(8,128)(2,1)S(1)}, bf16[512,256]{1,0:T(8,128)(2,1)S(1)}, u32[]{:S(2)}, u32[]{:S(2)}) collective-permute-start(bf16[512,256]{1,0:T(8,128)(2,1)S(1)} %get-tuple-element.69.refs_0_.ours), channel_id=1, source_target_pairs={{0,8},{8,0},{1,9},{9,1},{2,10},{10,2},{3,11},{11,3},{4,12},{12,4},... | collective-permute-start | bytes 786440 | tf_op jit(solution)/shard_map/ppermute | solution.py:484
  26.3 9.0 %collective-permute-start.3 = (bf16[512,256]{1,0:T(8,128)(2,1)S(1)}, bf16[512,256]{1,0:T(8,128)(2,1)S(1)}, u32[]{:S(2)}, u32[]{:S(2)}) collective-permute-start(bf16[512,256]{1,0:T(8,128)(2,1)S(1)} %get-tuple-element.69.refs_0_.ours), channel_id=1, source_target_pairs={{0,128},{128,0},{1,129},{129,1},{2,130},{130,2},{3,131},{131,3},{4... | collective-permute-start | bytes 786440 | tf_op jit(solution)/shard_map/ppermute | solution.py:484
  30.5 8.8 %collective-permute-start.5 = (bf16[512,256]{1,0:T(8,128)(2,1)S(1)}, bf16[512,256]{1,0:T(8,128)(2,1)S(1)}, u32[]{:S(2)}, u32[]{:S(2)}) collective-permute-start(bf16[512,256]{1,0:T(8,128)(2,1)S(1)} %collective-permute-done.4.refs_5_.refs_6_), channel_id=1, source_target_pairs={{0,112},{8,24},{16,0},{24,40},{32,16},{40,56},{48,32},{56,72},{64,... | collective-permute-start | bytes 786440 | tf_op jit(solution)/shard_map/ppermute | solution.py:553
  31.9 9.1 %collective-permute-start.7 = (bf16[512,256]{1,0:T(8,128)(2,1)S(1)}, bf16[512,256]{1,0:T(8,128)(2,1)S(1)}, u32[]{:S(2)}, u32[]{:S(2)}) collective-permute-start(bf16[512,256]{1,0:T(8,128)(2,1)S(1)} %collective-permute-done.6.refs_6_.refs_7_), channel_id=1, source_target_pairs={{0,16},{8,120},{16,32},{24,8},{32,48},{40,24},{48,64},{56,40},{64,... | collective-permute-start | bytes 786440 | tf_op jit(solution)/shard_map/ppermute | solution.py:553
  41.0 5.8 %collective-permute-start.10 = (bf16[256,256]{1,0:T(8,128)(2,1)S(1)}, bf16[256,256]{1,0:T(8,128)(2,1)S(1)}, u32[]{:S(2)}, u32[]{:S(2)}) collective-permute-start(bf16[256,256]{1,0:T(8,128)(2,1)S(1)} %slice.7), channel_id=1, source_target_pairs={{0,112},{8,24},{16,0},{24,40},{32,16},{40,56},{48,32},{56,72},{64,... | collective-permute-start | bytes 393224 | tf_op jit(solution)/shard_map/ppermute | solution.py:553
  41.1 5.8 %collective-permute-start.9 = (bf16[256,256]{1,0:T(8,128)(2,1)S(1)}, bf16[256,256]{1,0:T(8,128)(2,1)S(1)}, u32[]{:S(2)}, u32[]{:S(2)}) collective-permute-start(bf16[256,256]{1,0:T(8,128)(2,1)S(1)} %slice.6), channel_id=1, source_target_pairs={{0,16},{8,120},{16,32},{24,8},{32,48},{40,24},{48,64},{56,40},{64,... | collective-permute-start | bytes 393224 | tf_op jit(solution)/shard_map/ppermute | solution.py:553
  48.5 4.0 %collective-permute-start.11 = (f32[8,128]{1,0:T(8,128)S(1)}, f32[8,128]{1,0:T(8,128)S(1)}, u32[]{:S(2)}, u32[]{:S(2)}) collective-permute-start(f32[8,128]{1,0:T(8,128)S(1)} %get-tuple-element.82.part), channel_id=1, source_target_pairs={{0,128},{128,0},{1,129},{129,1},{2,130},{130,2},{3,131},{131,3},{4... | collective-permute-start | bytes 12296 | tf_op jit(solution)/shard_map/ppermute | solution.py:484
  67.7 6.7 %collective-permute-start.12 = (bf16[512,256]{1,0:T(8,128)(2,1)S(1)}, bf16[512,256]{1,0:T(8,128)(2,1)S(1)}, u32[]{:S(2)}, u32[]{:S(2)}) collective-permute-start(bf16[512,256]{1,0:T(8,128)(2,1)S(1)} %get-tuple-element.93), channel_id=1, source_target_pairs={{0,128},{128,0},{1,129},{129,1},{2,130},{130,2},{3,131},{131,3},{4... | collective-permute-start | bytes 786440 | tf_op jit(solution)/shard_map/ppermute | solution.py:484
  127.7 7.4 %collective-permute-start.13 = (f32[56,128]{1,0:T(8,128)S(1)}, f32[56,128]{1,0:T(8,128)S(1)}, u32[]{:S(2)}, u32[]{:S(2)}) collective-permute-start(f32[56,128]{1,0:T(8,128)S(1)} %get-tuple-element.104), channel_id=1, source_target_pairs={{0,8},{8,0},{1,9},{9,1},{2,10},{10,2},{3,11},{11,3},{4,12},{12,4},... | collective-permute-start | bytes 86024 | tf_op jit(solution)/shard_map/ppermute | solution.py:484

commit v9 on v7

--- a/solution.py
+++ b/solution.py
@@ -254,8 +254,8 @@
     n_exp = 3
     expos = refs[:n_exp]
     blocks = refs[n_exp : n_exp + n_z + 1]
-    send, scaled, across, loss = refs[n_exp + n_z + 1 : n_exp + n_z + 5]
-    lines, whole = refs[n_exp + n_z + 5 :]
+    low, high, scaled, across, loss = refs[n_exp + n_z + 1 : n_exp + n_z + 6]
+    lines, whole = refs[n_exp + n_z + 6 :]
     z, role = place[1], place[2]
     column = sums[0]
     for k in range(1, n_z):
@@ -280,7 +280,8 @@
             at += LANES
 
     def write(start, value):
-        send[pl.ds(start - CHIP, LANES), :] = value.astype(BF)
+        target = low if start < CHIP + ROWS else high
+        target[pl.ds(start % ROWS, LANES), :] = value.astype(BF)
 
     for start in range(CHIP, 2 * CHIP, ROWS):
         mix_rows(expos, scaled, total, columns, 4 * n_z, start, write)
@@ -339,41 +340,45 @@
     return call(slope_kernel, outs, [VMEM], cost=cost)(normed)
 
 
-def backward_kernel(
-    coef, place, own, recv, other, embed, inv, n1, f1, s1, h1, n2, f2, s2, h2, x,
+def row_kernel(
+    coef, start, place, own, recv, other, embed, inv, n1, f1, s1, n2, f2, s2,
     sa_mid, sa_out, goal_mid, goal_out,
-    grads,
-    w_mid, w_out, ge_s, p1_s, p2_s, sems,
+    ge_s, p1_s, p2_s,
+    w_mid, w_out, sems,
 ):
     role = place[2]
     pairs = [((sa_out, goal_out), w_out), ((sa_mid, goal_mid), w_mid)]
     by_role(role, pairs, sems)
-    for start in range(0, CHIP, CHIP):
-        rows = pl.ds(start, CHIP)
-        grad = coef * (
-            own[rows, :] + recv[rows, :].astype(F32) - 2.0 * other[rows, :].astype(F32)
-        )
-        e = embed[rows, :]
-        scale = inv[rows, :]
-        along = jnp.mean(grad * e, axis=-1, keepdims=True)
-        ge = (EMB ** (-0.5) * scale * (grad - e * (scale * scale * along))).astype(BF)
-        ge_s[rows, :] = ge
-
-        def step(back, normed, factor, slope, out):
-            v = normed[rows, :]
-            back = back * slope[rows, :]
-            mean = jnp.mean(back, axis=-1, keepdims=True)
-            tilt = jnp.mean(back * v, axis=-1, keepdims=True)
-            pre = (factor[rows, :] * (back - mean - v * tilt)).astype(BF)
-            out[rows, :] = pre
-            return pre
-
-        if start == 0:
-            wait_role(role, pairs[:1], sems, 0)
-        p2 = step(dot_nt(ge, w_out[...]), n2, f2, s2, p2_s)
-        if start == 0:
-            wait_role(role, pairs[1:], sems, 1)
-        step(dot_nt(p2, w_mid[...]), n1, f1, s1, p1_s)
+    rows = pl.ds(start, ROWS)
+    grad = coef * (
+        own[rows, :] + recv[...].astype(F32) - 2.0 * other[rows, :].astype(F32)
+    )
+    e = embed[rows, :]
+    scale = inv[rows, :]
+    along = jnp.mean(grad * e, axis=-1, keepdims=True)
+    ge = (EMB ** (-0.5) * scale * (grad - e * (scale * scale * along))).astype(BF)
+    ge_s[...] = ge
+
+    def step(back, normed, factor, slope, out):
+        v = normed[rows, :]
+        back = back * slope[rows, :]
+        mean = jnp.mean(back, axis=-1, keepdims=True)
+        tilt = jnp.mean(back * v, axis=-1, keepdims=True)
+        pre = (factor[rows, :] * (back - mean - v * tilt)).astype(BF)
+        out[...] = pre
+        return pre
+
+    wait_role(role, pairs[:1], sems, 0)
+    p2 = step(dot_nt(ge, w_out[...]), n2, f2, s2, p2_s)
+    wait_role(role, pairs[1:], sems, 1)
+    step(dot_nt(p2, w_mid[...]), n1, f1, s1, p1_s)
+
+def product_kernel(place, h1, h2, x, ge_a, p1_a, p2_a, ge_b, p1_b, p2_b, grads):
+    role = place[2]
+
+    def times(units, pair):
+        return dot_nn(units[:, :ROWS], pair[0][...]) + dot_nn(units[:, ROWS:], pair[1][...])
+
     tall = TALL
     order = unit_order(tall)
 
@@ -390,13 +395,17 @@
     packed = []
     for xh in range(2):
         start = xh * CHIP
-        for left, right, tile in ((h1, p2_s, 0), (h2, ge_s, 8), (None, x, 10)):
+        for left, right, tile in ((h1, (p2_a, p2_b), 0), (h2, (ge_a, ge_b), 8), (None, None, 10)):
             if left is None:
                 spans = [slice(start + half * tall, start + (half + 1) * tall) for half in range(2)]
-                units = jnp.concatenate([turned(order, p1_s[:, span]) for span in spans], axis=0)
+                units = [
+                    jnp.concatenate([turned(order, p1[:, span]) for span in spans], axis=0)
+                    for p1 in (p1_a, p1_b)
+                ]
+                units = jnp.concatenate(units, axis=1)
+                value = dot_nn(units, x[:, :EMB])
             else:
-                units = left[start : start + CHIP, :]
-            value = dot_nn(units, right[:, : right.shape[1] // EMB * EMB])
+                value = times(left[start : start + CHIP, :], right)
             for part in range(8):
                 first, second = slot(part // 2, xh * 2 + part % 2)
                 for z in range(8):
@@ -572,10 +581,11 @@
     partner = shifted(part, "xh", 1)
     partner, columns = lax.optimization_barrier((partner, columns))
     sums = lax.all_to_all(jnp.broadcast_to(columns[None], (n_z, n_z, 4, LANES)), "z", 0, 0)
-    partial, scaled, across, loss = call(
+    low, high, scaled, across, loss = call(
         functools.partial(send_kernel, n_z, logit),
         [
-            shape((CHIP, EMB), BF),
+            shape((ROWS, EMB), BF),
+            shape((ROWS, EMB), BF),
             shape((n_z * CHIP, EMB), BF),
             shape((LANES, LANES), F32),
             shape((1, ROWS), F32),
@@ -583,7 +593,7 @@
         [SMEM] + [VMEM] * (5 + len(expos) + len(blocks)),
         scratch=[pltpu.VMEM((LANES, LANES), F32), pltpu.VMEM((n_z, 4, LANES), F32)],
     )(place, sums, part, partner, total, unit, *expos, *blocks)
-    added = shifted(partial, "xh", 1)
+    added = [shifted(low, "xh", 1), shifted(high, "xh", 1)]
     own = call(
         functools.partial(own_kernel, n_z),
         [shape((CHIP, EMB), F32)],
@@ -594,22 +604,29 @@
             transcendentals=0,
         ),
     )(total, scaled, across, *expos)[0]
+    halves = []
+    for half, recv in enumerate(added):
+        halves += call(
+            functools.partial(row_kernel, coef, half * ROWS),
+            [shape((ROWS, EMB), BF), shape((ROWS, HID), BF), shape((ROWS, HID), BF)],
+            [SMEM] + [VMEM] * 11 + [HBM] * 4,
+            scratch=[
+                pltpu.VMEM((HID, HID), BF),
+                pltpu.VMEM((HID, EMB), BF),
+                pltpu.SemaphoreType.DMA((2,)),
+            ],
+            cost=pl.CostEstimate(
+                flops=2 * ROWS * HID * (HID + EMB), bytes_accessed=8 * HID * HID, transcendentals=0
+            ),
+        )(
+            place, own, recv, other, embed, inv, n1, f1, s1, n2, f2, s2,
+            sa_mid, sa_out, goal_mid, goal_out,
+        )
     grads = call(
-        functools.partial(backward_kernel, coef),
+        product_kernel,
         [shape((8, 16 * TILES * 8 + 32, LANES), BF)],
-        [SMEM] + [VMEM] * 14 + [HBM] * 4,
-        scratch=[
-            pltpu.VMEM((HID, HID), BF),
-            pltpu.VMEM((HID, EMB), BF),
-            pltpu.VMEM((CHIP, EMB), BF),
-            pltpu.VMEM((CHIP, HID), BF),
-            pltpu.VMEM((CHIP, HID), BF),
-            pltpu.SemaphoreType.DMA((2,)),
-        ],
-    )(
-        place, own, added, other, embed, inv, n1, f1, s1, h1, n2, f2, s2, h2, x,
-        sa_mid, sa_out, goal_mid, goal_out,
-    )[0]
+        [SMEM] + [VMEM] * 9,
+    )(place, h1, h2, x, *halves)[0]
 
     def member(c, first, second, z):
         y, x_at = (first, second) if c == 0 else (second, first)

time: 137 us -> 139 us (1.015)
  Pallas kernels: 29.7 us -> 32.9 us
  waiting for transfers between devices: 15.1 us -> 13.4 us
    pallas_call x2 -> x4, Pallas kernels: 9.26 us -> 12.5 us  [the longest x2 6.79 us: body(): call(functools.partial(row_kernel, coef, half * ROWS), [shape((ROWS, EMB)...]
    ppermute x12 -> x13, waiting for transfers between devices: 10.8 us -> 9.12 us  [shifted(): lax.ppermute(value, axis, [(k, (k + shift) % count) for k in range(count)])]
    ppermute x12 -> x13, starting transfers between devices: 28.2 us -> 28.3 us  [shifted(): lax.ppermute(value, axis, [(k, (k + shift) % count) for k in range(count)])]
  transfers between devices with their start and end apart: 14 -> 15, of which waited for: 9 -> 9; matrix products, arithmetic and copies ran while one was open for 0% -> 0% of each run, Pallas kernels for 7% -> 9%
where the time goes in v9:
time: 139 us; the launch traced here: 138 us
  blocking collectives  58.5 us (42%)
  Pallas kernels  32.9 us (24%)
  starting transfers between devices  32.6 us (23%)
  waiting for transfers between devices  13.4 us (10%)
    ppermute x13, starting transfers between devices, shifted(): lax.ppermute(value, axis, [(k, (k + shift) % count) for k in range(count)])  28.3 us
    all_to_all x1, blocking collectives, body(): grads = lax.all_to_all(grads, axes, 0, 0, axis_index_groups=near)  27.1 us
    all_to_all x1, blocking collectives, body(): grads = lax.all_to_all(grads, axes, 0, 0, axis_index_groups=far)  18.4 us
    all_to_all x1, blocking collectives, body(): lax.all_to_all(jnp.broadcast_to(columns[None], (n_z, n_z, 4, LANES)), 'z'...  13 us
    ppermute x13, waiting for transfers between devices, shifted(): lax.ppermute(value, axis, [(k, (k + shift) % count) for k in range(count)])  9.12 us
    pallas_call x3, Pallas kernels, scores(): call(kernel, outs, [SMEM] + [VMEM] * (len(args) - 1), cost=cost)(*args)  7.54 us
    pallas_call x2, Pallas kernels, body(): call(functools.partial(row_kernel, coef, half * ROWS), [shape((ROWS, EMB)...  6.79 us
    pallas_call x1, Pallas kernels, body(): call(forward_kernel, [shape((CHIP, WIDE), BF), shape((CHIP, HID), F32), s...  5.41 us
  transfers between devices with their start and end apart: 15, of which 9 were waited for; matrix products, arithmetic and copies ran while one was open for 0% of the time, Pallas kernels for 9%

profile of v9, /device:TPU:1, one launch (start us, length us, event | category | flops | bytes accessed | tf_op | source)
XLA Modules:
  0.0 138.3 jit_solution(7436650905300014545)
XLA Ops:
  0.7 2.0 %shard_map.170 = (bf16[256,384]{1,0:T(8,128)(2,1)S(1)}, bf16[256,384]{1,0:T(8,128)(2,1)S(1)}) custom-call(s32[4]{0:T(128)S(1)} %pad_add_fusion.place, s32[1,256]{1,0:T(1,128)} %replay.1, s32[1,256]{1,0:T(1,128)} %offset.1, bf16[320,256]{1,0:T(8,128)(2,1)} %bitcast.11, bf16[16,320]{1,0:T(8,128)(2,1)} %bitcast.12), custom_call_target="tpu_custom_call" | custom-call | tf_op jit(solution)/shard_map/pallas_call | solution.py:520
  2.7 3.3 %collective-permute-start = (bf16[256,384]{1,0:T(8,128)(2,1)S(1)}, bf16[256,384]{1,0:T(8,128)(2,1)S(1)}, u32[]{:S(2)}, u32[]{:S(2)}) collective-permute-start(bf16[256,384]{1,0:T(8,128)(2,1)S(1)} %get-tuple-element.68), channel_id=1, source_target_pairs={{0,8},{8,0},{1,9},{9,1},{2,10},{10,2},{3,11},{11,3},{4,12},{12,4},... | collective-permute-start | bytes 589832 | tf_op jit(solution)/shard_map/ppermute | solution.py:491
  6.0 1.1 collective-permute-done.recv
  7.1 5.4 %shard_map.171 = (bf16[512,384]{1,0:T(8,128)(2,1)S(1)}, f32[512,1024]{1,0:T(8,128)S(1)}, f32[512,1]{1,0:T(8,128)S(1)}, f32[512,1024]{1,0:T(8,128)S(1)}, f32[512,...) custom-call(s32[4]{0:T(128)S(1)} %pad_add_fusion.place, ...), custom_call_target="tpu_custom_call" | custom-call | tf_op jit(solution)/shard_map/pallas_call | solution.py:533
  12.8 4.0 %collective-permute-start.1 = (bf16[512,256]{1,0:T(8,128)(2,1)S(1)}, bf16[512,256]{1,0:T(8,128)(2,1)S(1)}, u32[]{:S(2)}, u32[]{:S(2)}) collective-permute-start(bf16[512,256]{1,0:T(8,128)(2,1)S(1)} %get-tuple-element.76.refs_0_.ours), channel_id=1, source_target_pairs={{0,120},{8,112},{16,8},{24,0},{32,24},{40,16},{48,40},{56,32},{64,... | collective-permute-start | bytes 786440 | tf_op jit(solution)/shard_map/ppermute | solution.py:556
  16.8 0.9 shard_map.172
  17.7 1.0 shard_map.173
  18.7 4.3 %collective-permute-done.2.refs_3_.refs_4_ = bf16[512,256]{1,0:T(8,128)(2,1)S(1)} collective-permute-done((bf16[512,256]{1,0:T(8,128)(2,1)S(1)}, bf16[512,256]{1,0:T(8,128)(2,1)S(1)}, u32[]{:S(2)}, u32[]{:S(2)}) %collective-permute-start.2) | collective-permute-done | bytes 262176 | tf_op jit(solution)/shard_map/ppermute | solution.py:556
  23.0 3.0 %collective-permute-start.6 = (bf16[512,256]{1,0:T(8,128)(2,1)S(1)}, bf16[512,256]{1,0:T(8,128)(2,1)S(1)}, u32[]{:S(2)}, u32[]{:S(2)}) collective-permute-start(bf16[512,256]{1,0:T(8,128)(2,1)S(1)} %collective-permute-done.1.refs_4_.refs_5_), channel_id=1, source_target_pairs={{0,112},{16,0},{32,16},{48,32},{64,48},{80,64},{96,80},{112,96},{1... | collective-permute-start | bytes 786440 | tf_op jit(solution)/shard_map/ppermute | solution.py:491
  26.7 2.7 %collective-permute-start.3 = (bf16[512,256]{1,0:T(8,128)(2,1)S(1)}, bf16[512,256]{1,0:T(8,128)(2,1)S(1)}, u32[]{:S(2)}, u32[]{:S(2)}) collective-permute-start(bf16[512,256]{1,0:T(8,128)(2,1)S(1)} %get-tuple-element.76.refs_0_.ours), channel_id=1, source_target_pairs={{0,128},{128,0},{1,129},{129,1},{2,130},{130,2},{3,131},{131,3},{4... | collective-permute-start | bytes 786440 | tf_op jit(solution)/shard_map/ppermute | solution.py:491
  29.4 3.0 %collective-permute-done.4.refs_5_.refs_6_ = bf16[512,256]{1,0:T(8,128)(2,1)S(1)} collective-permute-done((bf16[512,256]{1,0:T(8,128)(2,1)S(1)}, bf16[512,256]{1,0:T(8,128)(2,1)S(1)}, u32[]{:S(2)}, u32[]{:S(2)}) %collective-permute-start.4) | collective-permute-done | bytes 262176 | tf_op jit(solution)/shard_map/ppermute | solution.py:491
  32.4 2.7 %collective-permute-start.7 = (bf16[512,256]{1,0:T(8,128)(2,1)S(1)}, bf16[512,256]{1,0:T(8,128)(2,1)S(1)}, u32[]{:S(2)}, u32[]{:S(2)}) collective-permute-start(bf16[512,256]{1,0:T(8,128)(2,1)S(1)} %collective-permute-done.6.refs_6_.refs_7_), channel_id=1, source_target_pairs={{0,112},{16,0},{32,16},{48,32},{64,48},{80,64},{96,80},{112,96},{1... | collective-permute-start | bytes 786440 | tf_op jit(solution)/shard_map/ppermute | solution.py:491
  35.1 1.0 collective-permute-done.3.refs_1_
  36.1 4.0 %shard_map.174 = (bf16[1024,2560]{1,0:T(8,128)(2,1)S(1)}, f32[1024,128]{1,0:T(8,128)S(1)}, f32[1024,256]{1,0:T(8,128)S(1)}, f32[20,128]{1,0:T(8,128)S(1)}) custom-call(s32[4]{0:T(128)S(1)} %pad_add_fusion.place, bf16[512,256]{1,0:T(8,128)(2,1)S(1)} %get-tuple-element.76.refs_0_.ours, bf16[512,256]{1,0:T(8,128)(2,1)S(1)} %collective-permute-done.3.refs_1_, ...), custom_call_target="tpu_custom_call" | custom-call | flops 2684354560 | bytes 6291456 | tf_op jit(solution)/shard_map/pallas_call | solution.py:236
  41.3 2.1 %collective-permute-start.9 = (bf16[256,256]{1,0:T(8,128)(2,1)S(1)}, bf16[256,256]{1,0:T(8,128)(2,1)S(1)}, u32[]{:S(2)}, u32[]{:S(2)}) collective-permute-start(bf16[256,256]{1,0:T(8,128)(2,1)S(1)} %slice.6), channel_id=1, source_target_pairs={{0,112},{16,0},{32,16},{48,32},{64,48},{80,64},{96,80},{112,96},{1... | collective-permute-start | bytes 393224 | tf_op jit(solution)/shard_map/ppermute | solution.py:491
  43.4 2.0 %shard_map.175 = (bf16[1024,1024]{1,0:T(8,128)(2,1)S(1)}, f32[1024,128]{1,0:T(8,128)S(1)}, f32[1024,256]{1,0:T(8,128)S(1)}, f32[8,128]{1,0:T(8,128)S(1)}) custom-call(s32[4]{0:T(128)S(1)} %pad_add_fusion.place, bf16[512,256]{1,0:T(8,128)(2,1)S(1)} %get-tuple-element.76.refs_0_.ours, bf16[512,256]{1,0:T(8,128)(2,1)S(1)} %collective-permute-done.3.refs_1_, ...), custom_call_target="tpu_custom_call" | custom-call | flops 1073741824 | bytes 3145728 | tf_op jit(solution)/shard_map/pallas_call | solution.py:236
  45.7 1.6 %shard_map.176 = (bf16[1024,512]{1,0:T(8,128)(2,1)S(1)}, f32[8,128]{1,0:T(8,128)S(1)}, f32[1024,256]{1,0:T(8,128)S(1)}, f32[8,4,128]{2,1,0:T(4,128)S(1)}) custom-call(s32[4]{0:T(128)S(1)} %pad_add_fusion.place, bf16[512,256]{1,0:T(8,128)(2,1)S(1)} %get-tuple-element.76.refs_0_.ours, bf16[512,256]{1,0:T(8,128)(2,1)S(1)} %collective-permute-done.3.refs_1_, ...), custom_call_target="tpu_custom_call" | custom-call | flops 536870912 | bytes 2097152 | tf_op jit(solution)/shard_map/pallas_call | solution.py:236
  47.3 2.8 %collective-permute-start.11 = (f32[8,128]{1,0:T(8,128)S(1)}, f32[8,128]{1,0:T(8,128)S(1)}, u32[]{:S(2)}, u32[]{:S(2)}) collective-permute-start(f32[8,128]{1,0:T(8,128)S(1)} %get-tuple-element.89.part), channel_id=1, source_target_pairs={{0,128},{128,0},{1,129},{129,1},{2,130},{130,2},{3,131},{131,3},{4... | collective-permute-start | bytes 12296 | tf_op jit(solution)/shard_map/ppermute | solution.py:491
  50.1 1.2 collective-permute-done.11.partner
  51.4 13.0 %all_to_all.15.sums = f32[8,8,4,128]{3,2,1,0:T(4,128)S(1)} all-to-all(f32[8,8,4,128]{3,2,1,0:T(4,128)S(1)} %broadcast_in_dim.2), channel_id=1, replica_groups=mesh['xh'=2,'z'=8,'c'=2,'y'=4,'xl'=2] {'z'}, dimensions={0} | all-to-all | bytes 262144 | tf_op jit(solution)/shard_map/all_to_all | solution.py:583
  64.4 2.5 %shard_map.177 = (bf16[256,256]{1,0:T(8,128)(2,1)S(1)}, bf16[256,256]{1,0:T(8,128)(2,1)S(1)}, bf16[4096,256]{1,0:T(8,128)(2,1)S(1)}, f32[128,128]{1,0:T(8,128)S(1)}, f32[1,256]{1,0:T(1,128)}) custom-call(s32[4]{0:T(128)S(1)} %pad_add_fusion.place, f32[8,8,4,128]{3,2,1,0:T(4,128)S(1)} %all_to_all.15.sums, f32[8,128]{1,0:T(8,128)S(1)} %get-tuple-element.89.part, ...), custom_call_target="tpu_custom_call" | custom-call | tf_op jit(solution)/shard_map/pallas_call | solution.py:584
  66.9 2.7 %collective-permute-start.13 = (bf16[256,256]{1,0:T(8,128)(2,1)S(1)}, bf16[256,256]{1,0:T(8,128)(2,1)S(1)}, u32[]{:S(2)}, u32[]{:S(2)}) collective-permute-start(bf16[256,256]{1,0:T(8,128)(2,1)S(1)} %get-tuple-element.113), channel_id=1, source_target_pairs={{0,128},{128,0},{1,129},{129,1},{2,130},{130,2},{3,131},{131,3},{4... | collective-permute-start | bytes 393224 | tf_op jit(solution)/shard_map/ppermute | solution.py:491
  69.9 1.2 shard_map.178.own
  71.2 1.1 collective-permute-done.13.recv
  72.3 3.4 %shard_map.180 = (bf16[256,256]{1,0:T(8,128)(2,1)S(1)}, bf16[256,1024]{1,0:T(8,128)(2,1)S(1)}, bf16[256,1024]{1,0:T(8,128)(2,1)S(1)}) custom-call(s32[4]{0:T(128)S(1)} %pad_add_fusion.place, f32[512,256]{1,0:T(8,128)S(1)} %shard_map.178.own, bf16[256,256]{1,0:T(8,128)(2,1)S(1)} %collective-permute-done.13.recv, ...), custom_call_target="tpu_custom_call" | custom-call | flops 671088640 | bytes 8388608 | tf_op jit(solution)/shard_map/pallas_call | solution.py:609
  75.7 3.4 %shard_map.179 = (bf16[256,256]{1,0:T(8,128)(2,1)S(1)}, bf16[256,1024]{1,0:T(8,128)(2,1)S(1)}, bf16[256,1024]{1,0:T(8,128)(2,1)S(1)}) custom-call(s32[4]{0:T(128)S(1)} %pad_add_fusion.place, f32[512,256]{1,0:T(8,128)S(1)} %shard_map.178.own, bf16[256,256]{1,0:T(8,128)(2,1)S(1)} %collective-permute-done.12.recv, ...), custom_call_target="tpu_custom_call" | custom-call | flops 671088640 | bytes 8388608 | tf_op jit(solution)/shard_map/pallas_call | solution.py:609
  79.1 3.2 %shard_map.181 = bf16[8,1568,128]{2,1,0:T(8,128)(2,1)S(1)} custom-call(s32[4]{0:T(128)S(1)} %pad_add_fusion.place, bf16[1024,512]{1,0:T(8,128)(2,1)S(1)} %get-tuple-element.98.h1, bf16[1024,512]{1,0:T(8,128)(2,1)S(1)} %get-tuple-element.99.h2, bf16[512,384]{1,0:T(8,128)(2,1)S(1)} %get-tuple-element.100.x, bf16[256,256]{1,0:T(8,128)(2,1)S(1)} %get-tuple-element.110.ge_a, ...), custom_call_target="tpu_custom_call" | custom-call | tf_op jit(solution)/shard_map/pallas_call | solution.py:625
  82.3 27.1 %all_to_all.16.parts = bf16[8,1568,128]{2,1,0:T(8,128)(2,1)S(1)} all-to-all(bf16[8,1568,128]{2,1,0:T(8,128)(2,1)S(1)} %shard_map.181), channel_id=1, replica_groups={{0,16,2,18,4,20,6,22},{32,48,34,50,36,52,38,54},{64,80,66,82,68,84,70,8..., dimensions={0} | all-to-all | bytes 6422528 | tf_op jit(solution)/shard_map/all_to_all | solution.py:649
  109.8 18.4 %all_to_all.17.parts = bf16[16,112,128]{2,1,0:T(8,128)(2,1)S(1)} all-to-all(bf16[16,112,128]{2,1,0:T(8,128)(2,1)S(1)} %shard_map.182), channel_id=1, replica_groups={{0,32,64,96,1,33,65,97,128,160,192,224,129,161,193,225},{16,48,80,112,1..., dimensions={0} | all-to-all | bytes 917504 | tf_op jit(solution)/shard_map/all_to_all | solution.py:651
  128.8 7.4 %collective-permute-start.14 = (f32[56,128]{1,0:T(8,128)S(1)}, f32[56,128]{1,0:T(8,128)S(1)}, u32[]{:S(2)}, u32[]{:S(2)}) collective-permute-start(f32[56,128]{1,0:T(8,128)S(1)} %get-tuple-element.118), channel_id=1, source_target_pairs={{0,8},{8,0},{1,9},{9,1},{2,10},{10,2},{3,11},{11,3},{4,12},{12,4},... | collective-permute-start | bytes 86024 | tf_op jit(solution)/shard_map/ppermute | solution.py:491
  136.2 0.9 collective-permute-done.14.recv
  137.0 1.3 shard_map.184
  (20 shorter events, 3.8 us)
Async XLA Ops:
  2.7 4.4 %collective-permute-start = (bf16[256,384]{1,0:T(8,128)(2,1)S(1)}, bf16[256,384]{1,0:T(8,128)(2,1)S(1)}, u32[]{:S(2)}, u32[]{:S(2)}) collective-permute-start(bf16[256,384]{1,0:T(8,128)(2,1)S(1)} %get-tuple-element.68), channel_id=1, source_target_pairs={{0,8},{8,0},{1,9},{9,1},{2,10},{10,2},{3,11},{11,3},{4,12},{12,4},... | collective-permute-start | bytes 589832 | tf_op jit(solution)/shard_map/ppermute | solution.py:491
  12.5 10.5 %collective-permute-start.2 = (bf16[512,256]{1,0:T(8,128)(2,1)S(1)}, bf16[512,256]{1,0:T(8,128)(2,1)S(1)}, u32[]{:S(2)}, u32[]{:S(2)}) collective-permute-start(bf16[512,256]{1,0:T(8,128)(2,1)S(1)} %get-tuple-element.76.refs_0_.ours), channel_id=1, source_target_pairs={{0,24},{8,16},{16,40},{24,32},{32,56},{40,48},{48,72},{56,64},{64,... | collective-permute-start | bytes 786440 | tf_op jit(solution)/shard_map/ppermute | solution.py:556
  12.8 10.3 %collective-permute-start.1 = (bf16[512,256]{1,0:T(8,128)(2,1)S(1)}, bf16[512,256]{1,0:T(8,128)(2,1)S(1)}, u32[]{:S(2)}, u32[]{:S(2)}) collective-permute-start(bf16[512,256]{1,0:T(8,128)(2,1)S(1)} %get-tuple-element.76.refs_0_.ours), channel_id=1, source_target_pairs={{0,120},{8,112},{16,8},{24,0},{32,24},{40,16},{48,40},{56,32},{64,... | collective-permute-start | bytes 786440 | tf_op jit(solution)/shard_map/ppermute | solution.py:556
  23.0 9.4 %collective-permute-start.4 = (bf16[512,256]{1,0:T(8,128)(2,1)S(1)}, bf16[512,256]{1,0:T(8,128)(2,1)S(1)}, u32[]{:S(2)}, u32[]{:S(2)}) collective-permute-start(bf16[512,256]{1,0:T(8,128)(2,1)S(1)} %collective-permute-done.2.refs_3_.refs_4_), channel_id=1, source_target_pairs={{0,16},{16,32},{32,48},{48,64},{64,80},{80,96},{96,112},{112,0},{1... | collective-permute-start | bytes 786440 | tf_op jit(solution)/shard_map/ppermute | solution.py:491
  23.0 9.4 %collective-permute-start.6 = (bf16[512,256]{1,0:T(8,128)(2,1)S(1)}, bf16[512,256]{1,0:T(8,128)(2,1)S(1)}, u32[]{:S(2)}, u32[]{:S(2)}) collective-permute-start(bf16[512,256]{1,0:T(8,128)(2,1)S(1)} %collective-permute-done.1.refs_4_.refs_5_), channel_id=1, source_target_pairs={{0,112},{16,0},{32,16},{48,32},{64,48},{80,64},{96,80},{112,96},{1... | collective-permute-start | bytes 786440 | tf_op jit(solution)/shard_map/ppermute | solution.py:491
  26.0 9.1 %collective-permute-start.8 = (bf16[512,256]{1,0:T(8,128)(2,1)S(1)}, bf16[512,256]{1,0:T(8,128)(2,1)S(1)}, u32[]{:S(2)}, u32[]{:S(2)}) collective-permute-start(bf16[512,256]{1,0:T(8,128)(2,1)S(1)} %get-tuple-element.76.refs_0_.ours), channel_id=1, source_target_pairs={{0,8},{8,0},{1,9},{9,1},{2,10},{10,2},{3,11},{11,3},{4,12},{12,4},... | collective-permute-start | bytes 786440 | tf_op jit(solution)/shard_map/ppermute | solution.py:491
  26.7 9.4 %collective-permute-start.3 = (bf16[512,256]{1,0:T(8,128)(2,1)S(1)}, bf16[512,256]{1,0:T(8,128)(2,1)S(1)}, u32[]{:S(2)}, u32[]{:S(2)}) collective-permute-start(bf16[512,256]{1,0:T(8,128)(2,1)S(1)} %get-tuple-element.76.refs_0_.ours), channel_id=1, source_target_pairs={{0,128},{128,0},{1,129},{129,1},{2,130},{130,2},{3,131},{131,3},{4... | collective-permute-start | bytes 786440 | tf_op jit(solution)/shard_map/ppermute | solution.py:491
  32.4 8.2 %collective-permute-start.5 = (bf16[512,256]{1,0:T(8,128)(2,1)S(1)}, bf16[512,256]{1,0:T(8,128)(2,1)S(1)}, u32[]{:S(2)}, u32[]{:S(2)}) collective-permute-start(bf16[512,256]{1,0:T(8,128)(2,1)S(1)} %collective-permute-done.4.refs_5_.refs_6_), channel_id=1, source_target_pairs={{0,16},{16,32},{32,48},{48,64},{64,80},{80,96},{96,112},{112,0},{1... | collective-permute-start | bytes 786440 | tf_op jit(solution)/shard_map/ppermute | solution.py:491
  32.4 8.2 %collective-permute-start.7 = (bf16[512,256]{1,0:T(8,128)(2,1)S(1)}, bf16[512,256]{1,0:T(8,128)(2,1)S(1)}, u32[]{:S(2)}, u32[]{:S(2)}) collective-permute-start(bf16[512,256]{1,0:T(8,128)(2,1)S(1)} %collective-permute-done.6.refs_6_.refs_7_), channel_id=1, source_target_pairs={{0,112},{16,0},{32,16},{48,32},{64,48},{80,64},{96,80},{112,96},{1... | collective-permute-start | bytes 786440 | tf_op jit(solution)/shard_map/ppermute | solution.py:491
  40.6 5.1 %collective-permute-start.10 = (bf16[256,256]{1,0:T(8,128)(2,1)S(1)}, bf16[256,256]{1,0:T(8,128)(2,1)S(1)}, u32[]{:S(2)}, u32[]{:S(2)}) collective-permute-start(bf16[256,256]{1,0:T(8,128)(2,1)S(1)} %slice.7), channel_id=1, source_target_pairs={{0,16},{16,32},{32,48},{48,64},{64,80},{80,96},{96,112},{112,0},{1... | collective-permute-start | bytes 393224 | tf_op jit(solution)/shard_map/ppermute | solution.py:491
  41.3 4.4 %collective-permute-start.9 = (bf16[256,256]{1,0:T(8,128)(2,1)S(1)}, bf16[256,256]{1,0:T(8,128)(2,1)S(1)}, u32[]{:S(2)}, u32[]{:S(2)}) collective-permute-start(bf16[256,256]{1,0:T(8,128)(2,1)S(1)} %slice.6), channel_id=1, source_target_pairs={{0,112},{16,0},{32,16},{48,32},{64,48},{80,64},{96,80},{112,96},{1... | collective-permute-start | bytes 393224 | tf_op jit(solution)/shard_map/ppermute | solution.py:491
  47.3 4.0 %collective-permute-start.11 = (f32[8,128]{1,0:T(8,128)S(1)}, f32[8,128]{1,0:T(8,128)S(1)}, u32[]{:S(2)}, u32[]{:S(2)}) collective-permute-start(f32[8,128]{1,0:T(8,128)S(1)} %get-tuple-element.89.part), channel_id=1, source_target_pairs={{0,128},{128,0},{1,129},{129,1},{2,130},{130,2},{3,131},{131,3},{4... | collective-permute-start | bytes 12296 | tf_op jit(solution)/shard_map/ppermute | solution.py:491
  66.9 5.3 %collective-permute-start.13 = (bf16[256,256]{1,0:T(8,128)(2,1)S(1)}, bf16[256,256]{1,0:T(8,128)(2,1)S(1)}, u32[]{:S(2)}, u32[]{:S(2)}) collective-permute-start(bf16[256,256]{1,0:T(8,128)(2,1)S(1)} %get-tuple-element.113), channel_id=1, source_target_pairs={{0,128},{128,0},{1,129},{129,1},{2,130},{130,2},{3,131},{131,3},{4... | collective-permute-start | bytes 393224 | tf_op jit(solution)/shard_map/ppermute | solution.py:491
  69.7 6.0 %collective-permute-start.12 = (bf16[256,256]{1,0:T(8,128)(2,1)S(1)}, bf16[256,256]{1,0:T(8,128)(2,1)S(1)}, u32[]{:S(2)}, u32[]{:S(2)}) collective-permute-start(bf16[256,256]{1,0:T(8,128)(2,1)S(1)} %get-tuple-element.103), channel_id=1, source_target_pairs={{0,128},{128,0},{1,129},{129,1},{2,130},{130,2},{3,131},{131,3},{4... | collective-permute-start | bytes 393224 | tf_op jit(solution)/shard_map/ppermute | solution.py:491
  128.8 8.2 %collective-permute-start.14 = (f32[56,128]{1,0:T(8,128)S(1)}, f32[56,128]{1,0:T(8,128)S(1)}, u32[]{:S(2)}, u32[]{:S(2)}) collective-permute-start(f32[56,128]{1,0:T(8,128)S(1)} %get-tuple-element.118), channel_id=1, source_target_pairs={{0,8},{8,0},{1,9},{9,1},{2,10},{10,2},{3,11},{11,3},{4,12},{12,4},... | collective-permute-start | bytes 86024 | tf_op jit(solution)/shard_map/ppermute | solution.py:491

commit v10 on v8

--- a/solution.py
+++ b/solution.py
@@ -159,7 +159,7 @@
         order += [k, n_z - k]
     order.append(n_z // 2)
     z, role = place[1], place[2]
-    return [lax.rem(z + jnp.where(role == 0, shift, n_z - shift), n_z) for shift in order]
+    return [lax.rem(z + jnp.where(role == 0, n_z - shift, shift), n_z) for shift in order]
 
 
 def score_kernel(n_blocks, first, last, factor, place, *refs):
@@ -549,13 +549,13 @@
         for k in range(n_z):
             for c in range(2):
                 to = c ^ cross
-                pairs.append((k * 2 + c, (k + (way if to else -way)) % n_z * 2 + to))
+                pairs.append((k * 2 + c, (k + (-way if to else way)) % n_z * 2 + to))
         return lax.ppermute(value, ("z", "c"), pairs)
 
     ahead, back = hop(unit, 1, 1), hop(unit, -1, 1)
     s1, h1 = slopes(n1)
     s2, h2 = slopes(n2)
-    back, ahead, s1, h1, s2, h2, late = lax.optimization_barrier((back, ahead, s1, h1, s2, h2, unit))
+    ahead, back, s1, h1, s2, h2, late = lax.optimization_barrier((ahead, back, s1, h1, s2, h2, unit))
     steps = [[ahead, back]]
     for k in range(2, n_z // 2 - 1):
         ahead, back = hop(ahead, 1), hop(back, -1)

time: 137 us -> 137 us (level)
  waiting for transfers between devices: 16.1 us -> 19.2 us
  blocking collectives: 58.1 us -> 55.9 us
    ppermute x8, starting transfers between devices: 13.8 us -> 11.2 us  [hop(): return lax.ppermute(value, ('z', 'c'), pairs)]
    all_to_all x1, blocking collectives: 12.6 us -> 10.3 us  [body(): lax.all_to_all(jnp.broadcast_to(columns[None], (n_z, n_z, 4, LANES)), 'z'...]
    ppermute x6, waiting for transfers between devices: 6.35 us -> 8.53 us  [shifted(): lax.ppermute(value, axis, [(k, (k + shift) % count) for k in range(count)])]
    ppermute x6, starting transfers between devices: 17.8 us -> 19.7 us  [shifted(): lax.ppermute(value, axis, [(k, (k + shift) % count) for k in range(count)])]
  transfers between devices with their start and end apart: 14 -> 14, of which waited for: 9 -> 11; matrix products, arithmetic and copies ran while one was open for 0% -> 0% of each run, Pallas kernels for 7% -> 7%
where the time goes in v10:
time: 137 us
  blocking collectives  55.9 us (41%)
  starting transfers between devices  30.9 us (23%)
  Pallas kernels  29.7 us (22%)
  waiting for transfers between devices  19.2 us (14%)
    all_to_all x1, blocking collectives, body(): grads = lax.all_to_all(grads, axes, 0, 0, axis_index_groups=near)  27.1 us
    ppermute x6, starting transfers between devices, shifted(): lax.ppermute(value, axis, [(k, (k + shift) % count) for k in range(count)])  19.7 us
    all_to_all x1, blocking collectives, body(): grads = lax.all_to_all(grads, axes, 0, 0, axis_index_groups=far)  18.5 us
    ppermute x8, starting transfers between devices, hop(): return lax.ppermute(value, ('z', 'c'), pairs)  11.2 us
    ppermute x8, waiting for transfers between devices, hop(): return lax.ppermute(value, ('z', 'c'), pairs)  10.7 us
    all_to_all x1, blocking collectives, body(): lax.all_to_all(jnp.broadcast_to(columns[None], (n_z, n_z, 4, LANES)), 'z'...  10.3 us
    ppermute x6, waiting for transfers between devices, shifted(): lax.ppermute(value, axis, [(k, (k + shift) % count) for k in range(count)])  8.53 us
    pallas_call x3, Pallas kernels, scores(): call(kernel, outs, [SMEM] + [VMEM] * (len(args) - 1), cost=cost)(*args)  7.51 us
  transfers between devices with their start and end apart: 14, of which 11 were waited for; matrix products, arithmetic and copies ran while one was open for 0% of the time, Pallas kernels for 7%

profile of v10, /device:TPU:1, one launch (start us, length us, event | category | flops | bytes accessed | tf_op | source)
XLA Modules:
  0.0 136.6 jit_solution(2780563937369917816)
XLA Ops:
  0.7 2.0 %shard_map.170 = (bf16[256,384]{1,0:T(8,128)(2,1)S(1)}, bf16[256,384]{1,0:T(8,128)(2,1)S(1)}) custom-call(s32[4]{0:T(128)S(1)} %pad_add_fusion.place, s32[1,256]{1,0:T(1,128)} %replay.1, s32[1,256]{1,0:T(1,128)} %offset.1, bf16[320,256]{1,0:T(8,128)(2,1)} %bitcast.11, bf16[16,320]{1,0:T(8,128)(2,1)} %bitcast.12), custom_call_target="tpu_custom_call" | custom-call | tf_op jit(solution)/shard_map/pallas_call | solution.py:513
  2.7 3.3 %collective-permute-start = (bf16[256,384]{1,0:T(8,128)(2,1)S(1)}, bf16[256,384]{1,0:T(8,128)(2,1)S(1)}, u32[]{:S(2)}, u32[]{:S(2)}) collective-permute-start(bf16[256,384]{1,0:T(8,128)(2,1)S(1)} %get-tuple-element.61), channel_id=1, source_target_pairs={{0,8},{8,0},{1,9},{9,1},{2,10},{10,2},{3,11},{11,3},{4,12},{12,4},... | collective-permute-start | bytes 589832 | tf_op jit(solution)/shard_map/ppermute | solution.py:484
  6.0 1.1 collective-permute-done.recv
  7.1 5.4 %shard_map.171 = (bf16[512,384]{1,0:T(8,128)(2,1)S(1)}, f32[512,1024]{1,0:T(8,128)S(1)}, f32[512,1]{1,0:T(8,128)S(1)}, f32[512,1024]{1,0:T(8,128)S(1)}, f32[512,...) custom-call(s32[4]{0:T(128)S(1)} %pad_add_fusion.place, ...), custom_call_target="tpu_custom_call" | custom-call | tf_op jit(solution)/shard_map/pallas_call | solution.py:526
  12.5 4.2 %collective-permute-start.2 = (bf16[512,256]{1,0:T(8,128)(2,1)S(1)}, bf16[512,256]{1,0:T(8,128)(2,1)S(1)}, u32[]{:S(2)}, u32[]{:S(2)}) collective-permute-start(bf16[512,256]{1,0:T(8,128)(2,1)S(1)} %get-tuple-element.69.refs_0_.ours), channel_id=1, source_target_pairs={{0,24},{8,112},{16,40},{24,0},{32,56},{40,16},{48,72},{56,32},{64,... | collective-permute-start | bytes 786440 | tf_op jit(solution)/shard_map/ppermute | solution.py:553
  16.7 0.9 shard_map.172
  17.7 1.0 shard_map.173
  18.6 4.9 %collective-permute-done.2.refs_4_.refs_5_ = bf16[512,256]{1,0:T(8,128)(2,1)S(1)} collective-permute-done((bf16[512,256]{1,0:T(8,128)(2,1)S(1)}, bf16[512,256]{1,0:T(8,128)(2,1)S(1)}, u32[]{:S(2)}, u32[]{:S(2)}) %collective-permute-start.2) | collective-permute-done | bytes 262176 | tf_op jit(solution)/shard_map/ppermute | solution.py:553
  23.5 2.4 %collective-permute-start.4 = (bf16[512,256]{1,0:T(8,128)(2,1)S(1)}, bf16[512,256]{1,0:T(8,128)(2,1)S(1)}, u32[]{:S(2)}, u32[]{:S(2)}) collective-permute-start(bf16[512,256]{1,0:T(8,128)(2,1)S(1)} %collective-permute-done.1.refs_3_.refs_4_), channel_id=1, source_target_pairs={{0,16},{8,120},{16,32},{24,8},{32,48},{40,24},{48,64},{56,40},{64,... | collective-permute-start | bytes 786440 | tf_op jit(solution)/shard_map/ppermute | solution.py:553
  26.0 1.5 %collective-permute-start.8 = (bf16[512,256]{1,0:T(8,128)(2,1)S(1)}, bf16[512,256]{1,0:T(8,128)(2,1)S(1)}, u32[]{:S(2)}, u32[]{:S(2)}) collective-permute-start(bf16[512,256]{1,0:T(8,128)(2,1)S(1)} %get-tuple-element.69.refs_0_.ours), channel_id=1, source_target_pairs={{0,8},{8,0},{1,9},{9,1},{2,10},{10,2},{3,11},{11,3},{4,12},{12,4},... | collective-permute-start | bytes 786440 | tf_op jit(solution)/shard_map/ppermute | solution.py:484
  27.5 2.7 %collective-permute-start.3 = (bf16[512,256]{1,0:T(8,128)(2,1)S(1)}, bf16[512,256]{1,0:T(8,128)(2,1)S(1)}, u32[]{:S(2)}, u32[]{:S(2)}) collective-permute-start(bf16[512,256]{1,0:T(8,128)(2,1)S(1)} %get-tuple-element.69.refs_0_.ours), channel_id=1, source_target_pairs={{0,128},{128,0},{1,129},{129,1},{2,130},{130,2},{3,131},{131,3},{4... | collective-permute-start | bytes 786440 | tf_op jit(solution)/shard_map/ppermute | solution.py:484
  30.6 3.1 %collective-permute-start.5 = (bf16[512,256]{1,0:T(8,128)(2,1)S(1)}, bf16[512,256]{1,0:T(8,128)(2,1)S(1)}, u32[]{:S(2)}, u32[]{:S(2)}) collective-permute-start(bf16[512,256]{1,0:T(8,128)(2,1)S(1)} %collective-permute-done.4.refs_5_.refs_6_), channel_id=1, source_target_pairs={{0,16},{8,120},{16,32},{24,8},{32,48},{40,24},{48,64},{56,40},{64,... | collective-permute-start | bytes 786440 | tf_op jit(solution)/shard_map/ppermute | solution.py:553
  34.3 2.7 %collective-permute-done.3.refs_1_ = bf16[512,256]{1,0:T(8,128)(2,1)S(1)} collective-permute-done((bf16[512,256]{1,0:T(8,128)(2,1)S(1)}, bf16[512,256]{1,0:T(8,128)(2,1)S(1)}, u32[]{:S(2)}, u32[]{:S(2)}) %collective-permute-start.3) | collective-permute-done | bytes 262176 | tf_op jit(solution)/shard_map/ppermute | solution.py:484
  36.9 3.9 %shard_map.174 = (bf16[1024,2560]{1,0:T(8,128)(2,1)S(1)}, f32[1024,128]{1,0:T(8,128)S(1)}, f32[1024,256]{1,0:T(8,128)S(1)}, f32[20,128]{1,0:T(8,128)S(1)}) custom-call(s32[4]{0:T(128)S(1)} %pad_add_fusion.place, bf16[512,256]{1,0:T(8,128)(2,1)S(1)} %get-tuple-element.69.refs_0_.ours, bf16[512,256]{1,0:T(8,128)(2,1)S(1)} %collective-permute-done.3.refs_1_, ...), custom_call_target="tpu_custom_call" | custom-call | flops 2684354560 | bytes 6291456 | tf_op jit(solution)/shard_map/pallas_call | solution.py:238
  40.9 2.2 %collective-permute-done.7.refs_3_.refs_9_ = bf16[512,256]{1,0:T(8,128)(2,1)S(1)} collective-permute-done((bf16[512,256]{1,0:T(8,128)(2,1)S(1)}, bf16[512,256]{1,0:T(8,128)(2,1)S(1)}, u32[]{:S(2)}, u32[]{:S(2)}) %collective-permute-start.7) | collective-permute-done | bytes 262176 | tf_op jit(solution)/shard_map/ppermute | solution.py:553
  43.2 1.5 %collective-permute-start.9 = (bf16[256,256]{1,0:T(8,128)(2,1)S(1)}, bf16[256,256]{1,0:T(8,128)(2,1)S(1)}, u32[]{:S(2)}, u32[]{:S(2)}) collective-permute-start(bf16[256,256]{1,0:T(8,128)(2,1)S(1)} %slice.6), channel_id=1, source_target_pairs={{0,112},{8,24},{16,0},{24,40},{32,16},{40,56},{48,32},{56,72},{64,... | collective-permute-start | bytes 393224 | tf_op jit(solution)/shard_map/ppermute | solution.py:553
  44.7 2.0 %shard_map.175 = (bf16[1024,1024]{1,0:T(8,128)(2,1)S(1)}, f32[1024,128]{1,0:T(8,128)S(1)}, f32[1024,256]{1,0:T(8,128)S(1)}, f32[8,128]{1,0:T(8,128)S(1)}) custom-call(s32[4]{0:T(128)S(1)} %pad_add_fusion.place, bf16[512,256]{1,0:T(8,128)(2,1)S(1)} %get-tuple-element.69.refs_0_.ours, bf16[512,256]{1,0:T(8,128)(2,1)S(1)} %collective-permute-done.3.refs_1_, ...), custom_call_target="tpu_custom_call" | custom-call | flops 1073741824 | bytes 3145728 | tf_op jit(solution)/shard_map/pallas_call | solution.py:238
  46.7 1.1 collective-permute-done.10.refs_3_.refs_11_
  47.8 1.5 %collective-permute-done.9.refs_2_.refs_10_ = bf16[256,256]{1,0:T(8,128)(2,1)S(1)} collective-permute-done((bf16[256,256]{1,0:T(8,128)(2,1)S(1)}, bf16[256,256]{1,0:T(8,128)(2,1)S(1)}, u32[]{:S(2)}, u32[]{:S(2)}) %collective-permute-start.9) | collective-permute-done | bytes 131104 | tf_op jit(solution)/shard_map/ppermute | solution.py:553
  49.3 1.6 %shard_map.176 = (bf16[1024,512]{1,0:T(8,128)(2,1)S(1)}, f32[8,128]{1,0:T(8,128)S(1)}, f32[1024,256]{1,0:T(8,128)S(1)}, f32[8,4,128]{2,1,0:T(4,128)S(1)}) custom-call(s32[4]{0:T(128)S(1)} %pad_add_fusion.place, bf16[512,256]{1,0:T(8,128)(2,1)S(1)} %get-tuple-element.69.refs_0_.ours, bf16[512,256]{1,0:T(8,128)(2,1)S(1)} %collective-permute-done.3.refs_1_, ...), custom_call_target="tpu_custom_call" | custom-call | flops 536870912 | bytes 2097152 | tf_op jit(solution)/shard_map/pallas_call | solution.py:238
  50.9 2.8 %collective-permute-start.11 = (f32[8,128]{1,0:T(8,128)S(1)}, f32[8,128]{1,0:T(8,128)S(1)}, u32[]{:S(2)}, u32[]{:S(2)}) collective-permute-start(f32[8,128]{1,0:T(8,128)S(1)} %get-tuple-element.82.part), channel_id=1, source_target_pairs={{0,128},{128,0},{1,129},{129,1},{2,130},{130,2},{3,131},{131,3},{4... | collective-permute-start | bytes 12296 | tf_op jit(solution)/shard_map/ppermute | solution.py:484
  53.8 1.2 collective-permute-done.11.partner
  55.0 10.3 %all_to_all.15.sums = f32[8,8,4,128]{3,2,1,0:T(4,128)S(1)} all-to-all(f32[8,8,4,128]{3,2,1,0:T(4,128)S(1)} %broadcast_in_dim.2), channel_id=1, replica_groups=mesh['xh'=2,'z'=8,'c'=2,'y'=4,'xl'=2] {'z'}, dimensions={0} | all-to-all | bytes 262144 | tf_op jit(solution)/shard_map/all_to_all | solution.py:580
  65.3 2.5 %shard_map.177 = (bf16[512,256]{1,0:T(8,128)(2,1)S(1)}, bf16[4096,256]{1,0:T(8,128)(2,1)S(1)}, f32[128,128]{1,0:T(8,128)S(1)}, f32[1,256]{1,0:T(1,128)}) custom-call(s32[4]{0:T(128)S(1)} %pad_add_fusion.place, f32[8,8,4,128]{3,2,1,0:T(4,128)S(1)} %all_to_all.15.sums, f32[8,128]{1,0:T(8,128)S(1)} %get-tuple-element.82.part, ...), custom_call_target="tpu_custom_call" | custom-call | tf_op jit(solution)/shard_map/pallas_call | solution.py:581
  67.8 2.7 %collective-permute-start.12 = (bf16[512,256]{1,0:T(8,128)(2,1)S(1)}, bf16[512,256]{1,0:T(8,128)(2,1)S(1)}, u32[]{:S(2)}, u32[]{:S(2)}) collective-permute-start(bf16[512,256]{1,0:T(8,128)(2,1)S(1)} %get-tuple-element.93), channel_id=1, source_target_pairs={{0,128},{128,0},{1,129},{129,1},{2,130},{130,2},{3,131},{131,3},{4... | collective-permute-start | bytes 786440 | tf_op jit(solution)/shard_map/ppermute | solution.py:484
  70.6 1.3 shard_map.178.own
  71.9 2.7 %collective-permute-done.12.recv = bf16[512,256]{1,0:T(8,128)(2,1)S(1)} collective-permute-done((bf16[512,256]{1,0:T(8,128)(2,1)S(1)}, bf16[512,256]{1,0:T(8,128)(2,1)S(1)}, u32[]{:S(2)}, u32[]{:S(2)}) %collective-permute-start.12) | collective-permute-done | bytes 262176 | tf_op jit(solution)/shard_map/ppermute | solution.py:484
  74.6 6.8 %shard_map.179 = bf16[8,1568,128]{2,1,0:T(8,128)(2,1)S(1)} custom-call(s32[4]{0:T(128)S(1)} %pad_add_fusion.place, f32[512,256]{1,0:T(8,128)S(1)} %shard_map.178.own, bf16[512,256]{1,0:T(8,128)(2,1)S(1)} %collective-permute-done.12.recv, bf16[512,256]{1,0:T(8,128)(2,1)S(1)} %collective-permute-done.8.refs_2_.refs_3_.other, ...), custom_call_target="tpu_custom_call" | custom-call | tf_op jit(solution)/shard_map/pallas_call | solution.py:603
  81.3 27.1 %all_to_all.16.parts = bf16[8,1568,128]{2,1,0:T(8,128)(2,1)S(1)} all-to-all(bf16[8,1568,128]{2,1,0:T(8,128)(2,1)S(1)} %shard_map.179), channel_id=1, replica_groups={{0,16,2,18,4,20,6,22},{32,48,34,50,36,52,38,54},{64,80,66,82,68,84,70,8..., dimensions={0} | all-to-all | bytes 6422528 | tf_op jit(solution)/shard_map/all_to_all | solution.py:638
  108.9 18.5 %all_to_all.17.parts = bf16[16,112,128]{2,1,0:T(8,128)(2,1)S(1)} all-to-all(bf16[16,112,128]{2,1,0:T(8,128)(2,1)S(1)} %shard_map.180), channel_id=1, replica_groups={{0,32,64,96,1,33,65,97,128,160,192,224,129,161,193,225},{16,48,80,112,1..., dimensions={0} | all-to-all | bytes 917504 | tf_op jit(solution)/shard_map/all_to_all | solution.py:640
  127.9 6.5 %collective-permute-start.13 = (f32[56,128]{1,0:T(8,128)S(1)}, f32[56,128]{1,0:T(8,128)S(1)}, u32[]{:S(2)}, u32[]{:S(2)}) collective-permute-start(f32[56,128]{1,0:T(8,128)S(1)} %get-tuple-element.104), channel_id=1, source_target_pairs={{0,8},{8,0},{1,9},{9,1},{2,10},{10,2},{3,11},{11,3},{4,12},{12,4},... | collective-permute-start | bytes 86024 | tf_op jit(solution)/shard_map/ppermute | solution.py:484
  135.3 1.3 shard_map.182
  (16 shorter events, 3.1 us)
Async XLA Ops:
  2.7 4.4 %collective-permute-start = (bf16[256,384]{1,0:T(8,128)(2,1)S(1)}, bf16[256,384]{1,0:T(8,128)(2,1)S(1)}, u32[]{:S(2)}, u32[]{:S(2)}) collective-permute-start(bf16[256,384]{1,0:T(8,128)(2,1)S(1)} %get-tuple-element.61), channel_id=1, source_target_pairs={{0,8},{8,0},{1,9},{9,1},{2,10},{10,2},{3,11},{11,3},{4,12},{12,4},... | collective-permute-start | bytes 589832 | tf_op jit(solution)/shard_map/ppermute | solution.py:484
  12.5 11.0 %collective-permute-start.2 = (bf16[512,256]{1,0:T(8,128)(2,1)S(1)}, bf16[512,256]{1,0:T(8,128)(2,1)S(1)}, u32[]{:S(2)}, u32[]{:S(2)}) collective-permute-start(bf16[512,256]{1,0:T(8,128)(2,1)S(1)} %get-tuple-element.69.refs_0_.ours), channel_id=1, source_target_pairs={{0,24},{8,112},{16,40},{24,0},{32,56},{40,16},{48,72},{56,32},{64,... | collective-permute-start | bytes 786440 | tf_op jit(solution)/shard_map/ppermute | solution.py:553
  16.7 6.8 %collective-permute-start.1 = (bf16[512,256]{1,0:T(8,128)(2,1)S(1)}, bf16[512,256]{1,0:T(8,128)(2,1)S(1)}, u32[]{:S(2)}, u32[]{:S(2)}) collective-permute-start(bf16[512,256]{1,0:T(8,128)(2,1)S(1)} %get-tuple-element.69.refs_0_.ours), channel_id=1, source_target_pairs={{0,120},{8,16},{16,8},{24,32},{32,24},{40,48},{48,40},{56,64},{64,... | collective-permute-start | bytes 786440 | tf_op jit(solution)/shard_map/ppermute | solution.py:553
  23.5 7.1 %collective-permute-start.4 = (bf16[512,256]{1,0:T(8,128)(2,1)S(1)}, bf16[512,256]{1,0:T(8,128)(2,1)S(1)}, u32[]{:S(2)}, u32[]{:S(2)}) collective-permute-start(bf16[512,256]{1,0:T(8,128)(2,1)S(1)} %collective-permute-done.1.refs_3_.refs_4_), channel_id=1, source_target_pairs={{0,16},{8,120},{16,32},{24,8},{32,48},{40,24},{48,64},{56,40},{64,... | collective-permute-start | bytes 786440 | tf_op jit(solution)/shard_map/ppermute | solution.py:553
  26.0 8.3 %collective-permute-start.6 = (bf16[512,256]{1,0:T(8,128)(2,1)S(1)}, bf16[512,256]{1,0:T(8,128)(2,1)S(1)}, u32[]{:S(2)}, u32[]{:S(2)}) collective-permute-start(bf16[512,256]{1,0:T(8,128)(2,1)S(1)} %collective-permute-done.2.refs_4_.refs_5_), channel_id=1, source_target_pairs={{0,112},{8,24},{16,0},{24,40},{32,16},{40,56},{48,32},{56,72},{64,... | collective-permute-start | bytes 786440 | tf_op jit(solution)/shard_map/ppermute | solution.py:553
  26.0 8.3 %collective-permute-start.8 = (bf16[512,256]{1,0:T(8,128)(2,1)S(1)}, bf16[512,256]{1,0:T(8,128)(2,1)S(1)}, u32[]{:S(2)}, u32[]{:S(2)}) collective-permute-start(bf16[512,256]{1,0:T(8,128)(2,1)S(1)} %get-tuple-element.69.refs_0_.ours), channel_id=1, source_target_pairs={{0,8},{8,0},{1,9},{9,1},{2,10},{10,2},{3,11},{11,3},{4,12},{12,4},... | collective-permute-start | bytes 786440 | tf_op jit(solution)/shard_map/ppermute | solution.py:484
  27.5 9.4 %collective-permute-start.3 = (bf16[512,256]{1,0:T(8,128)(2,1)S(1)}, bf16[512,256]{1,0:T(8,128)(2,1)S(1)}, u32[]{:S(2)}, u32[]{:S(2)}) collective-permute-start(bf16[512,256]{1,0:T(8,128)(2,1)S(1)} %get-tuple-element.69.refs_0_.ours), channel_id=1, source_target_pairs={{0,128},{128,0},{1,129},{129,1},{2,130},{130,2},{3,131},{131,3},{4... | collective-permute-start | bytes 786440 | tf_op jit(solution)/shard_map/ppermute | solution.py:484
  30.6 10.3 %collective-permute-start.5 = (bf16[512,256]{1,0:T(8,128)(2,1)S(1)}, bf16[512,256]{1,0:T(8,128)(2,1)S(1)}, u32[]{:S(2)}, u32[]{:S(2)}) collective-permute-start(bf16[512,256]{1,0:T(8,128)(2,1)S(1)} %collective-permute-done.4.refs_5_.refs_6_), channel_id=1, source_target_pairs={{0,16},{8,120},{16,32},{24,8},{32,48},{40,24},{48,64},{56,40},{64,... | collective-permute-start | bytes 786440 | tf_op jit(solution)/shard_map/ppermute | solution.py:553
  34.3 8.8 %collective-permute-start.7 = (bf16[512,256]{1,0:T(8,128)(2,1)S(1)}, bf16[512,256]{1,0:T(8,128)(2,1)S(1)}, u32[]{:S(2)}, u32[]{:S(2)}) collective-permute-start(bf16[512,256]{1,0:T(8,128)(2,1)S(1)} %collective-permute-done.6.refs_6_.refs_7_), channel_id=1, source_target_pairs={{0,112},{8,24},{16,0},{24,40},{32,16},{40,56},{48,32},{56,72},{64,... | collective-permute-start | bytes 786440 | tf_op jit(solution)/shard_map/ppermute | solution.py:553
  43.1 4.7 %collective-permute-start.10 = (bf16[256,256]{1,0:T(8,128)(2,1)S(1)}, bf16[256,256]{1,0:T(8,128)(2,1)S(1)}, u32[]{:S(2)}, u32[]{:S(2)}) collective-permute-start(bf16[256,256]{1,0:T(8,128)(2,1)S(1)} %slice.7), channel_id=1, source_target_pairs={{0,16},{8,120},{16,32},{24,8},{32,48},{40,24},{48,64},{56,40},{64,... | collective-permute-start | bytes 393224 | tf_op jit(solution)/shard_map/ppermute | solution.py:553
  43.2 6.1 %collective-permute-start.9 = (bf16[256,256]{1,0:T(8,128)(2,1)S(1)}, bf16[256,256]{1,0:T(8,128)(2,1)S(1)}, u32[]{:S(2)}, u32[]{:S(2)}) collective-permute-start(bf16[256,256]{1,0:T(8,128)(2,1)S(1)} %slice.6), channel_id=1, source_target_pairs={{0,112},{8,24},{16,0},{24,40},{32,16},{40,56},{48,32},{56,72},{64,... | collective-permute-start | bytes 393224 | tf_op jit(solution)/shard_map/ppermute | solution.py:553
  50.9 4.0 %collective-permute-start.11 = (f32[8,128]{1,0:T(8,128)S(1)}, f32[8,128]{1,0:T(8,128)S(1)}, u32[]{:S(2)}, u32[]{:S(2)}) collective-permute-start(f32[8,128]{1,0:T(8,128)S(1)} %get-tuple-element.82.part), channel_id=1, source_target_pairs={{0,128},{128,0},{1,129},{129,1},{2,130},{130,2},{3,131},{131,3},{4... | collective-permute-start | bytes 12296 | tf_op jit(solution)/shard_map/ppermute | solution.py:484
  67.8 6.7 %collective-permute-start.12 = (bf16[512,256]{1,0:T(8,128)(2,1)S(1)}, bf16[512,256]{1,0:T(8,128)(2,1)S(1)}, u32[]{:S(2)}, u32[]{:S(2)}) collective-permute-start(bf16[512,256]{1,0:T(8,128)(2,1)S(1)} %get-tuple-element.93), channel_id=1, source_target_pairs={{0,128},{128,0},{1,129},{129,1},{2,130},{130,2},{3,131},{131,3},{4... | collective-permute-start | bytes 786440 | tf_op jit(solution)/shard_map/ppermute | solution.py:484
  127.9 7.4 %collective-permute-start.13 = (f32[56,128]{1,0:T(8,128)S(1)}, f32[56,128]{1,0:T(8,128)S(1)}, u32[]{:S(2)}, u32[]{:S(2)}) collective-permute-start(f32[56,128]{1,0:T(8,128)S(1)} %get-tuple-element.104), channel_id=1, source_target_pairs={{0,8},{8,0},{1,9},{9,1},{2,10},{10,2},{3,11},{11,3},{4,12},{12,4},... | collective-permute-start | bytes 86024 | tf_op jit(solution)/shard_map/ppermute | solution.py:484
